TPU v7x, 512 devices: a whole 4x4x16 slice. The times are simulated.
512 devices in a mesh: rows: 32 (over z, x_hi), cols: 16 (over y, x_lo, core).
Axes of the slice: x: 4 (x_hi: 2, x_lo: 2; x = x_hi * 2 + x_lo), y: 4, z: 16, core: 2. Of those that a mesh axis runs over, the one named last changes fastest.
Arguments:
- features: bfloat16 [256, 1024, 64], P('rows', 'cols'), may hold values from -6 to 6
- hidden_prev: bfloat16 [256, 1024, 128], P('rows', 'cols'), may hold values from -6 to 6
- cell_prev: float32 [256, 1024, 128], P('rows', 'cols'), may hold values from -6 to 6
- kernel: bfloat16 [3, 3, 192, 512], replicated, may hold values from -0.15625 to 0.15625
- bias: float32 [512], replicated, may hold values from -3 to 3
- hidden_cot: bfloat16 [256, 1024, 128], P('rows', 'cols'), may hold values from -6 to 6
- cell_cot: float32 [256, 1024, 128], P('rows', 'cols'), may hold values from -6 to 6
Outputs:
- hidden_new: bfloat16 [256, 1024, 128], P('rows', 'cols')
- cell_new: float32 [256, 1024, 128], P('rows', 'cols')
- grad_features: bfloat16 [256, 1024, 64], P('rows', 'cols')
- grad_hidden: bfloat16 [256, 1024, 128], P('rows', 'cols')
- grad_cell: float32 [256, 1024, 128], P('rows', 'cols')
- grad_kernel: bfloat16 [3, 3, 192, 512], replicated
- grad_bias: float32 [512], replicated
All inputs are finite; a program needn't handle non-finite values.
Results may differ from a plain program's by a relative error of at most 0.0075.
Values may be sent and summed in bfloat16 or wider, within the bound.
No kernel may reach another device: no remote copies, remote signals or barrier semaphores. Data moves between devices by JAX's collectives and lax.ppermute only.
A program may use at most 64 MiB of HBM per device.

v0:
```python
import jax
import jax.numpy as jnp
from jax import lax
from jax.sharding import PartitionSpec as P


def with_halo(block, sides, width):
    for axis, dim in sides:
        count = lax.axis_size(axis)
        forward = [(i, i + 1) for i in range(count - 1)]
        backward = [(target, source) for source, target in forward]
        low = lax.ppermute(
            lax.slice_in_dim(block, block.shape[dim] - width, None, axis=dim), axis, forward
        )
        high = lax.ppermute(lax.slice_in_dim(block, 0, width, axis=dim), axis, backward)
        block = jnp.concatenate([low, block, high], axis=dim)
    return block


def patch_rows(padded, tile_rows, tile_cols, offsets):
    pieces = [padded[a : a + tile_rows, b : b + tile_cols] for a, b in offsets]
    return jnp.concatenate(pieces, axis=2).reshape(tile_rows * tile_cols, -1)


def local(features, hidden_prev, cell_prev, kernel, bias, hidden_cot, cell_cot):
    tile_rows, tile_cols, nfeat = features.shape
    chans = hidden_prev.shape[2]
    zch = nfeat + chans
    gate_count = 4 * chans
    forward_taps = [(a, b) for a in range(3) for b in range(3)]
    stacked = jnp.concatenate([features, hidden_prev], axis=2)
    padded = with_halo(stacked, (("rows", 0), ("cols", 1)), 1)
    source = patch_rows(padded, tile_rows, tile_cols, forward_taps)
    gates = (
        jnp.dot(source, kernel.reshape(9 * zch, gate_count), preferred_element_type=jnp.float32)
        + bias
    )
    gates = gates.reshape(tile_rows, tile_cols, gate_count)
    in_gate = jax.nn.sigmoid(gates[..., :chans])
    forget = jax.nn.sigmoid(gates[..., chans : 2 * chans])
    out_gate = jax.nn.sigmoid(gates[..., 2 * chans : 3 * chans])
    cand = jnp.tanh(gates[..., 3 * chans :])
    cell_new = forget * cell_prev + in_gate * cand
    squash = jnp.tanh(cell_new)
    hidden_new = (out_gate * squash).astype(jnp.bfloat16)
    hid_cot = hidden_cot.astype(jnp.float32)
    cell_total = cell_cot + hid_cot * out_gate * (1.0 - squash * squash)
    grad_cell = cell_total * forget
    grad_gates = jnp.concatenate(
        [
            cell_total * cand * in_gate * (1.0 - in_gate),
            cell_total * cell_prev * forget * (1.0 - forget),
            hid_cot * squash * out_gate * (1.0 - out_gate),
            cell_total * in_gate * (1.0 - cand * cand),
        ],
        axis=2,
    ).astype(jnp.bfloat16)
    grad_pad = with_halo(grad_gates, (("rows", 0), ("cols", 1)), 1)
    flat_grad = grad_gates.reshape(tile_rows * tile_cols, gate_count)
    kernel_term = lax.dot_general(
        source, flat_grad, (((0,), (0,)), ((), ())), preferred_element_type=jnp.float32
    )
    bias_term = jnp.sum(flat_grad.astype(jnp.float32), axis=0)[None, :]
    flipped = jnp.transpose(kernel[::-1, ::-1], (0, 1, 3, 2)).reshape(9 * gate_count, zch)
    grad_source = patch_rows(grad_pad, tile_rows, tile_cols, forward_taps)
    grad_stacked = jnp.dot(grad_source, flipped, preferred_element_type=jnp.float32)
    grad_stacked = grad_stacked.astype(jnp.bfloat16).reshape(tile_rows, tile_cols, zch)
    kernel_sum, bias_sum = lax.psum((kernel_term, bias_term), ("rows", "cols"))
    scale = 1.0 / (tile_rows * lax.axis_size("rows"))
    grad_kernel = (kernel_sum * scale).astype(jnp.bfloat16).reshape(3, 3, zch, gate_count)
    grad_bias = bias_sum[0] * scale
    return (
        hidden_new,
        cell_new,
        grad_stacked[..., :nfeat],
        grad_stacked[..., nfeat:],
        grad_cell,
        grad_kernel,
        grad_bias,
    )


def solution(mesh):
    in_specs = (
        P("rows", "cols", None),
        P("rows", "cols", None),
        P("rows", "cols", None),
        P(),
        P(),
        P("rows", "cols", None),
        P("rows", "cols", None),
    )
    out_specs = (
        P("rows", "cols", None),
        P("rows", "cols", None),
        P("rows", "cols", None),
        P("rows", "cols", None),
        P("rows", "cols", None),
        P(),
        P(),
    )
    return jax.shard_map(local, mesh=mesh, in_specs=in_specs, out_specs=out_specs, check_vma=False)
```

profile of v0, /device:TPU:1, one launch (start us, length us, event | category | flops | bytes accessed | tf_op | source)
XLA Modules:
  0.0 555.0 jit_solution(13216387500049517931)
XLA Ops:
  7.2 0.0 all-reduce.2.cloned.1.call-start
  7.2 0.9 pad_maximum_fusion.17
  8.1 1.3 collective-permute-start.1
  9.4 6.1 %collective-permute-start = (bf16[1,64,192]{2,1,0:T(8,128)(2,1)S(1)}, bf16[1,64,192]{2,1,0:T(8,128)(2,1)S(1)}, u32[]{:S(2)}, u32[]{:S(2)}) collective-permute-start(bf16[1,64,192]{2,1,0:T(8,128)(2,1)S(1)} %get-tuple-element.35), channel_id=1, source_target_pairs={{0,16},{16,32},{32,48},{48,64},{64,80},{80,96},{96,112},{112,128},... | collective-permute-start | bytes 73736 | tf_op jit(solution)/shard_map/ppermute | solution.py:12
  15.5 1.6 reverse_bitcast_fusion
  17.1 1.5 copy.16
  18.6 0.0 copy-start
  18.6 0.0 copy-start.1
  18.6 3.8 reshape.51
  22.4 0.0 collective-permute-done.1
  22.4 0.0 collective-permute-done
  22.4 0.0 copy-done
  22.4 0.0 copy-done.1
  22.4 0.1 pad_maximum_fusion.24
  22.5 8.7 %collective-permute-start.3 = (bf16[10,1,192]{2,1,0:T(2,128)(2,1)S(1)}, bf16[10,1,192]{2,1,0:T(2,128)(2,1)S(1)}, u32[]{:S(2)}, u32[]{:S(2)}) collective-permute-start(bf16[10,1,192]{2,1,0:T(2,128)(2,1)S(1)} %get-tuple-element.31), channel_id=1, source_target_pairs={{1,0},{2,1},{3,2},{4,3},{5,4},{6,5},{7,6},{8,7},{9,8},{10,9},{11,1... | collective-permute-start | bytes 11528 | tf_op jit(solution)/shard_map/ppermute | solution.py:15
  31.3 1.9 collective-permute-start.2
  33.2 1.0 pad_maximum_fusion.10
  34.2 0.0 collective-permute-done.3
  34.2 0.2 collective-permute-done.2
  34.3 0.3 pad_maximum_fusion.9
  34.6 0.8 fusion.26
  35.5 0.0 copy-start.7
  35.5 2.5 concatenate.73
  38.0 0.0 copy-done.7
  38.0 0.0 copy-start.3
  38.0 0.0 copy-start.5
  38.0 0.0 copy-start.6
  38.1 2.6 convolution_add_fusion
  40.7 0.0 copy-done.3
  40.7 0.0 copy-done.5
  40.7 0.0 copy-done.6
  40.7 1.0 fusion.24
  41.7 0.0 copy-start.4
  41.7 1.0 multiply_convert_fusion.3
  42.8 1.3 collective-permute-start.5
  44.1 5.5 collective-permute-start.4
  49.6 2.9 convolution_bitcast_fusion
  52.5 0.0 copy-done.4
  52.5 0.0 all-reduce.2.cloned.1.call-update
  52.5 0.1 convert_reduce_fusion
  52.6 110.7 %psum.15 = f32[1,512]{1,0:T(1,128)S(1)} all-reduce(f32[1,512]{1,0:T(1,128)S(1)} %bitcast.35), channel_id=1, replica_groups=mesh['rows'=32,'cols'=16] {'rows','cols'}, use_global_device_ids=true, to_apply=%region_2.0 | all-reduce | flops 512 | bytes 4096 | tf_op jit(solution)/shard_map/psum | solution.py:68
  163.4 0.0 collective-permute-done.5
  163.4 0.0 collective-permute-done.4
  163.4 2.9 collective-permute-start.7
  166.3 2.7 collective-permute-start.6
  169.0 0.6 broadcast_multiply_fusion
  169.6 0.0 collective-permute-done.7
  169.6 0.3 collective-permute-done.6
  169.9 0.4 pad_maximum_fusion
  170.3 0.1 fusion.1
  170.4 0.1 slice_dynamic-update-slice_fusion.4
  170.7 0.0 copy-start.2
  170.7 0.1 slice_dynamic-update-slice_fusion.2
  170.9 0.1 fusion
  171.0 0.1 slice_dynamic-update-slice_fusion
  171.1 1.0 copy-done.2
  172.1 1.7 convolution_convert_fusion
  173.8 0.1 copy.17
  174.0 0.7 slice.152
  174.6 0.8 slice.153
  175.4 369.0 %all-reduce.2.cloned.1.call-done = f32[1728,512]{1,0:T(8,128)} async-done(((f32[1728,512]{1,0:T(8,128)}), f32[1728,512]{1,0:T(8,128)}) %all-reduce.2.cloned.1.call-update) | async-done | bytes 3538960 | tf_op jit(solution)/shard_map/psum | solution.py:68
  544.4 3.7 multiply_convert_fusion
  (9 shorter events, 0.3 us)
Async XLA Ops:
  7.2 537.3 %all-reduce.2.cloned.1.call-start = ((), (), s32[]{:S(2)}) async-start(), calls=%async_computation | async-start | bytes 7077888 | tf_op jit(solution)/shard_map/psum | solution.py:68
  8.1 14.3 %collective-permute-start.1 = (bf16[1,64,192]{2,1,0:T(8,128)(2,1)S(1)}, bf16[1,64,192]{2,1,0:T(8,128)(2,1)S(1)}, u32[]{:S(2)}, u32[]{:S(2)}) collective-permute-start(bf16[1,64,192]{2,1,0:T(8,128)(2,1)S(1)} %get-tuple-element.36), channel_id=1, source_target_pairs={{16,0},{32,16},{48,32},{64,48},{80,64},{96,80},{112,96},{128,112},... | collective-permute-start | bytes 73736 | tf_op jit(solution)/shard_map/ppermute | solution.py:15
  9.4 13.0 %collective-permute-start = (bf16[1,64,192]{2,1,0:T(8,128)(2,1)S(1)}, bf16[1,64,192]{2,1,0:T(8,128)(2,1)S(1)}, u32[]{:S(2)}, u32[]{:S(2)}) collective-permute-start(bf16[1,64,192]{2,1,0:T(8,128)(2,1)S(1)} %get-tuple-element.35), channel_id=1, source_target_pairs={{0,16},{16,32},{32,48},{48,64},{64,80},{80,96},{96,112},{112,128},... | collective-permute-start | bytes 73736 | tf_op jit(solution)/shard_map/ppermute | solution.py:12
  18.6 3.8 copy-start
  18.6 3.8 copy-start.1
  22.5 11.7 %collective-permute-start.3 = (bf16[10,1,192]{2,1,0:T(2,128)(2,1)S(1)}, bf16[10,1,192]{2,1,0:T(2,128)(2,1)S(1)}, u32[]{:S(2)}, u32[]{:S(2)}) collective-permute-start(bf16[10,1,192]{2,1,0:T(2,128)(2,1)S(1)} %get-tuple-element.31), channel_id=1, source_target_pairs={{1,0},{2,1},{3,2},{4,3},{5,4},{6,5},{7,6},{8,7},{9,8},{10,9},{11,1... | collective-permute-start | bytes 11528 | tf_op jit(solution)/shard_map/ppermute | solution.py:15
  31.3 3.1 collective-permute-start.2
  35.5 2.6 copy-start.7
  38.0 2.7 copy-start.3
  38.0 2.7 copy-start.5
  38.0 2.7 copy-start.6
  41.7 10.8 %copy-start.4 = (f32[8,64,128]{2,1,0:T(8,128)}, f32[8,64,128]{2,1,0:T(8,128)S(1)}, u32[]{:S(2)}) copy-start(f32[8,64,128]{2,1,0:T(8,128)S(1)} %get-tuple-element.9) | copy-start | bytes 786436
  42.8 120.6 %collective-permute-start.5 = (bf16[1,64,512]{2,1,0:T(8,128)(2,1)S(1)}, bf16[1,64,512]{2,1,0:T(8,128)(2,1)S(1)}, u32[]{:S(2)}, u32[]{:S(2)}) collective-permute-start(bf16[1,64,512]{2,1,0:T(8,128)(2,1)S(1)} %get-tuple-element.22), channel_id=1, source_target_pairs={{16,0},{32,16},{48,32},{64,48},{80,64},{96,80},{112,96},{128,112},... | collective-permute-start | bytes 196616 | tf_op jit(solution)/shard_map/ppermute | solution.py:15
  44.1 119.3 %collective-permute-start.4 = (bf16[1,64,512]{2,1,0:T(8,128)(2,1)S(1)}, bf16[1,64,512]{2,1,0:T(8,128)(2,1)S(1)}, u32[]{:S(2)}, u32[]{:S(2)}) collective-permute-start(bf16[1,64,512]{2,1,0:T(8,128)(2,1)S(1)} %get-tuple-element.21), channel_id=1, source_target_pairs={{0,16},{16,32},{32,48},{48,64},{64,80},{80,96},{96,112},{112,128},... | collective-permute-start | bytes 196616 | tf_op jit(solution)/shard_map/ppermute | solution.py:12
  163.4 6.2 %collective-permute-start.7 = (bf16[10,1,512]{2,1,0:T(2,128)(2,1)S(1)}, bf16[10,1,512]{2,1,0:T(2,128)(2,1)S(1)}, u32[]{:S(2)}, u32[]{:S(2)}) collective-permute-start(bf16[10,1,512]{2,1,0:T(2,128)(2,1)S(1)} %get-tuple-element.19), channel_id=1, source_target_pairs={{1,0},{2,1},{3,2},{4,3},{5,4},{6,5},{7,6},{8,7},{9,8},{10,9},{11,1... | collective-permute-start | bytes 30728 | tf_op jit(solution)/shard_map/ppermute | solution.py:15
  166.3 3.6 collective-permute-start.6
  170.7 1.5 copy-start.2
Sparse Core Ops, SparseCore 0:
  52.6 491.7 all-reduce.1
where the time goes:
time: 556 us; the launch traced here: 555 us
  waiting for transfers between devices  370 us (67%)
  blocking collectives  111 us (20%)
  starting transfers between devices  30.4 us (5%)
  between operations  14.3 us (3%)
  local copies, waits for them, and re-layouts  13.5 us (2%)
  other arithmetic  9.17 us (2%)
  matrix products  7.24 us (1%)
    psum x1, waiting for transfers between devices, local(): kernel_sum, bias_sum = lax.psum((kernel_term, bias_term), ('rows', 'cols'))  369 us
    psum x1, blocking collectives, local(): kernel_sum, bias_sum = lax.psum((kernel_term, bias_term), ('rows', 'cols'))  111 us
    ppermute x4, starting transfers between devices, with_halo(): lax.ppermute(lax.slice_in_dim(block, block.shape[dim] - width, None, axis...  16.2 us
    ppermute x4, starting transfers between devices, with_halo(): lax.ppermute(lax.slice_in_dim(block, 0, width, axis=dim), axis, backward)  14.2 us
  transfers between devices with their start and end apart: 9, of which 3 were waited for; matrix products, arithmetic and copies ran while one was open for 3% of the time, Pallas kernels for 0%

commit v1 on v0

--- a/solution.py
+++ b/solution.py
@@ -1,7 +1,13 @@
 import jax
 import jax.numpy as jnp
 from jax import lax
-from jax.sharding import PartitionSpec as P
+from jax.sharding import Mesh, PartitionSpec as P
+
+ROWS = ("z", "xh")
+COLS = ("y", "xl", "core")
+PLANE = ("xh", "y", "xl")
+GROUP_ROWS = 216
+SLOT_ROWS = 224
 
 
 def with_halo(block, sides, width):
@@ -22,6 +28,36 @@
     return jnp.concatenate(pieces, axis=2).reshape(tile_rows * tile_cols, -1)
 
 
+def spread(part, axes, count):
+    copies = lax.optimization_barrier(jnp.broadcast_to(part[None], (count,) + part.shape))
+    return lax.all_to_all(copies, axes, 0, 0, tiled=True)
+
+
+def total_of(kernel_term, bias_term, scale):
+    bf16 = jnp.bfloat16
+    plane = lax.axis_size(PLANE)
+    depth = lax.axis_size("z")
+    groups = plane // 2
+    blocks = kernel_term.reshape(groups, GROUP_ROWS, 4, 128).transpose(2, 0, 1, 3)
+    extra = jnp.broadcast_to(
+        bias_term.reshape(4, 1, 1, 128), (4, groups, SLOT_ROWS - GROUP_ROWS, 128)
+    )
+    blocks = jnp.concatenate([blocks, extra], axis=2).reshape(2, plane, SLOT_ROWS, 128)
+    core = lax.axis_index("core")
+    mine = lax.dynamic_index_in_dim(blocks, core, 0, keepdims=False)
+    other = lax.dynamic_index_in_dim(blocks, 1 - core, 0, keepdims=False)
+    half = mine + lax.ppermute(other.astype(bf16), "core", [(0, 1), (1, 0)]).astype(jnp.float32)
+    part = lax.all_to_all(half.astype(bf16), PLANE, 0, 0, tiled=True)
+    part = jnp.sum(part.astype(jnp.float32), axis=0).astype(bf16)
+    part = lax.all_to_all(part.reshape(depth, SLOT_ROWS // depth, 128), "z", 0, 0, tiled=True)
+    part = (jnp.sum(part.astype(jnp.float32), axis=0) * scale).astype(bf16)
+    part = spread(part, "z", depth).reshape(SLOT_ROWS, 128)
+    half = spread(part, PLANE, plane)
+    whole = lax.all_gather(half, "core", axis=0).reshape(4, groups, SLOT_ROWS, 128)
+    grad_kernel = whole[:, :, :GROUP_ROWS].transpose(1, 2, 0, 3).reshape(groups * GROUP_ROWS, 512)
+    return grad_kernel, whole[:, 0, GROUP_ROWS].reshape(512).astype(jnp.float32)
+
+
 def local(features, hidden_prev, cell_prev, kernel, bias, hidden_cot, cell_cot):
     tile_rows, tile_cols, nfeat = features.shape
     chans = hidden_prev.shape[2]
@@ -29,7 +65,7 @@
     gate_count = 4 * chans
     forward_taps = [(a, b) for a in range(3) for b in range(3)]
     stacked = jnp.concatenate([features, hidden_prev], axis=2)
-    padded = with_halo(stacked, (("rows", 0), ("cols", 1)), 1)
+    padded = with_halo(stacked, ((ROWS, 0), (COLS, 1)), 1)
     source = patch_rows(padded, tile_rows, tile_cols, forward_taps)
     gates = (
         jnp.dot(source, kernel.reshape(9 * zch, gate_count), preferred_element_type=jnp.float32)
@@ -55,7 +91,7 @@
         ],
         axis=2,
     ).astype(jnp.bfloat16)
-    grad_pad = with_halo(grad_gates, (("rows", 0), ("cols", 1)), 1)
+    grad_pad = with_halo(grad_gates, ((ROWS, 0), (COLS, 1)), 1)
     flat_grad = grad_gates.reshape(tile_rows * tile_cols, gate_count)
     kernel_term = lax.dot_general(
         source, flat_grad, (((0,), (0,)), ((), ())), preferred_element_type=jnp.float32
@@ -65,38 +101,26 @@
     grad_source = patch_rows(grad_pad, tile_rows, tile_cols, forward_taps)
     grad_stacked = jnp.dot(grad_source, flipped, preferred_element_type=jnp.float32)
     grad_stacked = grad_stacked.astype(jnp.bfloat16).reshape(tile_rows, tile_cols, zch)
-    kernel_sum, bias_sum = lax.psum((kernel_term, bias_term), ("rows", "cols"))
-    scale = 1.0 / (tile_rows * lax.axis_size("rows"))
-    grad_kernel = (kernel_sum * scale).astype(jnp.bfloat16).reshape(3, 3, zch, gate_count)
-    grad_bias = bias_sum[0] * scale
+    scale = 1.0 / (tile_rows * lax.axis_size(ROWS))
+    grad_kernel, grad_bias = total_of(kernel_term, bias_term, scale)
     return (
         hidden_new,
         cell_new,
         grad_stacked[..., :nfeat],
         grad_stacked[..., nfeat:],
         grad_cell,
-        grad_kernel,
+        grad_kernel.reshape(3, 3, zch, gate_count),
         grad_bias,
     )
 
 
 def solution(mesh):
-    in_specs = (
-        P("rows", "cols", None),
-        P("rows", "cols", None),
-        P("rows", "cols", None),
-        P(),
-        P(),
-        P("rows", "cols", None),
-        P("rows", "cols", None),
+    grid = Mesh(mesh.devices.reshape(16, 2, 4, 2, 2), ROWS + COLS)
+    tile = P(ROWS, COLS, None)
+    return jax.shard_map(
+        local,
+        mesh=grid,
+        in_specs=(tile, tile, tile, P(), P(), tile, tile),
+        out_specs=(tile, tile, tile, tile, tile, P(), P()),
+        check_vma=False,
     )
-    out_specs = (
-        P("rows", "cols", None),
-        P("rows", "cols", None),
-        P("rows", "cols", None),
-        P("rows", "cols", None),
-        P("rows", "cols", None),
-        P(),
-        P(),
-    )
-    return jax.shard_map(local, mesh=mesh, in_specs=in_specs, out_specs=out_specs, check_vma=False)

time: 556 us -> 181 us (0.33)
  waiting for transfers between devices: 370 us -> 36.3 us
  blocking collectives: 111 us -> 23 us
  starting transfers between devices: 30.4 us -> 54.4 us
  local copies, waits for them, and re-layouts: 13.5 us -> 31.3 us
    psum x1 -> x0, waiting for transfers between devices: 369 us -> none  [local(): kernel_sum, bias_sum = lax.psum((kernel_term, bias_term), ('rows', 'cols'))]
    psum x1 -> x0, blocking collectives: 111 us -> none  [local(): kernel_sum, bias_sum = lax.psum((kernel_term, bias_term), ('rows', 'cols'))]
    all_to_all x0 -> x3, starting transfers between devices: none -> 27.9 us  [the longest x1 14.8 us: total_of(): lax.all_to_all(part.reshape(depth, SLOT_ROWS // depth, 128), 'z', 0, 0, t...]
    all_to_all x0 -> x1, blocking collectives: none -> 23 us  [total_of(): part = lax.all_to_all(half.astype(bf16), PLANE, 0, 0, tiled=True)]
    all_to_all x0 -> x3, waiting for transfers between devices: none -> 17.7 us  [the longest x2 9.69 us: spread(): return lax.all_to_all(copies, axes, 0, 0, tiled=True)]
    all_gather x0 -> x1, waiting for transfers between devices: none -> 11.2 us  [total_of(): lax.all_gather(half, 'core', axis=0).reshape(4, groups, SLOT_ROWS, 128)]
    unnamed x25 -> x31, local copies, waits for them, and re-layouts: 1.57 us -> 9.3 us
    ppermute x4, starting transfers between devices: 14.2 us -> 7.33 us  [with_halo(): lax.ppermute(lax.slice_in_dim(block, 0, width, axis=dim), axis, backward)]
  transfers between devices with their start and end apart: 9 -> 13, of which waited for: 3 -> 6; matrix products, arithmetic and copies ran while one was open for 3% -> 14% of each run, Pallas kernels for 0% -> 0%
where the time goes in v1:
time: 181 us; the launch traced here: 180 us
  starting transfers between devices  54.4 us (30%)
  waiting for transfers between devices  36.3 us (20%)
  local copies, waits for them, and re-layouts  31.3 us (17%)
  blocking collectives  23 us (13%)
  between operations  14.4 us (8%)
  other arithmetic  13 us (7%)
  matrix products  7.8 us (4%)
    all_to_all x1, blocking collectives, total_of(): part = lax.all_to_all(half.astype(bf16), PLANE, 0, 0, tiled=True)  23 us
    ppermute x4, starting transfers between devices, with_halo(): lax.ppermute(lax.slice_in_dim(block, block.shape[dim] - width, None, axis...  17 us
    all_to_all x1, starting transfers between devices, total_of(): lax.all_to_all(part.reshape(depth, SLOT_ROWS // depth, 128), 'z', 0, 0, t...  14.8 us
    all_to_all x2, starting transfers between devices, spread(): return lax.all_to_all(copies, axes, 0, 0, tiled=True)  13.1 us
    all_gather x1, waiting for transfers between devices, total_of(): lax.all_gather(half, 'core', axis=0).reshape(4, groups, SLOT_ROWS, 128)  11.2 us
    all_to_all x2, waiting for transfers between devices, spread(): return lax.all_to_all(copies, axes, 0, 0, tiled=True)  9.69 us
    unnamed x31, local copies, waits for them, and re-layouts  9.3 us
    all_to_all x1, waiting for transfers between devices, total_of(): lax.all_to_all(part.reshape(depth, SLOT_ROWS // depth, 128), 'z', 0, 0, t...  7.99 us
  transfers between devices with their start and end apart: 13, of which 6 were waited for; matrix products, arithmetic and copies ran while one was open for 14% of the time, Pallas kernels for 0%

profile of v1, /device:TPU:1, one launch (start us, length us, event | category | flops | bytes accessed | tf_op | source)
XLA Modules:
  0.0 180.2 jit_solution(8586463579758242066)
XLA Ops:
  7.2 0.9 pad_maximum_fusion.21
  8.0 5.5 %collective-permute-start = (bf16[1,64,192]{2,1,0:T(8,128)(2,1)S(1)}, bf16[1,64,192]{2,1,0:T(8,128)(2,1)S(1)}, u32[]{:S(2)}, u32[]{:S(2)}) collective-permute-start(bf16[1,64,192]{2,1,0:T(8,128)(2,1)S(1)} %get-tuple-element.37), channel_id=1, source_target_pairs={{0,16},{16,32},{32,48},{48,64},{64,80},{80,96},{96,112},{112,128},... | collective-permute-start | bytes 73736 | tf_op jit(solution)/shard_map/ppermute | solution.py:18
  13.5 1.3 collective-permute-start.1
  14.8 4.8 %collective-permute-done.1 = bf16[1,64,192]{2,1,0:T(8,128)(2,1)S(1)} collective-permute-done((bf16[1,64,192]{2,1,0:T(8,128)(2,1)S(1)}, bf16[1,64,192]{2,1,0:T(8,128)(2,1)S(1)}, u32[]{:S(2)}, u32[]{:S(2)}) %collective-permute-start.1) | collective-permute-done | bytes 24608 | tf_op jit(solution)/shard_map/ppermute | solution.py:21
  19.7 0.9 pad_maximum_fusion.28
  20.5 4.2 %collective-permute-start.2 = (bf16[10,1,192]{2,1,0:T(2,128)(2,1)S(1)}, bf16[10,1,192]{2,1,0:T(2,128)(2,1)S(1)}, u32[]{:S(2)}, u32[]{:S(2)}) collective-permute-start(bf16[10,1,192]{2,1,0:T(2,128)(2,1)S(1)} %get-tuple-element.34), channel_id=1, source_target_pairs={{0,1},{1,2},{2,3},{3,4},{4,5},{5,6},{6,7},{7,8},{8,9},{9,10},{10,1... | collective-permute-start | bytes 11528 | tf_op jit(solution)/shard_map/ppermute | solution.py:18
  24.8 2.8 %collective-permute-start.3 = (bf16[10,1,192]{2,1,0:T(2,128)(2,1)S(1)}, bf16[10,1,192]{2,1,0:T(2,128)(2,1)S(1)}, u32[]{:S(2)}, u32[]{:S(2)}) collective-permute-start(bf16[10,1,192]{2,1,0:T(2,128)(2,1)S(1)} %get-tuple-element.33), channel_id=1, source_target_pairs={{1,0},{2,1},{3,2},{4,3},{5,4},{6,5},{7,6},{8,7},{9,8},{10,9},{11,1... | collective-permute-start | bytes 11528 | tf_op jit(solution)/shard_map/ppermute | solution.py:21
  27.6 2.1 %pad_maximum_fusion.12 = (bf16[8,64,192]{2,1,0:T(8,128)(2,1)}, bf16[8,64,192]{2,1,0:T(8,128)(2,1)}) fusion(bf16[1,64,192]{2,1,0:T(8,128)(2,1)S(1)} %collective-permute-done.1, bf16[8,64,128]{2,1,0:T(8,128)(2,1)} %param.8, bf16[8,64,64]{2,1,0:T(8,128)(2,1)} %param.7, bf16[1,64,192]{2,1,0:T(8,128)(2,1)S(1)} %collective-permute-done), kind=kLoop, calls=%fused_computation.52 | loop fusion | flops 1179648 | bytes 638976 | tf_op jit(solution)/shard_map/concatenate | solution.py:22
  29.8 1.4 pad_maximum_fusion.11
  31.2 0.8 fusion.20
  32.1 2.5 %concatenate.76 = bf16[8,64,1728]{2,1,0:T(8,128)(2,1)S(1)} concatenate(bf16[8,64,192]{2,1,0:T(8,128)(2,1)S(1)} %get-tuple-element.39, bf16[8,64,192]{2,1,0:T(8,128)(2,1)} %get-tuple-element.36, bf16[8,64,192]{2,1,0:T(8,128)(2,1)S(1)} %get-tuple-element.27, bf16[8,64,192]{2,1,0:T(8,128)(2,1)S(1)} %get-tuple-element.40, bf16[8,64,64]{2,1,0:T(8,128)(2,1)S(1)} %copy-done.3, ...), dimensions={2} | concatenate | bytes 3538944 | tf_op jit(solution)/shard_map/concatenate | solution.py:28
  34.7 2.3 %copy.40 = bf16[512,1728]{0,1:T(8,128)(2,1)} copy(bf16[512,1728]{1,0:T(8,128)(2,1)S(1)} %bitcast.51) | data formatting | bytes 3538944 | tf_op jit(solution)/shard_map/reshape | solution.py:28
  37.0 2.6 %convolution_add_fusion = f32[512,512]{1,0:T(8,128)S(1)} fusion(bf16[512,1728]{1,0:T(8,128)(2,1)S(1)} %bitcast.52, bf16[1728,512]{1,0:T(8,128)(2,1)} %bitcast.57, f32[512]{0:T(512)S(1)} %copy-done.10), kind=kOutput, calls=%fused_computation.7 | convolution fusion | flops 906231808 | bytes 4589568 | tf_op jit(solution)/shard_map/dot_general | solution.py:71
  39.7 1.0 fusion.18
  40.7 1.0 multiply_convert_fusion.2
  42.2 0.1 convert_reduce_fusion
  42.3 1.1 convolution_bitcast_fusion
  43.5 0.4 pad_maximum_fusion
  43.9 0.3 copy.45
  44.2 1.8 copy-done
  46.0 0.1 fusion.1
  46.1 1.9 %collective-permute-start.8 = (bf16[16,224,128]{2,1,0:T(8,128)(2,1)S(1)}, bf16[16,224,128]{2,1,0:T(8,128)(2,1)S(1)}, u32[]{:S(2)}, u32[]{:S(2)}) collective-permute-start(bf16[16,224,128]{2,1,0:T(8,128)(2,1)S(1)} %fusion.1), channel_id=1, source_target_pairs={{0,1},{1,0},{2,3},{3,2},{4,5},{5,4},{6,7},{7,6},{8,9},{9,8},{10,11... | collective-permute-start | bytes 2752520 | tf_op jit(solution)/shard_map/ppermute | solution.py:49
  48.0 2.4 %collective-permute-done.8 = bf16[16,224,128]{2,1,0:T(8,128)(2,1)S(1)} collective-permute-done((bf16[16,224,128]{2,1,0:T(8,128)(2,1)S(1)}, bf16[16,224,128]{2,1,0:T(8,128)(2,1)S(1)}, u32[]{:S(2)}, u32[]{:S(2)}) %collective-permute-start.8) | collective-permute-done | bytes 917536 | tf_op jit(solution)/shard_map/ppermute | solution.py:49
  50.5 1.7 fusion
  52.2 23.0 %all_to_all.20 = bf16[16,224,128]{2,1,0:T(8,128)(2,1)S(1)} all-to-all(bf16[16,224,128]{2,1,0:T(8,128)(2,1)S(1)} %fusion), channel_id=1, replica_groups=mesh['z'=16,'xh'=2,'y'=4,'xl'=2,'core'=2] {'xh','y','xl'}, dimensions={0} | all-to-all | bytes 1835008 | tf_op jit(solution)/shard_map/all_to_all | solution.py:50
  75.2 0.1 reduce_sum.31
  75.3 0.7 reshape.70
  76.0 14.8 %all-to-all-start.1 = ((bf16[16,14,128]{2,1,0:T(8,128)(2,1)}), bf16[16,14,128]{2,1,0:T(8,128)(2,1)S(1)}, u32[]{:S(2)}, u32[]{:S(2)}) async-start(bf16[16,14,128]{2,1,0:T(8,128)(2,1)} %reshape.70), calls=%async_computation.1 | async-start | bytes 131072 | tf_op jit(solution)/shard_map/all_to_all | solution.py:52
  90.8 2.2 %collective-permute-start.4 = (bf16[1,64,512]{2,1,0:T(8,128)(2,1)S(1)}, bf16[1,64,512]{2,1,0:T(8,128)(2,1)S(1)}, u32[]{:S(2)}, u32[]{:S(2)}) collective-permute-start(bf16[1,64,512]{2,1,0:T(8,128)(2,1)S(1)} %get-tuple-element.23), channel_id=1, source_target_pairs={{0,16},{16,32},{32,48},{48,64},{64,80},{80,96},{96,112},{112,128},... | collective-permute-start | bytes 196616 | tf_op jit(solution)/shard_map/ppermute | solution.py:18
  93.0 1.3 collective-permute-start.5
  94.3 8.0 %all-to-all-done.1 = bf16[16,14,128]{2,1,0:T(8,128)(2,1)S(1)} async-done(((bf16[16,14,128]{2,1,0:T(8,128)(2,1)}), bf16[16,14,128]{2,1,0:T(8,128)(2,1)S(1)}, u32[]{:S(2)}, u32[]{:S(2)}) %all-to-all-start.1) | async-done | bytes 57376 | tf_op jit(solution)/shard_map/all_to_all | solution.py:52
  102.3 0.6 broadcast_in_dim.23
  103.0 8.8 %all-to-all-start.2 = ((bf16[16,14,128]{2,1,0:T(8,128)(2,1)}), bf16[16,14,128]{2,1,0:T(8,128)(2,1)S(1)}, u32[]{:S(2)}, u32[]{:S(2)}) async-start(bf16[16,14,128]{2,1,0:T(8,128)(2,1)} %broadcast_in_dim.23), calls=%async_computation.2 | async-start | bytes 131072 | tf_op jit(solution)/shard_map/all_to_all | solution.py:33
  111.9 5.0 %collective-permute-start.6 = (bf16[10,1,512]{2,1,0:T(2,128)(2,1)S(1)}, bf16[10,1,512]{2,1,0:T(2,128)(2,1)S(1)}, u32[]{:S(2)}, u32[]{:S(2)}) collective-permute-start(bf16[10,1,512]{2,1,0:T(2,128)(2,1)S(1)} %get-tuple-element.22), channel_id=1, source_target_pairs={{0,1},{1,2},{2,3},{3,4},{4,5},{5,6},{6,7},{7,8},{8,9},{9,10},{10,1... | collective-permute-start | bytes 30728 | tf_op jit(solution)/shard_map/ppermute | solution.py:18
  117.0 1.9 %collective-permute-start.7 = (bf16[10,1,512]{2,1,0:T(2,128)(2,1)S(1)}, bf16[10,1,512]{2,1,0:T(2,128)(2,1)S(1)}, u32[]{:S(2)}, u32[]{:S(2)}) collective-permute-start(bf16[10,1,512]{2,1,0:T(2,128)(2,1)S(1)} %get-tuple-element.21), channel_id=1, source_target_pairs={{1,0},{2,1},{3,2},{4,3},{5,4},{6,5},{7,6},{8,7},{9,8},{10,9},{11,1... | collective-permute-start | bytes 30728 | tf_op jit(solution)/shard_map/ppermute | solution.py:21
  118.9 0.2 reverse_bitcast_fusion
  119.1 1.5 copy.38
  120.6 3.8 %reshape.67 = bf16[4608,192]{0,1:T(8,128)(2,1)} reshape(bf16[3,3,512,192]{2,1,0,3:T(4,128)(2,1)S(1)} %copy.38) | data formatting | bytes 3538944 | tf_op jit(solution)/shard_map/reshape | solution.py:100
  124.4 1.1 broadcast_in_dim.25
  125.5 4.3 %all-to-all-start.3 = ((bf16[16,224,128]{2,1,0:T(8,128)(2,1)}), bf16[16,224,128]{2,1,0:T(8,128)(2,1)}, u32[]{:S(2)}, u32[]{:S(2)}) async-start(bf16[16,224,128]{2,1,0:T(8,128)(2,1)} %broadcast_in_dim.25), calls=%async_computation.3 | async-start | bytes 1835008 | tf_op jit(solution)/shard_map/all_to_all | solution.py:33
  129.8 0.2 all-gather.3.cloned.1.call-start
  130.0 0.4 pad_maximum_fusion.1
  130.4 0.9 slice_dynamic-update-slice_fusion.5
  131.3 0.9 fusion.3
  132.2 1.0 slice_dynamic-update-slice_fusion.4
  133.2 9.7 %all-to-all-done.3 = bf16[16,224,128]{2,1,0:T(8,128)(2,1)} async-done(((bf16[16,224,128]{2,1,0:T(8,128)(2,1)}), bf16[16,224,128]{2,1,0:T(8,128)(2,1)}, u32[]{:S(2)}, u32[]{:S(2)}) %all-to-all-start.3) | async-done | bytes 917536 | tf_op jit(solution)/shard_map/all_to_all | solution.py:33
  142.9 0.9 slice_dynamic-update-slice_fusion.3
  143.8 0.7 constant_dynamic-update-slice_fusion.3
  144.5 0.7 constant_dynamic-update-slice_fusion.2
  145.2 0.7 constant_dynamic-update-slice_fusion.1
  145.8 0.7 constant_dynamic-update-slice_fusion
  146.6 0.9 slice_dynamic-update-slice_fusion.2
  147.5 0.9 slice_dynamic-update-slice_fusion.1
  148.4 0.9 fusion.2
  149.3 0.9 slice_dynamic-update-slice_fusion
  150.2 4.0 %convolution_convert_fusion = bf16[512,192]{0,1:T(8,128)(2,1)S(1)} fusion(bf16[512,4608]{1,0:T(8,128)(2,1)} %bitcast.3, bf16[4608,192]{0,1:T(8,128)(2,1)S(1)} %copy-done.5), kind=kOutput, calls=%fused_computation.8 | convolution fusion | flops 906067968 | bytes 6684672 | tf_op jit(solution)/shard_map/dot_general | solution.py:102
  154.2 0.1 copy.39
  154.4 0.7 slice.160
  155.0 0.8 slice.161
  155.8 11.2 %all-gather.3.cloned.1.call-done = bf16[32,224,128]{2,1,0:T(8,128)(2,1)} async-done(((bf16[16,224,128]{2,1,0:T(8,128)(2,1)}), bf16[32,224,128]{2,1,0:T(8,128)(2,1)}) %all-gather.3.cloned.1.call-update) | async-done | bytes 1835024 | tf_op jit(solution)/shard_map/all_gather | solution.py:56
  167.0 1.6 slice_bitcast_fusion
  168.6 1.3 slice_convert_fusion
  169.9 1.4 copy.46
  171.3 2.1 %reshape_reshape.3 = bf16[3,3,192,512]{3,2,1,0:T(8,128)(2,1)} reshape(bf16[8,216,4,128]{3,2,1,0:T(4,128)(2,1)S(1)} %copy.46) | data formatting | bytes 3538944 | tf_op jit(solution)/shard_map/reshape;reshape | solution.py:112
  (40 shorter events, 0.8 us)
Async XLA Ops:
  8.0 6.8 %collective-permute-start = (bf16[1,64,192]{2,1,0:T(8,128)(2,1)S(1)}, bf16[1,64,192]{2,1,0:T(8,128)(2,1)S(1)}, u32[]{:S(2)}, u32[]{:S(2)}) collective-permute-start(bf16[1,64,192]{2,1,0:T(8,128)(2,1)S(1)} %get-tuple-element.37), channel_id=1, source_target_pairs={{0,16},{16,32},{32,48},{48,64},{64,80},{80,96},{96,112},{112,128},... | collective-permute-start | bytes 73736 | tf_op jit(solution)/shard_map/ppermute | solution.py:18
  13.5 6.2 %collective-permute-start.1 = (bf16[1,64,192]{2,1,0:T(8,128)(2,1)S(1)}, bf16[1,64,192]{2,1,0:T(8,128)(2,1)S(1)}, u32[]{:S(2)}, u32[]{:S(2)}) collective-permute-start(bf16[1,64,192]{2,1,0:T(8,128)(2,1)S(1)} %get-tuple-element.38), channel_id=1, source_target_pairs={{16,0},{32,16},{48,32},{64,48},{80,64},{96,80},{112,96},{128,112},... | collective-permute-start | bytes 73736 | tf_op jit(solution)/shard_map/ppermute | solution.py:21
  20.5 9.1 %collective-permute-start.2 = (bf16[10,1,192]{2,1,0:T(2,128)(2,1)S(1)}, bf16[10,1,192]{2,1,0:T(2,128)(2,1)S(1)}, u32[]{:S(2)}, u32[]{:S(2)}) collective-permute-start(bf16[10,1,192]{2,1,0:T(2,128)(2,1)S(1)} %get-tuple-element.34), channel_id=1, source_target_pairs={{0,1},{1,2},{2,3},{3,4},{4,5},{5,6},{6,7},{7,8},{8,9},{9,10},{10,1... | collective-permute-start | bytes 11528 | tf_op jit(solution)/shard_map/ppermute | solution.py:18
  24.8 5.0 %collective-permute-start.3 = (bf16[10,1,192]{2,1,0:T(2,128)(2,1)S(1)}, bf16[10,1,192]{2,1,0:T(2,128)(2,1)S(1)}, u32[]{:S(2)}, u32[]{:S(2)}) collective-permute-start(bf16[10,1,192]{2,1,0:T(2,128)(2,1)S(1)} %get-tuple-element.33), channel_id=1, source_target_pairs={{1,0},{2,1},{3,2},{4,3},{5,4},{6,5},{7,6},{8,7},{9,8},{10,9},{11,1... | collective-permute-start | bytes 11528 | tf_op jit(solution)/shard_map/ppermute | solution.py:21
  31.2 0.9 copy-start.2
  31.2 1.0 copy-start.3
  34.7 2.3 %copy-start.10 = (f32[512]{0:T(512)S(1)}, f32[512]{0:T(512)}, u32[]{:S(2)}) copy-start(f32[512]{0:T(512)} %param.11) | copy-start | bytes 6148
  37.0 2.7 %copy-start.6 = (f32[8,64,128]{2,1,0:T(8,128)S(1)}, f32[8,64,128]{2,1,0:T(8,128)}, u32[]{:S(2)}) copy-start(f32[8,64,128]{2,1,0:T(8,128)} %param.9) | copy-start | bytes 786436
  37.0 2.7 %copy-start.8 = (bf16[8,64,128]{2,1,0:T(8,128)(2,1)S(1)}, bf16[8,64,128]{2,1,0:T(8,128)(2,1)}, u32[]{:S(2)}) copy-start(bf16[8,64,128]{2,1,0:T(8,128)(2,1)} %param.12) | copy-start | bytes 393220
  37.0 2.7 %copy-start.9 = (f32[8,64,128]{2,1,0:T(8,128)S(1)}, f32[8,64,128]{2,1,0:T(8,128)}, u32[]{:S(2)}) copy-start(f32[8,64,128]{2,1,0:T(8,128)} %param.13) | copy-start | bytes 786436
  40.7 1.5 copy-start.7
  40.7 1.7 copy-start.1
  44.2 1.8 copy-start
  46.1 4.4 %collective-permute-start.8 = (bf16[16,224,128]{2,1,0:T(8,128)(2,1)S(1)}, bf16[16,224,128]{2,1,0:T(8,128)(2,1)S(1)}, u32[]{:S(2)}, u32[]{:S(2)}) collective-permute-start(bf16[16,224,128]{2,1,0:T(8,128)(2,1)S(1)} %fusion.1), channel_id=1, source_target_pairs={{0,1},{1,0},{2,3},{3,2},{4,5},{5,4},{6,7},{7,6},{8,9},{9,8},{10,11... | collective-permute-start | bytes 2752520 | tf_op jit(solution)/shard_map/ppermute | solution.py:49
  75.2 43.7 %copy-start.4 = (bf16[3,3,192,512]{3,2,1,0:T(8,128)(2,1)S(1)}, bf16[3,3,192,512]{3,2,1,0:T(8,128)(2,1)}, u32[]{:S(2)}) copy-start(bf16[3,3,192,512]{3,2,1,0:T(8,128)(2,1)} %param.10) | copy-start | bytes 5308420
  76.0 26.3 %all-to-all-start.1 = ((bf16[16,14,128]{2,1,0:T(8,128)(2,1)}), bf16[16,14,128]{2,1,0:T(8,128)(2,1)S(1)}, u32[]{:S(2)}, u32[]{:S(2)}) async-start(bf16[16,14,128]{2,1,0:T(8,128)(2,1)} %reshape.70), calls=%async_computation.1 | async-start | bytes 131072 | tf_op jit(solution)/shard_map/all_to_all | solution.py:52
  90.8 21.1 %collective-permute-start.4 = (bf16[1,64,512]{2,1,0:T(8,128)(2,1)S(1)}, bf16[1,64,512]{2,1,0:T(8,128)(2,1)S(1)}, u32[]{:S(2)}, u32[]{:S(2)}) collective-permute-start(bf16[1,64,512]{2,1,0:T(8,128)(2,1)S(1)} %get-tuple-element.23), channel_id=1, source_target_pairs={{0,16},{16,32},{32,48},{48,64},{64,80},{80,96},{96,112},{112,128},... | collective-permute-start | bytes 196616 | tf_op jit(solution)/shard_map/ppermute | solution.py:18
  93.0 18.8 %collective-permute-start.5 = (bf16[1,64,512]{2,1,0:T(8,128)(2,1)S(1)}, bf16[1,64,512]{2,1,0:T(8,128)(2,1)S(1)}, u32[]{:S(2)}, u32[]{:S(2)}) collective-permute-start(bf16[1,64,512]{2,1,0:T(8,128)(2,1)S(1)} %get-tuple-element.24), channel_id=1, source_target_pairs={{16,0},{32,16},{48,32},{64,48},{80,64},{96,80},{112,96},{128,112},... | collective-permute-start | bytes 196616 | tf_op jit(solution)/shard_map/ppermute | solution.py:21
  103.0 21.4 %all-to-all-start.2 = ((bf16[16,14,128]{2,1,0:T(8,128)(2,1)}), bf16[16,14,128]{2,1,0:T(8,128)(2,1)S(1)}, u32[]{:S(2)}, u32[]{:S(2)}) async-start(bf16[16,14,128]{2,1,0:T(8,128)(2,1)} %broadcast_in_dim.23), calls=%async_computation.2 | async-start | bytes 131072 | tf_op jit(solution)/shard_map/all_to_all | solution.py:33
  111.9 18.1 %collective-permute-start.6 = (bf16[10,1,512]{2,1,0:T(2,128)(2,1)S(1)}, bf16[10,1,512]{2,1,0:T(2,128)(2,1)S(1)}, u32[]{:S(2)}, u32[]{:S(2)}) collective-permute-start(bf16[10,1,512]{2,1,0:T(2,128)(2,1)S(1)} %get-tuple-element.22), channel_id=1, source_target_pairs={{0,1},{1,2},{2,3},{3,4},{4,5},{5,6},{6,7},{7,8},{8,9},{9,10},{10,1... | collective-permute-start | bytes 30728 | tf_op jit(solution)/shard_map/ppermute | solution.py:18
  117.0 13.1 %collective-permute-start.7 = (bf16[10,1,512]{2,1,0:T(2,128)(2,1)S(1)}, bf16[10,1,512]{2,1,0:T(2,128)(2,1)S(1)}, u32[]{:S(2)}, u32[]{:S(2)}) collective-permute-start(bf16[10,1,512]{2,1,0:T(2,128)(2,1)S(1)} %get-tuple-element.21), channel_id=1, source_target_pairs={{1,0},{2,1},{3,2},{4,3},{5,4},{6,5},{7,6},{8,7},{9,8},{10,9},{11,1... | collective-permute-start | bytes 30728 | tf_op jit(solution)/shard_map/ppermute | solution.py:21
  125.5 17.4 %all-to-all-start.3 = ((bf16[16,224,128]{2,1,0:T(8,128)(2,1)}), bf16[16,224,128]{2,1,0:T(8,128)(2,1)}, u32[]{:S(2)}, u32[]{:S(2)}) async-start(bf16[16,224,128]{2,1,0:T(8,128)(2,1)} %broadcast_in_dim.25), calls=%async_computation.3 | async-start | bytes 1835008 | tf_op jit(solution)/shard_map/all_to_all | solution.py:33
  129.8 37.3 %all-gather.3.cloned.1.call-start = ((), (), s32[]{:S(2)}) async-start(), calls=%async_computation.4 | async-start | bytes 2752512 | tf_op jit(solution)/shard_map/all_gather | solution.py:56
  147.5 2.7 %copy-start.5 = (bf16[4608,192]{0,1:T(8,128)(2,1)S(1)}, bf16[4608,192]{0,1:T(8,128)(2,1)}, u32[]{:S(2)}) copy-start(bf16[4608,192]{0,1:T(8,128)(2,1)} %reshape.67) | copy-start | bytes 5308420
Sparse Core Ops, SparseCore 0:
  143.0 23.9 all-gather.2

commit v2 on v1

--- a/solution.py
+++ b/solution.py
@@ -53,7 +53,10 @@
     part = (jnp.sum(part.astype(jnp.float32), axis=0) * scale).astype(bf16)
     part = spread(part, "z", depth).reshape(SLOT_ROWS, 128)
     half = spread(part, PLANE, plane)
-    whole = lax.all_gather(half, "core", axis=0).reshape(4, groups, SLOT_ROWS, 128)
+    swapped = lax.ppermute(half, "core", [(0, 1), (1, 0)])
+    first = jnp.where(core == 0, half, swapped)
+    second = jnp.where(core == 0, swapped, half)
+    whole = jnp.stack([first, second]).reshape(4, groups, SLOT_ROWS, 128)
     grad_kernel = whole[:, :, :GROUP_ROWS].transpose(1, 2, 0, 3).reshape(groups * GROUP_ROWS, 512)
     return grad_kernel, whole[:, 0, GROUP_ROWS].reshape(512).astype(jnp.float32)
 

time: 181 us -> 171 us (0.945)
  blocking collectives: 23 us -> 0 us
  between operations: 14.4 us -> 1.03 us
  starting transfers between devices: 54.4 us -> 66.9 us
  waiting for transfers between devices: 36.3 us -> 45.3 us
  other arithmetic: 13 us -> 16 us
    all_to_all x1 -> x0, blocking collectives: 23 us -> none  [total_of(): part = lax.all_to_all(half.astype(bf16), PLANE, 0, 0, tiled=True)]
    all_gather x1 -> x0, waiting for transfers between devices: 11.2 us -> none  [total_of(): lax.all_gather(half, 'core', axis=0).reshape(4, groups, SLOT_ROWS, 128)]
    all_to_all x2, waiting for transfers between devices: 9.69 us -> 19.3 us  [spread(): return lax.all_to_all(copies, axes, 0, 0, tiled=True)]
    all_to_all x0 -> x1, starting transfers between devices: none -> 8.26 us  [total_of(): part = lax.all_to_all(half.astype(bf16), PLANE, 0, 0, tiled=True)]
    ppermute x4, waiting for transfers between devices: 0.01 us -> 6.75 us  [with_halo(): lax.ppermute(lax.slice_in_dim(block, block.shape[dim] - width, None, axis...]
    ppermute x0 -> x1, starting transfers between devices: none -> 6.17 us  [total_of(): swapped = lax.ppermute(half, 'core', [(0, 1), (1, 0)])]
    all_to_all x2, starting transfers between devices: 13.1 us -> 8.63 us  [spread(): return lax.all_to_all(copies, axes, 0, 0, tiled=True)]
    transpose x2, local copies, waits for them, and re-layouts: 1.69 us -> 4.38 us  [local(): jnp.transpose(kernel[::-1, ::-1], (0, 1, 3, 2)).reshape(9 * gate_count, zch)]
  transfers between devices with their start and end apart: 13 -> 14, of which waited for: 6 -> 8; matrix products, arithmetic and copies ran while one was open for 14% -> 16% of each run, Pallas kernels for 0% -> 0%
where the time goes in v2:
time: 171 us; the launch traced here: 169 us
  starting transfers between devices  66.9 us (39%)
  waiting for transfers between devices  45.3 us (26%)
  local copies, waits for them, and re-layouts  32.4 us (19%)
  other arithmetic  16 us (9%)
  matrix products  7.8 us (5%)
    all_to_all x2, waiting for transfers between devices, spread(): return lax.all_to_all(copies, axes, 0, 0, tiled=True)  19.3 us
    ppermute x4, starting transfers between devices, with_halo(): lax.ppermute(lax.slice_in_dim(block, block.shape[dim] - width, None, axis...  18.1 us
    all_to_all x1, starting transfers between devices, total_of(): lax.all_to_all(part.reshape(depth, SLOT_ROWS // depth, 128), 'z', 0, 0, t...  16.5 us
    all_to_all x1, waiting for transfers between devices, total_of(): lax.all_to_all(part.reshape(depth, SLOT_ROWS // depth, 128), 'z', 0, 0, t...  10.3 us
    unnamed x31, local copies, waits for them, and re-layouts  9.2 us
    all_to_all x2, starting transfers between devices, spread(): return lax.all_to_all(copies, axes, 0, 0, tiled=True)  8.63 us
    all_to_all x1, starting transfers between devices, total_of(): part = lax.all_to_all(half.astype(bf16), PLANE, 0, 0, tiled=True)  8.26 us
    ppermute x4, starting transfers between devices, with_halo(): lax.ppermute(lax.slice_in_dim(block, 0, width, axis=dim), axis, backward)  7.33 us
  transfers between devices with their start and end apart: 14, of which 8 were waited for; matrix products, arithmetic and copies ran while one was open for 16% of the time, Pallas kernels for 0%

profile of v2, /device:TPU:1, one launch (start us, length us, event | category | flops | bytes accessed | tf_op | source)
XLA Modules:
  0.0 169.4 jit_solution(16517317491965582440)
XLA Ops:
  0.6 0.9 pad_maximum_fusion.22
  1.5 5.5 %collective-permute-start = (bf16[1,64,192]{2,1,0:T(8,128)(2,1)S(1)}, bf16[1,64,192]{2,1,0:T(8,128)(2,1)S(1)}, u32[]{:S(2)}, u32[]{:S(2)}) collective-permute-start(bf16[1,64,192]{2,1,0:T(8,128)(2,1)S(1)} %get-tuple-element.39), channel_id=1, source_target_pairs={{0,16},{16,32},{32,48},{48,64},{64,80},{80,96},{96,112},{112,128},... | collective-permute-start | bytes 73736 | tf_op jit(solution)/shard_map/ppermute | solution.py:18
  7.0 1.3 collective-permute-start.1
  8.3 4.8 %collective-permute-done.1 = bf16[1,64,192]{2,1,0:T(8,128)(2,1)S(1)} collective-permute-done((bf16[1,64,192]{2,1,0:T(8,128)(2,1)S(1)}, bf16[1,64,192]{2,1,0:T(8,128)(2,1)S(1)}, u32[]{:S(2)}, u32[]{:S(2)}) %collective-permute-start.1) | collective-permute-done | bytes 24608 | tf_op jit(solution)/shard_map/ppermute | solution.py:21
  13.1 0.9 pad_maximum_fusion.29
  14.0 4.2 %collective-permute-start.2 = (bf16[10,1,192]{2,1,0:T(2,128)(2,1)S(1)}, bf16[10,1,192]{2,1,0:T(2,128)(2,1)S(1)}, u32[]{:S(2)}, u32[]{:S(2)}) collective-permute-start(bf16[10,1,192]{2,1,0:T(2,128)(2,1)S(1)} %get-tuple-element.36), channel_id=1, source_target_pairs={{0,1},{1,2},{2,3},{3,4},{4,5},{5,6},{6,7},{7,8},{8,9},{9,10},{10,1... | collective-permute-start | bytes 11528 | tf_op jit(solution)/shard_map/ppermute | solution.py:18
  18.2 2.8 %collective-permute-start.3 = (bf16[10,1,192]{2,1,0:T(2,128)(2,1)S(1)}, bf16[10,1,192]{2,1,0:T(2,128)(2,1)S(1)}, u32[]{:S(2)}, u32[]{:S(2)}) collective-permute-start(bf16[10,1,192]{2,1,0:T(2,128)(2,1)S(1)} %get-tuple-element.35), channel_id=1, source_target_pairs={{1,0},{2,1},{3,2},{4,3},{5,4},{6,5},{7,6},{8,7},{9,8},{10,9},{11,1... | collective-permute-start | bytes 11528 | tf_op jit(solution)/shard_map/ppermute | solution.py:21
  21.1 2.1 %pad_maximum_fusion.13 = (bf16[8,64,192]{2,1,0:T(8,128)(2,1)}, bf16[8,64,192]{2,1,0:T(8,128)(2,1)}) fusion(bf16[1,64,192]{2,1,0:T(8,128)(2,1)S(1)} %collective-permute-done.1, bf16[8,64,128]{2,1,0:T(8,128)(2,1)} %param.8, bf16[8,64,64]{2,1,0:T(8,128)(2,1)} %param.7, bf16[1,64,192]{2,1,0:T(8,128)(2,1)S(1)} %collective-permute-done), kind=kLoop, calls=%fused_computation.55 | loop fusion | flops 1179648 | bytes 638976 | tf_op jit(solution)/shard_map/concatenate | solution.py:22
  23.2 1.4 pad_maximum_fusion.12
  24.6 0.8 fusion.20
  25.6 2.5 %concatenate.76 = bf16[8,64,1728]{2,1,0:T(8,128)(2,1)S(1)} concatenate(bf16[8,64,192]{2,1,0:T(8,128)(2,1)S(1)} %get-tuple-element.41, bf16[8,64,192]{2,1,0:T(8,128)(2,1)} %get-tuple-element.38, bf16[8,64,192]{2,1,0:T(8,128)(2,1)S(1)} %get-tuple-element.29, bf16[8,64,192]{2,1,0:T(8,128)(2,1)S(1)} %get-tuple-element.42, bf16[8,64,64]{2,1,0:T(8,128)(2,1)S(1)} %copy-done.3, ...), dimensions={2} | concatenate | bytes 3538944 | tf_op jit(solution)/shard_map/concatenate | solution.py:28
  28.1 2.3 %copy.31 = bf16[512,1728]{0,1:T(8,128)(2,1)} copy(bf16[512,1728]{1,0:T(8,128)(2,1)S(1)} %bitcast.55) | data formatting | bytes 3538944 | tf_op jit(solution)/shard_map/reshape | solution.py:28
  30.5 2.6 %convolution_add_fusion = f32[512,512]{1,0:T(8,128)S(1)} fusion(bf16[512,1728]{1,0:T(8,128)(2,1)S(1)} %bitcast.56, bf16[1728,512]{1,0:T(8,128)(2,1)} %bitcast.63, f32[512]{0:T(512)S(1)} %copy-done.10), kind=kOutput, calls=%fused_computation.8 | convolution fusion | flops 906231808 | bytes 4589568 | tf_op jit(solution)/shard_map/dot_general | solution.py:74
  33.1 1.0 fusion.18
  34.1 1.0 multiply_convert_fusion.2
  35.8 1.1 convolution_bitcast_fusion
  37.0 0.4 pad_maximum_fusion
  37.4 0.3 copy.36
  37.7 1.8 %copy-done = f32[4,8,224,128]{3,2,1,0:T(8,128)} copy-done((f32[4,8,224,128]{3,2,1,0:T(8,128)}, f32[4,8,224,128]{3,2,1,0:T(8,128)S(1)}, u32[]{:S(2)}) %copy-start) | copy-done | bytes 3670040
  39.6 1.9 %collective-permute-start.8 = (bf16[16,224,128]{2,1,0:T(8,128)(2,1)S(1)}, bf16[16,224,128]{2,1,0:T(8,128)(2,1)S(1)}, u32[]{:S(2)}, u32[]{:S(2)}) collective-permute-start(bf16[16,224,128]{2,1,0:T(8,128)(2,1)S(1)} %fusion.1), channel_id=1, source_target_pairs={{0,1},{1,0},{2,3},{3,2},{4,5},{5,4},{6,7},{7,6},{8,9},{9,8},{10,11... | collective-permute-start | bytes 2752520 | tf_op jit(solution)/shard_map/ppermute | solution.py:49
  41.5 2.4 %collective-permute-done.8 = bf16[16,224,128]{2,1,0:T(8,128)(2,1)S(1)} collective-permute-done((bf16[16,224,128]{2,1,0:T(8,128)(2,1)S(1)}, bf16[16,224,128]{2,1,0:T(8,128)(2,1)S(1)}, u32[]{:S(2)}, u32[]{:S(2)}) %collective-permute-start.8) | collective-permute-done | bytes 917536 | tf_op jit(solution)/shard_map/ppermute | solution.py:49
  44.0 2.6 %fusion = bf16[16,224,128]{2,1,0:T(8,128)(2,1)} fusion(bf16[16,224,128]{2,1,0:T(8,128)(2,1)S(1)} %collective-permute-done.8, f32[2,16,224,128]{3,2,1,0:T(8,128)} %bitcast.50, s32[]{:T(128)S(6)} %select_n.20), kind=kLoop, calls=%fused_computation.4 | loop fusion | flops 1376256 | bytes 3670020 | tf_op jit(solution)/shard_map/convert_element_type | solution.py:50
  46.6 8.3 %all-to-all-start = ((bf16[16,224,128]{2,1,0:T(8,128)(2,1)}), bf16[16,224,128]{2,1,0:T(8,128)(2,1)}, u32[]{:S(2)}, u32[]{:S(2)}) async-start(bf16[16,224,128]{2,1,0:T(8,128)(2,1)} %fusion), calls=%async_computation | async-start | bytes 1835008 | tf_op jit(solution)/shard_map/all_to_all | solution.py:50
  54.9 4.7 %collective-permute-start.4 = (bf16[1,64,512]{2,1,0:T(8,128)(2,1)S(1)}, bf16[1,64,512]{2,1,0:T(8,128)(2,1)S(1)}, u32[]{:S(2)}, u32[]{:S(2)}) collective-permute-start(bf16[1,64,512]{2,1,0:T(8,128)(2,1)S(1)} %get-tuple-element.25), channel_id=1, source_target_pairs={{0,16},{16,32},{32,48},{48,64},{64,80},{80,96},{96,112},{112,128},... | collective-permute-start | bytes 196616 | tf_op jit(solution)/shard_map/ppermute | solution.py:18
  59.6 1.3 collective-permute-start.5
  60.9 6.7 %collective-permute-done.4 = bf16[1,64,512]{2,1,0:T(8,128)(2,1)S(1)} collective-permute-done((bf16[1,64,512]{2,1,0:T(8,128)(2,1)S(1)}, bf16[1,64,512]{2,1,0:T(8,128)(2,1)S(1)}, u32[]{:S(2)}, u32[]{:S(2)}) %collective-permute-start.4) | collective-permute-done | bytes 65568 | tf_op jit(solution)/shard_map/ppermute | solution.py:18
  67.6 1.6 collective-permute-done.5
  69.3 3.6 %collective-permute-start.6 = (bf16[10,1,512]{2,1,0:T(2,128)(2,1)S(1)}, bf16[10,1,512]{2,1,0:T(2,128)(2,1)S(1)}, u32[]{:S(2)}, u32[]{:S(2)}) collective-permute-start(bf16[10,1,512]{2,1,0:T(2,128)(2,1)S(1)} %get-tuple-element.24), channel_id=1, source_target_pairs={{0,1},{1,2},{2,3},{3,4},{4,5},{5,6},{6,7},{7,8},{8,9},{9,10},{10,1... | collective-permute-start | bytes 30728 | tf_op jit(solution)/shard_map/ppermute | solution.py:18
  72.9 1.9 %collective-permute-start.7 = (bf16[10,1,512]{2,1,0:T(2,128)(2,1)S(1)}, bf16[10,1,512]{2,1,0:T(2,128)(2,1)S(1)}, u32[]{:S(2)}, u32[]{:S(2)}) collective-permute-start(bf16[10,1,512]{2,1,0:T(2,128)(2,1)S(1)} %get-tuple-element.23), channel_id=1, source_target_pairs={{1,0},{2,1},{3,2},{4,3},{5,4},{6,5},{7,6},{8,7},{9,8},{10,9},{11,1... | collective-permute-start | bytes 30728 | tf_op jit(solution)/shard_map/ppermute | solution.py:21
  74.8 1.4 reverse_bitcast_fusion
  76.2 3.0 %copy.29 = bf16[3,3,512,192]{2,1,0,3:T(4,128)(2,1)S(1)} copy(bf16[3,3,512,192]{2,3,1,0:T(8,128)(2,1)} %reverse_bitcast_fusion) | data formatting | bytes 3538944 | tf_op jit(solution)/shard_map/transpose | solution.py:103
  79.2 3.8 %reshape.67 = bf16[4608,192]{0,1:T(8,128)(2,1)} reshape(bf16[3,3,512,192]{2,1,0,3:T(4,128)(2,1)S(1)} %copy.29) | data formatting | bytes 3538944 | tf_op jit(solution)/shard_map/reshape | solution.py:103
  83.0 0.4 pad_maximum_fusion.2
  83.4 1.3 reduce_sum.31
  84.7 0.7 reshape.70
  85.4 16.5 %all-to-all-start.1 = ((bf16[16,14,128]{2,1,0:T(8,128)(2,1)}), bf16[16,14,128]{2,1,0:T(8,128)(2,1)S(1)}, u32[]{:S(2)}, u32[]{:S(2)}) async-start(bf16[16,14,128]{2,1,0:T(8,128)(2,1)} %reshape.70), calls=%async_computation.1 | async-start | bytes 131072 | tf_op jit(solution)/shard_map/all_to_all | solution.py:52
  101.9 0.9 slice_dynamic-update-slice_fusion.5
  102.8 0.9 fusion.3
  103.7 10.3 %all-to-all-done.1 = bf16[16,14,128]{2,1,0:T(8,128)(2,1)S(1)} async-done(((bf16[16,14,128]{2,1,0:T(8,128)(2,1)}), bf16[16,14,128]{2,1,0:T(8,128)(2,1)S(1)}, u32[]{:S(2)}, u32[]{:S(2)}) %all-to-all-start.1) | async-done | bytes 57376 | tf_op jit(solution)/shard_map/all_to_all | solution.py:52
  114.0 0.6 broadcast_in_dim.23
  114.7 3.5 %all-to-all-start.2 = ((bf16[16,14,128]{2,1,0:T(8,128)(2,1)}), bf16[16,14,128]{2,1,0:T(8,128)(2,1)S(1)}, u32[]{:S(2)}, u32[]{:S(2)}) async-start(bf16[16,14,128]{2,1,0:T(8,128)(2,1)} %broadcast_in_dim.23), calls=%async_computation.2 | async-start | bytes 131072 | tf_op jit(solution)/shard_map/all_to_all | solution.py:33
  118.2 1.0 slice_dynamic-update-slice_fusion.4
  119.2 10.8 %all-to-all-done.2 = bf16[16,14,128]{2,1,0:T(8,128)(2,1)S(1)} async-done(((bf16[16,14,128]{2,1,0:T(8,128)(2,1)}), bf16[16,14,128]{2,1,0:T(8,128)(2,1)S(1)}, u32[]{:S(2)}, u32[]{:S(2)}) %all-to-all-start.2) | async-done | bytes 57376 | tf_op jit(solution)/shard_map/all_to_all | solution.py:33
  130.0 1.1 broadcast_in_dim.25
  131.1 5.1 %all-to-all-start.3 = ((bf16[16,224,128]{2,1,0:T(8,128)(2,1)}), bf16[16,224,128]{2,1,0:T(8,128)(2,1)S(1)}, u32[]{:S(2)}, u32[]{:S(2)}) async-start(bf16[16,224,128]{2,1,0:T(8,128)(2,1)} %broadcast_in_dim.25), calls=%async_computation.3 | async-start | bytes 1835008 | tf_op jit(solution)/shard_map/all_to_all | solution.py:33
  136.2 0.9 slice_dynamic-update-slice_fusion.3
  137.1 0.7 constant_dynamic-update-slice_fusion.3
  137.7 0.7 constant_dynamic-update-slice_fusion.2
  138.4 0.7 constant_dynamic-update-slice_fusion.1
  139.1 0.7 constant_dynamic-update-slice_fusion
  139.8 0.9 slice_dynamic-update-slice_fusion.2
  140.7 8.5 %all-to-all-done.3 = bf16[16,224,128]{2,1,0:T(8,128)(2,1)S(1)} async-done(((bf16[16,224,128]{2,1,0:T(8,128)(2,1)}), bf16[16,224,128]{2,1,0:T(8,128)(2,1)S(1)}, u32[]{:S(2)}, u32[]{:S(2)}) %all-to-all-start.3) | async-done | bytes 917536 | tf_op jit(solution)/shard_map/all_to_all | solution.py:33
  149.2 6.2 %collective-permute-start.9 = (bf16[16,224,128]{2,1,0:T(8,128)(2,1)S(1)}, bf16[16,224,128]{2,1,0:T(8,128)(2,1)}, u32[]{:S(2)}, u32[]{:S(2)}) collective-permute-start(bf16[16,224,128]{2,1,0:T(8,128)(2,1)S(1)} %all-to-all-done.3), channel_id=1, source_target_pairs={{0,1},{1,0},{2,3},{3,2},{4,5},{5,4},{6,7},{7,6},{8,9},{9,8},{10,11... | collective-permute-start | bytes 2752520 | tf_op jit(solution)/shard_map/ppermute | solution.py:56
  155.4 0.9 slice_dynamic-update-slice_fusion.1
  156.3 0.9 fusion.2
  157.2 0.9 slice_dynamic-update-slice_fusion
  158.1 4.0 %convolution_convert_fusion = bf16[512,192]{0,1:T(8,128)(2,1)S(1)} fusion(bf16[512,4608]{1,0:T(8,128)(2,1)} %bitcast.3, bf16[4608,192]{0,1:T(8,128)(2,1)S(1)} %copy-done.5), kind=kOutput, calls=%fused_computation.9 | convolution fusion | flops 906067968 | bytes 6684672 | tf_op jit(solution)/shard_map/dot_general | solution.py:105
  162.3 0.7 slice.160
  162.9 0.8 slice.161
  163.7 1.3 select_bitcast_fusion.1
  165.0 0.2 pad_maximum_fusion.1
  165.3 0.6 slice_convert_fusion
  165.9 1.4 copy.37
  167.3 2.1 %reshape_reshape.3 = bf16[3,3,192,512]{3,2,1,0:T(8,128)(2,1)} reshape(bf16[8,216,4,128]{3,2,1,0:T(4,128)(2,1)S(1)} %copy.37) | data formatting | bytes 3538944 | tf_op jit(solution)/shard_map/reshape;reshape | solution.py:115
  (42 shorter events, 1.3 us)
Async XLA Ops:
  1.5 6.8 %collective-permute-start = (bf16[1,64,192]{2,1,0:T(8,128)(2,1)S(1)}, bf16[1,64,192]{2,1,0:T(8,128)(2,1)S(1)}, u32[]{:S(2)}, u32[]{:S(2)}) collective-permute-start(bf16[1,64,192]{2,1,0:T(8,128)(2,1)S(1)} %get-tuple-element.39), channel_id=1, source_target_pairs={{0,16},{16,32},{32,48},{48,64},{64,80},{80,96},{96,112},{112,128},... | collective-permute-start | bytes 73736 | tf_op jit(solution)/shard_map/ppermute | solution.py:18
  7.0 6.2 %collective-permute-start.1 = (bf16[1,64,192]{2,1,0:T(8,128)(2,1)S(1)}, bf16[1,64,192]{2,1,0:T(8,128)(2,1)S(1)}, u32[]{:S(2)}, u32[]{:S(2)}) collective-permute-start(bf16[1,64,192]{2,1,0:T(8,128)(2,1)S(1)} %get-tuple-element.40), channel_id=1, source_target_pairs={{16,0},{32,16},{48,32},{64,48},{80,64},{96,80},{112,96},{128,112},... | collective-permute-start | bytes 73736 | tf_op jit(solution)/shard_map/ppermute | solution.py:21
  14.0 9.1 %collective-permute-start.2 = (bf16[10,1,192]{2,1,0:T(2,128)(2,1)S(1)}, bf16[10,1,192]{2,1,0:T(2,128)(2,1)S(1)}, u32[]{:S(2)}, u32[]{:S(2)}) collective-permute-start(bf16[10,1,192]{2,1,0:T(2,128)(2,1)S(1)} %get-tuple-element.36), channel_id=1, source_target_pairs={{0,1},{1,2},{2,3},{3,4},{4,5},{5,6},{6,7},{7,8},{8,9},{9,10},{10,1... | collective-permute-start | bytes 11528 | tf_op jit(solution)/shard_map/ppermute | solution.py:18
  18.2 5.0 %collective-permute-start.3 = (bf16[10,1,192]{2,1,0:T(2,128)(2,1)S(1)}, bf16[10,1,192]{2,1,0:T(2,128)(2,1)S(1)}, u32[]{:S(2)}, u32[]{:S(2)}) collective-permute-start(bf16[10,1,192]{2,1,0:T(2,128)(2,1)S(1)} %get-tuple-element.35), channel_id=1, source_target_pairs={{1,0},{2,1},{3,2},{4,3},{5,4},{6,5},{7,6},{8,7},{9,8},{10,9},{11,1... | collective-permute-start | bytes 11528 | tf_op jit(solution)/shard_map/ppermute | solution.py:21
  24.6 0.9 copy-start.2
  24.6 1.0 copy-start.3
  28.1 2.3 %copy-start.10 = (f32[512]{0:T(512)S(1)}, f32[512]{0:T(512)}, u32[]{:S(2)}) copy-start(f32[512]{0:T(512)} %param.11) | copy-start | bytes 6148
  30.4 2.7 %copy-start.6 = (f32[8,64,128]{2,1,0:T(8,128)S(1)}, f32[8,64,128]{2,1,0:T(8,128)}, u32[]{:S(2)}) copy-start(f32[8,64,128]{2,1,0:T(8,128)} %param.9) | copy-start | bytes 786436
  30.4 2.7 %copy-start.8 = (bf16[8,64,128]{2,1,0:T(8,128)(2,1)S(1)}, bf16[8,64,128]{2,1,0:T(8,128)(2,1)}, u32[]{:S(2)}) copy-start(bf16[8,64,128]{2,1,0:T(8,128)(2,1)} %param.12) | copy-start | bytes 393220
  30.4 2.7 %copy-start.9 = (f32[8,64,128]{2,1,0:T(8,128)S(1)}, f32[8,64,128]{2,1,0:T(8,128)}, u32[]{:S(2)}) copy-start(f32[8,64,128]{2,1,0:T(8,128)} %param.13) | copy-start | bytes 786436
  34.1 1.5 copy-start.7
  34.1 1.7 copy-start.1
  37.7 1.8 %copy-start = (f32[4,8,224,128]{3,2,1,0:T(8,128)}, f32[4,8,224,128]{3,2,1,0:T(8,128)S(1)}, u32[]{:S(2)}) copy-start(f32[4,8,224,128]{3,2,1,0:T(8,128)S(1)} %copy.36) | copy-start | bytes 11010052
  39.6 4.4 %collective-permute-start.8 = (bf16[16,224,128]{2,1,0:T(8,128)(2,1)S(1)}, bf16[16,224,128]{2,1,0:T(8,128)(2,1)S(1)}, u32[]{:S(2)}, u32[]{:S(2)}) collective-permute-start(bf16[16,224,128]{2,1,0:T(8,128)(2,1)S(1)} %fusion.1), channel_id=1, source_target_pairs={{0,1},{1,0},{2,3},{3,2},{4,5},{5,4},{6,7},{7,6},{8,9},{9,8},{10,11... | collective-permute-start | bytes 2752520 | tf_op jit(solution)/shard_map/ppermute | solution.py:49
  46.6 28.3 %copy-start.4 = (bf16[3,3,192,512]{3,2,1,0:T(8,128)(2,1)S(1)}, bf16[3,3,192,512]{3,2,1,0:T(8,128)(2,1)}, u32[]{:S(2)}) copy-start(bf16[3,3,192,512]{3,2,1,0:T(8,128)(2,1)} %param.10) | copy-start | bytes 5308420
  46.6 36.8 %all-to-all-start = ((bf16[16,224,128]{2,1,0:T(8,128)(2,1)}), bf16[16,224,128]{2,1,0:T(8,128)(2,1)}, u32[]{:S(2)}, u32[]{:S(2)}) async-start(bf16[16,224,128]{2,1,0:T(8,128)(2,1)} %fusion), calls=%async_computation | async-start | bytes 1835008 | tf_op jit(solution)/shard_map/all_to_all | solution.py:50
  54.9 12.8 %collective-permute-start.4 = (bf16[1,64,512]{2,1,0:T(8,128)(2,1)S(1)}, bf16[1,64,512]{2,1,0:T(8,128)(2,1)S(1)}, u32[]{:S(2)}, u32[]{:S(2)}) collective-permute-start(bf16[1,64,512]{2,1,0:T(8,128)(2,1)S(1)} %get-tuple-element.25), channel_id=1, source_target_pairs={{0,16},{16,32},{32,48},{48,64},{64,80},{80,96},{96,112},{112,128},... | collective-permute-start | bytes 196616 | tf_op jit(solution)/shard_map/ppermute | solution.py:18
  59.6 9.6 %collective-permute-start.5 = (bf16[1,64,512]{2,1,0:T(8,128)(2,1)S(1)}, bf16[1,64,512]{2,1,0:T(8,128)(2,1)S(1)}, u32[]{:S(2)}, u32[]{:S(2)}) collective-permute-start(bf16[1,64,512]{2,1,0:T(8,128)(2,1)S(1)} %get-tuple-element.26), channel_id=1, source_target_pairs={{16,0},{32,16},{48,32},{64,48},{80,64},{96,80},{112,96},{128,112},... | collective-permute-start | bytes 196616 | tf_op jit(solution)/shard_map/ppermute | solution.py:21
  69.3 13.7 %collective-permute-start.6 = (bf16[10,1,512]{2,1,0:T(2,128)(2,1)S(1)}, bf16[10,1,512]{2,1,0:T(2,128)(2,1)S(1)}, u32[]{:S(2)}, u32[]{:S(2)}) collective-permute-start(bf16[10,1,512]{2,1,0:T(2,128)(2,1)S(1)} %get-tuple-element.24), channel_id=1, source_target_pairs={{0,1},{1,2},{2,3},{3,4},{4,5},{5,6},{6,7},{7,8},{8,9},{9,10},{10,1... | collective-permute-start | bytes 30728 | tf_op jit(solution)/shard_map/ppermute | solution.py:18
  72.9 10.1 %collective-permute-start.7 = (bf16[10,1,512]{2,1,0:T(2,128)(2,1)S(1)}, bf16[10,1,512]{2,1,0:T(2,128)(2,1)S(1)}, u32[]{:S(2)}, u32[]{:S(2)}) collective-permute-start(bf16[10,1,512]{2,1,0:T(2,128)(2,1)S(1)} %get-tuple-element.23), channel_id=1, source_target_pairs={{1,0},{2,1},{3,2},{4,3},{5,4},{6,5},{7,6},{8,7},{9,8},{10,9},{11,1... | collective-permute-start | bytes 30728 | tf_op jit(solution)/shard_map/ppermute | solution.py:21
  85.4 28.6 %all-to-all-start.1 = ((bf16[16,14,128]{2,1,0:T(8,128)(2,1)}), bf16[16,14,128]{2,1,0:T(8,128)(2,1)S(1)}, u32[]{:S(2)}, u32[]{:S(2)}) async-start(bf16[16,14,128]{2,1,0:T(8,128)(2,1)} %reshape.70), calls=%async_computation.1 | async-start | bytes 131072 | tf_op jit(solution)/shard_map/all_to_all | solution.py:52
  114.7 15.3 %all-to-all-start.2 = ((bf16[16,14,128]{2,1,0:T(8,128)(2,1)}), bf16[16,14,128]{2,1,0:T(8,128)(2,1)S(1)}, u32[]{:S(2)}, u32[]{:S(2)}) async-start(bf16[16,14,128]{2,1,0:T(8,128)(2,1)} %broadcast_in_dim.23), calls=%async_computation.2 | async-start | bytes 131072 | tf_op jit(solution)/shard_map/all_to_all | solution.py:33
  131.1 18.2 %all-to-all-start.3 = ((bf16[16,224,128]{2,1,0:T(8,128)(2,1)}), bf16[16,224,128]{2,1,0:T(8,128)(2,1)S(1)}, u32[]{:S(2)}, u32[]{:S(2)}) async-start(bf16[16,224,128]{2,1,0:T(8,128)(2,1)} %broadcast_in_dim.25), calls=%async_computation.3 | async-start | bytes 1835008 | tf_op jit(solution)/shard_map/all_to_all | solution.py:33
  149.2 8.9 %copy-start.5 = (bf16[4608,192]{0,1:T(8,128)(2,1)S(1)}, bf16[4608,192]{0,1:T(8,128)(2,1)}, u32[]{:S(2)}) copy-start(bf16[4608,192]{0,1:T(8,128)(2,1)} %reshape.67) | copy-start | bytes 5308420
  149.2 14.5 %collective-permute-start.9 = (bf16[16,224,128]{2,1,0:T(8,128)(2,1)S(1)}, bf16[16,224,128]{2,1,0:T(8,128)(2,1)}, u32[]{:S(2)}, u32[]{:S(2)}) collective-permute-start(bf16[16,224,128]{2,1,0:T(8,128)(2,1)S(1)} %all-to-all-done.3), channel_id=1, source_target_pairs={{0,1},{1,0},{2,3},{3,2},{4,5},{5,4},{6,7},{7,6},{8,9},{9,8},{10,11... | collective-permute-start | bytes 2752520 | tf_op jit(solution)/shard_map/ppermute | solution.py:56

commit v3 on v1

v3 whole, which is shorter than its diff:
```python
import jax
import jax.numpy as jnp
from jax import lax
from jax.experimental import pallas as pl
from jax.experimental.pallas import tpu as pltpu
from jax.sharding import Mesh, PartitionSpec as P

ROWS = ("z", "xh")
COLS = ("y", "xl", "core")
PLANE = ("xh", "y", "xl")
BF16 = jnp.bfloat16
F32 = jnp.float32
TR, TC = 8, 64
CELLS = TR * TC
FEAT, CH, ZCH, GATES = 64, 128, 192, 512
TAPS = 3 * ZCH
GROUPS, SLOT = 8, 224
VMEM = 40 * 1024 * 1024


def halo_rows(block):
    count = lax.axis_size(ROWS)
    forward = [(i, i + 1) for i in range(count - 1)]
    backward = [(target, source) for source, target in forward]
    low = lax.ppermute(block[TR - 1 :], ROWS, forward)
    high = lax.ppermute(block[:1], ROWS, backward)
    return low, high


def halo_cols(low, block, high):
    count = lax.axis_size(COLS)
    forward = [(i, i + 1) for i in range(count - 1)]
    backward = [(target, source) for source, target in forward]
    last = jnp.concatenate([low[:, TC - 1 :], block[:, TC - 1 :], high[:, TC - 1 :]], axis=0)
    first = jnp.concatenate([low[:, :1], block[:, :1], high[:, :1]], axis=0)
    return lax.ppermute(last, COLS, forward), lax.ppermute(first, COLS, backward)


def shifted(row, before, after):
    place = lax.broadcasted_iota(jnp.int32, row.shape, 0)
    down = jnp.where(place == 0, before, pltpu.roll(row, 1, 0))
    up = jnp.where(place == TC - 1, after, pltpu.roll(row, TC - 1, 0))
    return down, up


def taps_kernel(stacked, taps):
    for r in range(TR):
        row = stacked[r].astype(F32)
        down, up = shifted(row, 0.0, 0.0)
        taps[(r + 1) * TC : (r + 2) * TC, :] = jnp.concatenate([down, row, up], axis=1).astype(BF16)


def half_products(taps, half_gates, half_bias, store):
    for a in range(3):
        term = lax.dot_general(
            taps[a * TC : a * TC + CELLS, :],
            half_gates,
            (((0,), (0,)), ((), ())),
            preferred_element_type=F32,
        )
        begin = a * TAPS
        while begin < (a + 1) * TAPS:
            end = min((begin // SLOT + 1) * SLOT, (a + 1) * TAPS)
            group, top = begin // SLOT, begin % SLOT
            for j in range(2):
                block = term[begin - a * TAPS : end - a * TAPS, j * 128 : (j + 1) * 128]
                store(j * GROUPS + group, top, top + end - begin, block)
            begin = end
    top = 3 * TAPS - (GROUPS - 1) * SLOT
    for j in range(2):
        slot = j * GROUPS + GROUPS - 1
        row = half_bias[:, j * 128 : (j + 1) * 128]
        store(slot, top, top + 16, jnp.concatenate([row, row], axis=0))
        store(slot, top + 16, SLOT, jnp.zeros((SLOT - top - 16, 128), F32))


def cell_kernel(
    own_taps, low, high, left, right, kernel, cell_prev, hidden_cot, cell_cot, bias,
    hidden_new, cell_new, grad_cell, grad_gates, taps, sums, send, gates,
):
    for r, halo in ((0, low), (TR + 1, high)):
        row = halo[0].astype(F32)
        down, up = shifted(row, left[r].astype(F32), right[r].astype(F32))
        taps[r * TC : (r + 1) * TC, :] = jnp.concatenate([down, row, up], axis=1).astype(BF16)
    place = lax.broadcasted_iota(jnp.int32, (16, ZCH), 0)
    for r in range(1, TR + 1):
        begin, end = r * TC, (r + 1) * TC
        taps[begin + 16 : end - 16, :] = own_taps[begin + 16 : end - 16, :]
        block = own_taps[begin : begin + 16, :].astype(F32)
        side = jnp.where(place == 0, left[r].astype(F32), block[:, :ZCH])
        taps[begin : begin + 16, :] = jnp.concatenate([side, block[:, ZCH:]], axis=1).astype(BF16)
        block = own_taps[end - 16 : end, :].astype(F32)
        side = jnp.where(place == 15, right[r].astype(F32), block[:, 2 * ZCH :])
        taps[end - 16 : end, :] = jnp.concatenate([block[:, : 2 * ZCH], side], axis=1).astype(BF16)
    total = jnp.dot(taps[0:CELLS, :], kernel[0], preferred_element_type=F32)
    total += jnp.dot(taps[TC : TC + CELLS, :], kernel[1], preferred_element_type=F32)
    total += jnp.dot(taps[2 * TC : 2 * TC + CELLS, :], kernel[2], preferred_element_type=F32)
    gates[...] = total + bias[...]
    bias_sum = jnp.zeros((8, GATES), F32)
    for r in range(TR):
        rows = slice(r * TC, (r + 1) * TC)
        in_gate = jax.nn.sigmoid(gates[rows, 0:CH])
        forget = jax.nn.sigmoid(gates[rows, CH : 2 * CH])
        out_gate = jax.nn.sigmoid(gates[rows, 2 * CH : 3 * CH])
        cand = jnp.tanh(gates[rows, 3 * CH :])
        before = cell_prev[r]
        new = forget * before + in_gate * cand
        squash = jnp.tanh(new)
        cell_new[r] = new
        hidden_new[r] = (out_gate * squash).astype(BF16)
        hid_cot = hidden_cot[r].astype(F32)
        total = cell_cot[r] + hid_cot * out_gate * (1.0 - squash * squash)
        grad_cell[r] = total * forget
        parts = [
            total * cand * in_gate * (1.0 - in_gate),
            total * before * forget * (1.0 - forget),
            hid_cot * squash * out_gate * (1.0 - out_gate),
            total * in_gate * (1.0 - cand * cand),
        ]
        rounded = jnp.concatenate([part.astype(BF16) for part in parts], axis=1)
        grad_gates[rows, :] = rounded
        wide = rounded.astype(F32).reshape(TC // 8, 8, GATES)
        bias_sum = bias_sum + jnp.sum(wide, axis=0)
    sums[...] = jnp.broadcast_to(jnp.sum(bias_sum, axis=0, keepdims=True), (8, GATES))
    columns = pl.ds(pl.multiple_of((1 - lax.axis_index("core")) * 256, 256), 256)

    def store(slot, top, end, block):
        send[slot, top:end, :] = block.astype(BF16)

    half_products(taps, grad_gates[:, columns], sums[:, columns], store)


def own_kernel(taps, grad_gates, sums, received, total):
    columns = pl.ds(pl.multiple_of(lax.axis_index("core") * 256, 256), 256)

    def store(slot, top, end, block):
        total[slot, top:end, :] = (block + received[slot, top:end, :].astype(F32)).astype(BF16)

    half_products(taps, grad_gates[:, columns], sums[:, columns], store)


def input_kernel(
    grad_gates, low, high, left, right, kernel, grad_features, grad_hidden, moved, result
):
    for r in range(TR + 2):
        if r == 0:
            row = low[0]
        elif r == TR + 1:
            row = high[0]
        else:
            row = grad_gates[(r - 1) * TC : r * TC, :]
        rows = slice(r * TC, (r + 1) * TC)
        down, up = shifted(row.astype(F32), left[r].astype(F32), right[r].astype(F32))
        moved[0, rows, :] = down.astype(BF16)
        moved[1, rows, :] = row
        moved[2, rows, :] = up.astype(BF16)
    for tap in range(9):
        a, b = tap // 3, tap % 3
        term = lax.dot_general(
            moved[2 - b, (2 - a) * TC : (2 - a) * TC + CELLS, :],
            kernel[a, b * ZCH : (b + 1) * ZCH, :],
            (((1,), (1,)), ((), ())),
            preferred_element_type=F32,
        )
        if tap == 0:
            result[...] = term
        else:
            result[...] += term
    for r in range(TR):
        block = result[r * TC : (r + 1) * TC, :]
        grad_features[r] = block[:, :FEAT].astype(BF16)
        grad_hidden[r] = block[:, FEAT:].astype(BF16)


def join_kernel(own, other, grad_kernel, grad_bias):
    core = lax.axis_index("core")
    last = 3 * TAPS - (GROUPS - 1) * SLOT
    for source, place in ((own, core), (other, 1 - core)):
        for j in range(2):
            columns = pl.ds(pl.multiple_of(place * 256 + j * 128, 128), 128)
            for i in range(GROUPS):
                count = SLOT if i < GROUPS - 1 else last
                grad_kernel[i * SLOT : i * SLOT + count, columns] = source[
                    j * GROUPS + i, 0:count, :
                ]
            row = source[j * GROUPS + GROUPS - 1, last : last + 16, :].astype(F32)
            grad_bias[:, columns] = row[0:1]


def call(body, outs, *args, scratch=(), flops=0):
    moved = sum(x.size * x.dtype.itemsize for x in list(args) + list(outs))
    whole = pl.BlockSpec(memory_space=pltpu.VMEM)
    return pl.pallas_call(
        body,
        out_shape=outs,
        in_specs=[whole] * len(args),
        out_specs=[whole] * len(outs),
        scratch_shapes=list(scratch),
        cost_estimate=pl.CostEstimate(flops=flops, bytes_accessed=moved, transcendentals=0),
        compiler_params=pltpu.CompilerParams(vmem_limit_bytes=VMEM),
    )(*args)


def copies_of(part, count):
    return lax.optimization_barrier(jnp.broadcast_to(part[None], (count,) + part.shape))


def local(features, hidden_prev, cell_prev, kernel, bias, hidden_cot, cell_cot):
    shape = jax.ShapeDtypeStruct
    work = 2 * CELLS * 3 * TAPS * GATES
    plane = lax.axis_size(PLANE)
    depth = lax.axis_size("z")
    swap = [(0, 1), (1, 0)]
    weights = kernel.reshape(3, TAPS, GATES)

    stacked = jnp.concatenate([features, hidden_prev], axis=2)
    low, high = halo_rows(stacked)
    (own_taps,) = call(
        taps_kernel, (shape(((TR + 2) * TC, TAPS), BF16),), stacked, flops=work
    )
    low, high, own_taps = lax.optimization_barrier((low, high, own_taps))
    left, right = halo_cols(low, stacked, high)
    hidden_new, cell_new, grad_cell, grad_gates, taps, sums, send = call(
        cell_kernel,
        (
            shape((TR, TC, CH), BF16),
            shape((TR, TC, CH), F32),
            shape((TR, TC, CH), F32),
            shape((CELLS, GATES), BF16),
            shape(((TR + 2) * TC, TAPS), BF16),
            shape((8, GATES), F32),
            shape((plane, SLOT, 128), BF16),
        ),
        own_taps, low, high, left, right, weights, cell_prev, hidden_cot, cell_cot,
        bias.reshape(1, GATES),
        scratch=[pltpu.VMEM((CELLS, GATES), F32)],
        flops=work + work // 2,
    )
    received = lax.ppermute(send, "core", swap)
    gate_tile = grad_gates.reshape(TR, TC, GATES)
    gate_low, gate_high = halo_rows(gate_tile)
    (half,) = call(
        own_kernel, (shape((plane, SLOT, 128), BF16),), taps, grad_gates, sums, received,
        flops=work // 2,
    )
    half, gate_low, gate_high = lax.optimization_barrier((half, gate_low, gate_high))
    part = lax.all_to_all(half, PLANE, 0, 0, tiled=True)
    part = jnp.sum(part.astype(F32), axis=0).astype(BF16)
    part = lax.all_to_all(part.reshape(depth, SLOT // depth, 128), "z", 0, 0, tiled=True)
    scale = 1.0 / (TR * lax.axis_size(ROWS))
    part = (jnp.sum(part.astype(F32), axis=0) * scale).astype(BF16)
    part = lax.all_to_all(copies_of(part, depth), "z", 0, 0, tiled=True).reshape(SLOT, 128)
    copies, gate_low, gate_tile, gate_high = lax.optimization_barrier(
        (copies_of(part, plane), gate_low, gate_tile, gate_high)
    )
    half = lax.all_to_all(copies, PLANE, 0, 0, tiled=True)
    gate_left, gate_right = halo_cols(gate_low, gate_tile, gate_high)
    grad_features, grad_hidden = call(
        input_kernel,
        (shape((TR, TC, FEAT), BF16), shape((TR, TC, CH), BF16)),
        grad_gates, gate_low, gate_high, gate_left, gate_right, weights,
        scratch=[pltpu.VMEM((3, (TR + 2) * TC, GATES), BF16), pltpu.VMEM((CELLS, ZCH), F32)],
        flops=work,
    )
    half, grad_features, grad_hidden = lax.optimization_barrier(
        (half, grad_features, grad_hidden)
    )
    other = lax.ppermute(half, "core", swap)
    grad_kernel, grad_bias = call(
        join_kernel, (shape((3 * TAPS, GATES), BF16), shape((1, GATES), F32)), half, other
    )
    return (
        hidden_new,
        cell_new,
        grad_features,
        grad_hidden,
        grad_cell,
        grad_kernel.reshape(3, 3, ZCH, GATES),
        grad_bias.reshape(GATES),
    )


def solution(mesh):
    grid = Mesh(mesh.devices.reshape(16, 2, 4, 2, 2), ROWS + COLS)
    tile = P(ROWS, COLS, None)
    return jax.shard_map(
        local,
        mesh=grid,
        in_specs=(tile, tile, tile, P(), P(), tile, tile),
        out_specs=(tile, tile, tile, tile, tile, P(), P()),
        check_vma=False,
    )
```

time: 181 us -> 130 us (0.72)
  blocking collectives: 23 us -> 65 us
  local copies, waits for them, and re-layouts: 31.3 us -> 1.2 us
  waiting for transfers between devices: 36.3 us -> 7.04 us
  between operations: 14.4 us -> 0.96 us
  starting transfers between devices: 54.4 us -> 44.4 us
  other arithmetic: 13 us -> 3.11 us
  matrix products: 7.8 us -> 0 us
  Pallas kernels: 0 us -> 7.57 us
    all_to_all x1 -> x3, blocking collectives: 23 us -> 65 us  [the longest x1 27.9 us: local(): lax.all_to_all(part.reshape(depth, SLOT // depth, 128), 'z', 0, 0, tiled=...]
    all_to_all x3 -> x1, starting transfers between devices: 27.9 us -> 3.63 us  [local(): half = lax.all_to_all(copies, PLANE, 0, 0, tiled=True)]
    all_to_all x3 -> x1, waiting for transfers between devices: 17.7 us -> 0.01 us  [local(): half = lax.all_to_all(copies, PLANE, 0, 0, tiled=True)]
    ppermute x9 -> x10, starting transfers between devices: 26.2 us -> 40.8 us  [the longest x2 13.9 us: halo_cols(): lax.ppermute(last, COLS, forward)]
    all_gather x1 -> x0, waiting for transfers between devices: 11.2 us -> none  [total_of(): lax.all_gather(half, 'core', axis=0).reshape(4, groups, SLOT_ROWS, 128)]
    unnamed x31 -> x10, local copies, waits for them, and re-layouts: 9.3 us -> 0.03 us
    dot_general x3 -> x0, matrix products: 7.8 us -> none  [the longest x1 4.01 us: local(): jnp.dot(grad_source, flipped, preferred_element_type=jnp.float32)]
    pallas_call x0 -> x5, Pallas kernels: none -> 7.57 us  [call(): pl.pallas_call(body, out_shape=outs, in_specs=[whole] * len(args), out_sp...]
  transfers between devices with their start and end apart: 13 -> 11, of which waited for: 6 -> 4; matrix products, arithmetic and copies ran while one was open for 14% -> 2% of each run, Pallas kernels for 0% -> 3%
where the time goes in v3:
time: 130 us; the launch traced here: 129 us
  blocking collectives  65 us (50%)
  starting transfers between devices  44.4 us (34%)
  Pallas kernels  7.57 us (6%)
  waiting for transfers between devices  7.04 us (5%)
  other arithmetic  3.11 us (2%)
    all_to_all x1, blocking collectives, local(): lax.all_to_all(part.reshape(depth, SLOT // depth, 128), 'z', 0, 0, tiled=...  27.9 us
    all_to_all x1, blocking collectives, local(): part = lax.all_to_all(half, PLANE, 0, 0, tiled=True)  22.6 us
    all_to_all x1, blocking collectives, local(): lax.all_to_all(copies_of(part, depth), 'z', 0, 0, tiled=True)  14.4 us
    ppermute x2, starting transfers between devices, halo_cols(): lax.ppermute(last, COLS, forward)  13.9 us
    ppermute x2, starting transfers between devices, halo_rows(): low = lax.ppermute(block[TR - 1:], ROWS, forward)  11.6 us
    pallas_call x5, Pallas kernels, call(): pl.pallas_call(body, out_shape=outs, in_specs=[whole] * len(args), out_sp...  7.57 us
    ppermute x2, starting transfers between devices, halo_cols(): lax.ppermute(first, COLS, backward)  7.49 us
    ppermute x2, waiting for transfers between devices, halo_cols(): lax.ppermute(first, COLS, backward)  4.4 us
  transfers between devices with their start and end apart: 11, of which 4 were waited for; matrix products, arithmetic and copies ran while one was open for 2% of the time, Pallas kernels for 3%

profile of v3, /device:TPU:1, one launch (start us, length us, event | category | flops | bytes accessed | tf_op | source)
XLA Modules:
  0.0 129.2 jit_solution(7560508340552527221)
XLA Ops:
  0.6 0.9 fusion.1
  1.5 1.3 collective-permute-start.1
  2.8 6.1 %collective-permute-start = (bf16[1,64,192]{2,1,0:T(8,128)(2,1)S(1)}, bf16[1,64,192]{2,1,0:T(8,128)(2,1)S(1)}, u32[]{:S(2)}, u32[]{:S(2)}) collective-permute-start(bf16[1,64,192]{2,1,0:T(8,128)(2,1)S(1)} %get-tuple-element.62), channel_id=1, source_target_pairs={{0,16},{16,32},{32,48},{48,64},{64,80},{80,96},{96,112},{112,128},... | collective-permute-start | bytes 73736 | tf_op jit(solution)/shard_map/ppermute | solution.py:25
  8.9 0.9 fusion.3
  9.8 1.1 pad_maximum_fusion.stacked
  10.9 0.0 copy-start
  10.9 0.0 copy-start.1
  10.9 0.0 copy-start.2
  10.9 0.0 copy-start.3
  10.9 0.0 copy-start.4
  11.0 0.2 shard_map.126.own_taps
  11.1 0.0 collective-permute-done.1.high
  11.1 0.0 collective-permute-done.low
  11.2 4.6 %collective-permute-start.2 = (bf16[10,1,192]{2,1,0:T(2,128)(2,1)S(1)}, bf16[10,1,192]{2,1,0:T(2,128)(2,1)S(1)}, u32[]{:S(2)}, u32[]{:S(2)}) collective-permute-start(bf16[10,1,192]{2,1,0:T(2,128)(2,1)S(1)} %pad_maximum_fusion.3), channel_id=1, source_target_pairs={{0,1},{1,2},{2,3},{3,4},{4,5},{5,6},{6,7},{7,8},{8,9},{9,10},{10,1... | collective-permute-start | bytes 11528 | tf_op jit(solution)/shard_map/ppermute | solution.py:36
  15.8 5.6 %collective-permute-start.3 = (bf16[10,1,192]{2,1,0:T(2,128)(2,1)S(1)}, bf16[10,1,192]{2,1,0:T(2,128)(2,1)S(1)}, u32[]{:S(2)}, u32[]{:S(2)}) collective-permute-start(bf16[10,1,192]{2,1,0:T(2,128)(2,1)S(1)} %pad_maximum_fusion.4), channel_id=1, source_target_pairs={{1,0},{2,1},{3,2},{4,3},{5,4},{6,5},{7,6},{8,7},{9,8},{10,9},{11,1... | collective-permute-start | bytes 11528 | tf_op jit(solution)/shard_map/ppermute | solution.py:36
  21.4 0.0 collective-permute-done.2.left
  21.4 0.8 collective-permute-done.3.right
  22.2 0.0 copy-done
  22.2 0.0 copy-done.1
  22.2 0.0 copy-done.2
  22.2 0.0 copy-done.3
  22.2 0.0 copy-done.4
  22.2 2.6 %shard_map.127 = (bf16[8,64,128]{2,1,0:T(8,128)(2,1)}, f32[8,64,128]{2,1,0:T(8,128)}, f32[8,64,128]{2,1,0:T(8,128)}, bf16[512,512]{1,0:T(8,128)(2,1)S(1)}, bf16[...) custom-call(bf16[640,576]{1,0:T(8,128)(2,1)S(1)} %shard_map.126.own_taps, ...), custom_call_target="tpu_custom_call" | custom-call | flops 1358954496 | bytes 6071808 | tf_op jit(solution)/shard_map/pallas_call | solution.py:193
  24.8 2.3 %collective-permute-start.4 = (bf16[16,224,128]{2,1,0:T(8,128)(2,1)S(1)}, bf16[16,224,128]{2,1,0:T(8,128)(2,1)S(1)}, u32[]{:S(2)}, u32[]{:S(2)}) collective-permute-start(bf16[16,224,128]{2,1,0:T(8,128)(2,1)S(1)} %get-tuple-element.39), channel_id=1, source_target_pairs={{0,1},{1,0},{2,3},{3,2},{4,5},{5,4},{6,7},{7,6},{8,9},{9,8},{10,11... | collective-permute-start | bytes 2752520 | tf_op jit(solution)/shard_map/ppermute | solution.py:239
  27.1 1.3 collective-permute-start.6
  28.4 5.5 %collective-permute-start.5 = (bf16[1,64,512]{2,1,0:T(8,128)(2,1)S(1)}, bf16[1,64,512]{2,1,0:T(8,128)(2,1)S(1)}, u32[]{:S(2)}, u32[]{:S(2)}) collective-permute-start(bf16[1,64,512]{2,1,0:T(8,128)(2,1)S(1)} %get-tuple-element.58), channel_id=1, source_target_pairs={{0,16},{16,32},{32,48},{48,64},{64,80},{80,96},{96,112},{112,128},... | collective-permute-start | bytes 196616 | tf_op jit(solution)/shard_map/ppermute | solution.py:25
  33.9 0.0 collective-permute-done.4.received
  33.9 0.8 shard_map.128
  34.7 0.0 collective-permute-done.6.high
  34.7 0.5 collective-permute-done.5.low
  35.3 22.6 %all_to_all.20 = bf16[16,224,128]{2,1,0:T(8,128)(2,1)S(1)} all-to-all(bf16[16,224,128]{2,1,0:T(8,128)(2,1)S(1)} %shard_map.128), channel_id=1, replica_groups=mesh['z'=16,'xh'=2,'y'=4,'xl'=2,'core'=2] {'xh','y','xl'}, dimensions={0} | all-to-all | bytes 1835008 | tf_op jit(solution)/shard_map/all_to_all | solution.py:247
  57.9 0.1 reduce_sum.21
  58.0 27.9 %all_to_all.21 = bf16[16,14,128]{2,1,0:T(8,128)(2,1)S(1)} all-to-all(bf16[16,14,128]{2,1,0:T(8,128)(2,1)S(1)} %reshape.41), channel_id=1, replica_groups=mesh['z'=16,'xh'=2,'y'=4,'xl'=2,'core'=2] {'z'}, dimensions={0} | all-to-all | bytes 114688 | tf_op jit(solution)/shard_map/all_to_all | solution.py:249
  86.0 14.4 %all_to_all.22 = bf16[16,14,128]{2,1,0:T(8,128)(2,1)S(1)} all-to-all(bf16[16,14,128]{2,1,0:T(8,128)(2,1)S(1)} %broadcast_in_dim.6), channel_id=1, replica_groups=mesh['z'=16,'xh'=2,'y'=4,'xl'=2,'core'=2] {'z'}, dimensions={0} | all-to-all | bytes 114688 | tf_op jit(solution)/shard_map/all_to_all | solution.py:252
  100.4 1.0 broadcast_in_dim.15
  101.5 3.6 %all-to-all-start.3 = ((bf16[16,224,128]{2,1,0:T(8,128)(2,1)}), bf16[16,224,128]{2,1,0:T(8,128)(2,1)S(1)}, u32[]{:S(2)}, u32[]{:S(2)}) async-start(bf16[16,224,128]{2,1,0:T(8,128)(2,1)} %broadcast_in_dim.15), calls=%async_computation.3 | async-start | bytes 1835008 | tf_op jit(solution)/shard_map/all_to_all | solution.py:256
  105.2 9.3 %collective-permute-start.7 = (bf16[10,1,512]{2,1,0:T(2,128)(2,1)S(1)}, bf16[10,1,512]{2,1,0:T(2,128)(2,1)S(1)}, u32[]{:S(2)}, u32[]{:S(2)}) collective-permute-start(bf16[10,1,512]{2,1,0:T(2,128)(2,1)S(1)} %pad_maximum_fusion.1), channel_id=1, source_target_pairs={{0,1},{1,2},{2,3},{3,4},{4,5},{5,6},{6,7},{7,8},{8,9},{9,10},{10,1... | collective-permute-start | bytes 30728 | tf_op jit(solution)/shard_map/ppermute | solution.py:36
  114.6 1.9 %collective-permute-start.8 = (bf16[10,1,512]{2,1,0:T(2,128)(2,1)S(1)}, bf16[10,1,512]{2,1,0:T(2,128)(2,1)S(1)}, u32[]{:S(2)}, u32[]{:S(2)}) collective-permute-start(bf16[10,1,512]{2,1,0:T(2,128)(2,1)S(1)} %pad_maximum_fusion.2), channel_id=1, source_target_pairs={{1,0},{2,1},{3,2},{4,3},{5,4},{6,5},{7,6},{8,7},{9,8},{10,9},{11,1... | collective-permute-start | bytes 30728 | tf_op jit(solution)/shard_map/ppermute | solution.py:36
  116.5 0.0 collective-permute-done.7.left
  116.5 3.6 %collective-permute-done.8.right = bf16[10,1,512]{2,1,0:T(2,128)(2,1)S(1)} collective-permute-done((bf16[10,1,512]{2,1,0:T(2,128)(2,1)S(1)}, bf16[10,1,512]{2,1,0:T(2,128)(2,1)S(1)}, u32[]{:S(2)}, u32[]{:S(2)}) %collective-permute-start.8) | collective-permute-done | bytes 10272 | tf_op jit(solution)/shard_map/ppermute | solution.py:36
  120.1 2.4 %shard_map.129 = (bf16[8,64,64]{2,1,0:T(8,128)(2,1)}, bf16[8,64,128]{2,1,0:T(8,128)(2,1)}) custom-call(bf16[512,512]{1,0:T(8,128)(2,1)S(1)} %get-tuple-element.37.grad_gates, bf16[1,64,512]{2,1,0:T(8,128)(2,1)S(1)} %collective-permute-done.5.low, bf16[1,64,512]{2,1,0:T(8,128)(2,1)S(1)} %collective-permute-done.6.high, ...), custom_call_target="tpu_custom_call" | custom-call | flops 905969664 | bytes 2641920 | tf_op jit(solution)/shard_map/pallas_call | solution.py:193
  122.5 0.0 all-to-all-done.3.own
  122.5 2.9 %collective-permute-start.9 = (bf16[16,224,128]{2,1,0:T(8,128)(2,1)S(1)}, bf16[16,224,128]{2,1,0:T(8,128)(2,1)S(1)}, u32[]{:S(2)}, u32[]{:S(2)}) collective-permute-start(bf16[16,224,128]{2,1,0:T(8,128)(2,1)S(1)} %all-to-all-done.3.own), channel_id=1, source_target_pairs={{0,1},{1,0},{2,3},{3,2},{4,5},{5,4},{6,7},{7,6},{8,9},{9,8},{10,11... | collective-permute-start | bytes 2752520 | tf_op jit(solution)/shard_map/ppermute | solution.py:268
  125.5 2.1 %collective-permute-done.9.other = bf16[16,224,128]{2,1,0:T(8,128)(2,1)S(1)} collective-permute-done((bf16[16,224,128]{2,1,0:T(8,128)(2,1)S(1)}, bf16[16,224,128]{2,1,0:T(8,128)(2,1)S(1)}, u32[]{:S(2)}, u32[]{:S(2)}) %collective-permute-start.9) | collective-permute-done | bytes 917536 | tf_op jit(solution)/shard_map/ppermute | solution.py:268
  127.5 1.7 %shard_map.130 = (bf16[1728,512]{1,0:T(8,128)(2,1)}, f32[1,512]{1,0:T(1,128)}) custom-call(bf16[16,224,128]{2,1,0:T(8,128)(2,1)S(1)} %all-to-all-done.3.own, bf16[16,224,128]{2,1,0:T(8,128)(2,1)S(1)} %collective-permute-done.9.other), custom_call_target="tpu_custom_call" | custom-call | bytes 3606528 | tf_op jit(solution)/shard_map/pallas_call | solution.py:193
  (14 shorter events, 0.3 us)
Async XLA Ops:
  1.5 9.6 %collective-permute-start.1 = (bf16[1,64,192]{2,1,0:T(8,128)(2,1)S(1)}, bf16[1,64,192]{2,1,0:T(8,128)(2,1)S(1)}, u32[]{:S(2)}, u32[]{:S(2)}) collective-permute-start(bf16[1,64,192]{2,1,0:T(8,128)(2,1)S(1)} %get-tuple-element.61), channel_id=1, source_target_pairs={{16,0},{32,16},{48,32},{64,48},{80,64},{96,80},{112,96},{128,112},... | collective-permute-start | bytes 73736 | tf_op jit(solution)/shard_map/ppermute | solution.py:26
  2.8 8.4 %collective-permute-start = (bf16[1,64,192]{2,1,0:T(8,128)(2,1)S(1)}, bf16[1,64,192]{2,1,0:T(8,128)(2,1)S(1)}, u32[]{:S(2)}, u32[]{:S(2)}) collective-permute-start(bf16[1,64,192]{2,1,0:T(8,128)(2,1)S(1)} %get-tuple-element.62), channel_id=1, source_target_pairs={{0,16},{16,32},{32,48},{48,64},{64,80},{80,96},{96,112},{112,128},... | collective-permute-start | bytes 73736 | tf_op jit(solution)/shard_map/ppermute | solution.py:25
  10.9 11.3 %copy-start = (bf16[3,3,192,512]{3,2,1,0:T(8,128)(2,1)S(1)}, bf16[3,3,192,512]{3,2,1,0:T(8,128)(2,1)}, u32[]{:S(2)}) copy-start(bf16[3,3,192,512]{3,2,1,0:T(8,128)(2,1)} %param.10) | copy-start | bytes 5308420
  10.9 11.3 %copy-start.1 = (f32[8,64,128]{2,1,0:T(8,128)S(1)}, f32[8,64,128]{2,1,0:T(8,128)}, u32[]{:S(2)}) copy-start(f32[8,64,128]{2,1,0:T(8,128)} %cell_prev.1) | copy-start | bytes 786436
  10.9 11.3 %copy-start.2 = (f32[8,64,128]{2,1,0:T(8,128)S(1)}, f32[8,64,128]{2,1,0:T(8,128)}, u32[]{:S(2)}) copy-start(f32[8,64,128]{2,1,0:T(8,128)} %cell_cot.1) | copy-start | bytes 786436
  10.9 11.3 %copy-start.3 = (bf16[8,64,128]{2,1,0:T(8,128)(2,1)S(1)}, bf16[8,64,128]{2,1,0:T(8,128)(2,1)}, u32[]{:S(2)}) copy-start(bf16[8,64,128]{2,1,0:T(8,128)(2,1)} %hidden_cot.1) | copy-start | bytes 393220
  10.9 11.3 %copy-start.4 = (f32[512]{0:T(512)S(1)}, f32[512]{0:T(512)}, u32[]{:S(2)}) copy-start(f32[512]{0:T(512)} %param.11) | copy-start | bytes 6148
  11.2 10.2 %collective-permute-start.2 = (bf16[10,1,192]{2,1,0:T(2,128)(2,1)S(1)}, bf16[10,1,192]{2,1,0:T(2,128)(2,1)S(1)}, u32[]{:S(2)}, u32[]{:S(2)}) collective-permute-start(bf16[10,1,192]{2,1,0:T(2,128)(2,1)S(1)} %pad_maximum_fusion.3), channel_id=1, source_target_pairs={{0,1},{1,2},{2,3},{3,4},{4,5},{5,6},{6,7},{7,8},{8,9},{9,10},{10,1... | collective-permute-start | bytes 11528 | tf_op jit(solution)/shard_map/ppermute | solution.py:36
  15.8 6.4 %collective-permute-start.3 = (bf16[10,1,192]{2,1,0:T(2,128)(2,1)S(1)}, bf16[10,1,192]{2,1,0:T(2,128)(2,1)S(1)}, u32[]{:S(2)}, u32[]{:S(2)}) collective-permute-start(bf16[10,1,192]{2,1,0:T(2,128)(2,1)S(1)} %pad_maximum_fusion.4), channel_id=1, source_target_pairs={{1,0},{2,1},{3,2},{4,3},{5,4},{6,5},{7,6},{8,7},{9,8},{10,9},{11,1... | collective-permute-start | bytes 11528 | tf_op jit(solution)/shard_map/ppermute | solution.py:36
  24.8 9.1 %collective-permute-start.4 = (bf16[16,224,128]{2,1,0:T(8,128)(2,1)S(1)}, bf16[16,224,128]{2,1,0:T(8,128)(2,1)S(1)}, u32[]{:S(2)}, u32[]{:S(2)}) collective-permute-start(bf16[16,224,128]{2,1,0:T(8,128)(2,1)S(1)} %get-tuple-element.39), channel_id=1, source_target_pairs={{0,1},{1,0},{2,3},{3,2},{4,5},{5,4},{6,7},{7,6},{8,9},{9,8},{10,11... | collective-permute-start | bytes 2752520 | tf_op jit(solution)/shard_map/ppermute | solution.py:239
  27.1 7.6 %collective-permute-start.6 = (bf16[1,64,512]{2,1,0:T(8,128)(2,1)S(1)}, bf16[1,64,512]{2,1,0:T(8,128)(2,1)S(1)}, u32[]{:S(2)}, u32[]{:S(2)}) collective-permute-start(bf16[1,64,512]{2,1,0:T(8,128)(2,1)S(1)} %get-tuple-element.57), channel_id=1, source_target_pairs={{16,0},{32,16},{48,32},{64,48},{80,64},{96,80},{112,96},{128,112},... | collective-permute-start | bytes 196616 | tf_op jit(solution)/shard_map/ppermute | solution.py:26
  28.4 6.8 %collective-permute-start.5 = (bf16[1,64,512]{2,1,0:T(8,128)(2,1)S(1)}, bf16[1,64,512]{2,1,0:T(8,128)(2,1)S(1)}, u32[]{:S(2)}, u32[]{:S(2)}) collective-permute-start(bf16[1,64,512]{2,1,0:T(8,128)(2,1)S(1)} %get-tuple-element.58), channel_id=1, source_target_pairs={{0,16},{16,32},{32,48},{48,64},{64,80},{80,96},{96,112},{112,128},... | collective-permute-start | bytes 196616 | tf_op jit(solution)/shard_map/ppermute | solution.py:25
  101.5 21.0 %all-to-all-start.3 = ((bf16[16,224,128]{2,1,0:T(8,128)(2,1)}), bf16[16,224,128]{2,1,0:T(8,128)(2,1)S(1)}, u32[]{:S(2)}, u32[]{:S(2)}) async-start(bf16[16,224,128]{2,1,0:T(8,128)(2,1)} %broadcast_in_dim.15), calls=%async_computation.3 | async-start | bytes 1835008 | tf_op jit(solution)/shard_map/all_to_all | solution.py:256
  105.2 11.3 %collective-permute-start.7 = (bf16[10,1,512]{2,1,0:T(2,128)(2,1)S(1)}, bf16[10,1,512]{2,1,0:T(2,128)(2,1)S(1)}, u32[]{:S(2)}, u32[]{:S(2)}) collective-permute-start(bf16[10,1,512]{2,1,0:T(2,128)(2,1)S(1)} %pad_maximum_fusion.1), channel_id=1, source_target_pairs={{0,1},{1,2},{2,3},{3,4},{4,5},{5,6},{6,7},{7,8},{8,9},{9,10},{10,1... | collective-permute-start | bytes 30728 | tf_op jit(solution)/shard_map/ppermute | solution.py:36
  114.6 5.5 %collective-permute-start.8 = (bf16[10,1,512]{2,1,0:T(2,128)(2,1)S(1)}, bf16[10,1,512]{2,1,0:T(2,128)(2,1)S(1)}, u32[]{:S(2)}, u32[]{:S(2)}) collective-permute-start(bf16[10,1,512]{2,1,0:T(2,128)(2,1)S(1)} %pad_maximum_fusion.2), channel_id=1, source_target_pairs={{1,0},{2,1},{3,2},{4,3},{5,4},{6,5},{7,6},{8,7},{9,8},{10,9},{11,1... | collective-permute-start | bytes 30728 | tf_op jit(solution)/shard_map/ppermute | solution.py:36
  122.5 5.0 %collective-permute-start.9 = (bf16[16,224,128]{2,1,0:T(8,128)(2,1)S(1)}, bf16[16,224,128]{2,1,0:T(8,128)(2,1)S(1)}, u32[]{:S(2)}, u32[]{:S(2)}) collective-permute-start(bf16[16,224,128]{2,1,0:T(8,128)(2,1)S(1)} %all-to-all-done.3.own), channel_id=1, source_target_pairs={{0,1},{1,0},{2,3},{3,2},{4,5},{5,4},{6,7},{7,6},{8,9},{9,8},{10,11... | collective-permute-start | bytes 2752520 | tf_op jit(solution)/shard_map/ppermute | solution.py:268

commit v4 on v3

--- a/solution.py
+++ b/solution.py
@@ -50,7 +50,7 @@
         taps[(r + 1) * TC : (r + 2) * TC, :] = jnp.concatenate([down, row, up], axis=1).astype(BF16)
 
 
-def half_products(taps, half_gates, half_bias, store):
+def half_products(taps, half_gates, half_bias, store, finish=lambda slot: None):
     for a in range(3):
         term = lax.dot_general(
             taps[a * TC : a * TC + CELLS, :],
@@ -65,6 +65,8 @@
             for j in range(2):
                 block = term[begin - a * TAPS : end - a * TAPS, j * 128 : (j + 1) * 128]
                 store(j * GROUPS + group, top, top + end - begin, block)
+                if end % SLOT == 0:
+                    finish(j * GROUPS + group)
             begin = end
     top = 3 * TAPS - (GROUPS - 1) * SLOT
     for j in range(2):
@@ -72,6 +74,7 @@
         row = half_bias[:, j * 128 : (j + 1) * 128]
         store(slot, top, top + 16, jnp.concatenate([row, row], axis=0))
         store(slot, top + 16, SLOT, jnp.zeros((SLOT - top - 16, 128), F32))
+        finish(slot)
 
 
 def cell_kernel(
@@ -130,13 +133,20 @@
     half_products(taps, grad_gates[:, columns], sums[:, columns], store)
 
 
-def own_kernel(taps, grad_gates, sums, received, total):
+def own_kernel(taps, grad_gates, sums, received, result, total, sent):
     columns = pl.ds(pl.multiple_of(lax.axis_index("core") * 256, 256), 256)
 
     def store(slot, top, end, block):
         total[slot, top:end, :] = (block + received[slot, top:end, :].astype(F32)).astype(BF16)
 
-    half_products(taps, grad_gates[:, columns], sums[:, columns], store)
+    def copy(slot):
+        return pltpu.make_async_copy(total.at[slot], result.at[slot], sent.at[slot])
+
+    half_products(
+        taps, grad_gates[:, columns], sums[:, columns], store, lambda slot: copy(slot).start()
+    )
+    for slot in range(2 * GROUPS):
+        copy(slot).wait()
 
 
 def input_kernel(
@@ -172,29 +182,57 @@
         grad_hidden[r] = block[:, FEAT:].astype(BF16)
 
 
-def join_kernel(own, other, grad_kernel, grad_bias):
-    core = lax.axis_index("core")
+def place_half(slots, place, grad_kernel, grad_bias, last_slots, sems):
     last = 3 * TAPS - (GROUPS - 1) * SLOT
-    for source, place in ((own, core), (other, 1 - core)):
-        for j in range(2):
-            columns = pl.ds(pl.multiple_of(place * 256 + j * 128, 128), 128)
-            for i in range(GROUPS):
-                count = SLOT if i < GROUPS - 1 else last
-                grad_kernel[i * SLOT : i * SLOT + count, columns] = source[
-                    j * GROUPS + i, 0:count, :
-                ]
-            row = source[j * GROUPS + GROUPS - 1, last : last + 16, :].astype(F32)
-            grad_bias[:, columns] = row[0:1]
-
-
-def call(body, outs, *args, scratch=(), flops=0):
+    copies = []
+    for j in range(2):
+        columns = pl.ds(pl.multiple_of(place * 256 + j * 128, 128), 128)
+        slot = j * GROUPS + GROUPS - 1
+        copies.append(
+            pltpu.make_async_copy(
+                slots.at[slot, last : last + 16, :], last_slots.at[j], sems.at[2 * GROUPS + j]
+            )
+        )
+        for i in range(GROUPS):
+            count = SLOT if i < GROUPS - 1 else last
+            copies.append(
+                pltpu.make_async_copy(
+                    slots.at[j * GROUPS + i, 0:count, :],
+                    grad_kernel.at[i * SLOT : i * SLOT + count, columns],
+                    sems.at[j * GROUPS + i],
+                )
+            )
+    for copy in copies:
+        copy.start()
+    for copy in copies:
+        copy.wait()
+    for j in range(2):
+        columns = pl.ds(pl.multiple_of(place * 256 + j * 128, 128), 128)
+        grad_bias[:, columns] = last_slots[j].astype(F32)[0:1]
+
+
+def join_own_kernel(slots, grad_kernel, grad_bias, last_slots, sems):
+    grad_bias[...] = jnp.zeros_like(grad_bias)
+    place_half(slots, lax.axis_index("core"), grad_kernel, grad_bias, last_slots, sems)
+
+
+def join_other_kernel(
+    own_bias, slots, own_kernel_part, grad_kernel, grad_bias, last_slots, sems
+):
+    grad_bias[...] = own_bias[...]
+    place_half(slots, 1 - lax.axis_index("core"), grad_kernel, grad_bias, last_slots, sems)
+
+
+def call(body, outs, *args, scratch=(), flops=0, far=0, far_outs=0, aliases=()):
     moved = sum(x.size * x.dtype.itemsize for x in list(args) + list(outs))
     whole = pl.BlockSpec(memory_space=pltpu.VMEM)
+    anywhere = pl.BlockSpec(memory_space=pl.ANY)
     return pl.pallas_call(
         body,
         out_shape=outs,
-        in_specs=[whole] * len(args),
-        out_specs=[whole] * len(outs),
+        in_specs=[whole] * (len(args) - far) + [anywhere] * far,
+        out_specs=[anywhere] * far_outs + [whole] * (len(outs) - far_outs),
+        input_output_aliases=dict(aliases),
         scratch_shapes=list(scratch),
         cost_estimate=pl.CostEstimate(flops=flops, bytes_accessed=moved, transcendentals=0),
         compiler_params=pltpu.CompilerParams(vmem_limit_bytes=VMEM),
@@ -237,14 +275,16 @@
         flops=work + work // 2,
     )
     received = lax.ppermute(send, "core", swap)
-    gate_tile = grad_gates.reshape(TR, TC, GATES)
-    gate_low, gate_high = halo_rows(gate_tile)
     (half,) = call(
         own_kernel, (shape((plane, SLOT, 128), BF16),), taps, grad_gates, sums, received,
+        scratch=[pltpu.VMEM((plane, SLOT, 128), BF16), pltpu.SemaphoreType.DMA((plane,))],
         flops=work // 2,
-    )
-    half, gate_low, gate_high = lax.optimization_barrier((half, gate_low, gate_high))
+        far_outs=1,
+    )
+    half, gate_tile = lax.optimization_barrier((half, grad_gates.reshape(TR, TC, GATES)))
     part = lax.all_to_all(half, PLANE, 0, 0, tiled=True)
+    gate_low, gate_high = halo_rows(gate_tile)
+    part, gate_low, gate_high = lax.optimization_barrier((part, gate_low, gate_high))
     part = jnp.sum(part.astype(F32), axis=0).astype(BF16)
     part = lax.all_to_all(part.reshape(depth, SLOT // depth, 128), "z", 0, 0, tiled=True)
     scale = 1.0 / (TR * lax.axis_size(ROWS))
@@ -266,8 +306,14 @@
         (half, grad_features, grad_hidden)
     )
     other = lax.ppermute(half, "core", swap)
+    outs = (shape((3 * TAPS, GATES), BF16), shape((1, GATES), F32))
+    scratch = [pltpu.VMEM((2, 16, 128), BF16), pltpu.SemaphoreType.DMA((2 * GROUPS + 2,))]
+    grad_kernel, own_bias = call(
+        join_own_kernel, outs, half, scratch=scratch, far=1, far_outs=1
+    )
     grad_kernel, grad_bias = call(
-        join_kernel, (shape((3 * TAPS, GATES), BF16), shape((1, GATES), F32)), half, other
+        join_other_kernel, outs, own_bias, other, grad_kernel,
+        scratch=scratch, far=2, far_outs=1, aliases={2: 0},
     )
     return (
         hidden_new,

time: 130 us -> 126 us (0.969)
  blocking collectives: 65 us -> 43.8 us
  waiting for transfers between devices: 7.04 us -> 16.7 us
  starting transfers between devices: 44.4 us -> 50.2 us
  Pallas kernels: 7.57 us -> 9.37 us
    all_to_all x1 -> x0, blocking collectives: 22.6 us -> none  [local(): part = lax.all_to_all(half, PLANE, 0, 0, tiled=True)]
    ppermute x2, waiting for transfers between devices: 0.01 us -> 7.91 us  [halo_rows(): high = lax.ppermute(block[:1], ROWS, backward)]
    all_to_all x0 -> x1, starting transfers between devices: none -> 6.97 us  [local(): part = lax.all_to_all(half, PLANE, 0, 0, tiled=True)]
    ppermute x2, starting transfers between devices: 13.9 us -> 11.7 us  [halo_cols(): lax.ppermute(last, COLS, forward)]
    ppermute x1, waiting for transfers between devices: 0.01 us -> 2.09 us  [local(): received = lax.ppermute(send, 'core', swap)]
    pallas_call x5 -> x6, Pallas kernels: 7.57 us -> 9.37 us  [call(): pl.pallas_call(body, out_shape=outs, in_specs=[whole] * (len(args) - far)...]
    all_to_all x1, blocking collectives: 27.9 us -> 29.4 us  [local(): lax.all_to_all(part.reshape(depth, SLOT // depth, 128), 'z', 0, 0, tiled=...]
  transfers between devices with their start and end apart: 11 -> 12, of which waited for: 4 -> 6; matrix products, arithmetic and copies ran while one was open for 2% -> 2% of each run, Pallas kernels for 3% -> 3%
where the time goes in v4:
time: 126 us; the launch traced here: 125 us
  starting transfers between devices  50.2 us (40%)
  blocking collectives  43.8 us (35%)
  waiting for transfers between devices  16.7 us (13%)
  Pallas kernels  9.37 us (7%)
  other arithmetic  3.11 us (2%)
    all_to_all x1, blocking collectives, local(): lax.all_to_all(part.reshape(depth, SLOT // depth, 128), 'z', 0, 0, tiled=...  29.4 us
    all_to_all x1, blocking collectives, local(): lax.all_to_all(copies_of(part, depth), 'z', 0, 0, tiled=True)  14.4 us
    ppermute x2, starting transfers between devices, halo_cols(): lax.ppermute(last, COLS, forward)  11.7 us
    ppermute x2, starting transfers between devices, halo_rows(): low = lax.ppermute(block[TR - 1:], ROWS, forward)  11.6 us
    pallas_call x6, Pallas kernels, call(): pl.pallas_call(body, out_shape=outs, in_specs=[whole] * (len(args) - far)...  9.37 us
    ppermute x2, waiting for transfers between devices, halo_rows(): high = lax.ppermute(block[:1], ROWS, backward)  7.91 us
    ppermute x2, starting transfers between devices, halo_cols(): lax.ppermute(first, COLS, backward)  7.49 us
    all_to_all x1, starting transfers between devices, local(): part = lax.all_to_all(half, PLANE, 0, 0, tiled=True)  6.97 us
  transfers between devices with their start and end apart: 12, of which 6 were waited for; matrix products, arithmetic and copies ran while one was open for 2% of the time, Pallas kernels for 3%

profile of v4, /device:TPU:1, one launch (start us, length us, event | category | flops | bytes accessed | tf_op | source)
XLA Modules:
  0.0 125.3 jit_solution(13887691641036858811)
XLA Ops:
  0.6 0.9 fusion.1
  1.5 1.3 %collective-permute-start.1 = (bf16[1,64,192]{2,1,0:T(8,128)(2,1)S(1)}, bf16[1,64,192]{2,1,0:T(8,128)(2,1)S(1)}, u32[]{:S(2)}, u32[]{:S(2)}) collective-permute-start(bf16[1,64,192]{2,1,0:T(8,128)(2,1)S(1)} %get-tuple-element.69), channel_id=1, source_target_pairs={{16,0},{32,16},{48,32},{64,48},{80,64},{96,80},{112,96},{128,112},... | collective-permute-start | bytes 73736 | tf_op jit(solution)/shard_map/ppermute | solution.py:26
  2.8 6.1 %collective-permute-start = (bf16[1,64,192]{2,1,0:T(8,128)(2,1)S(1)}, bf16[1,64,192]{2,1,0:T(8,128)(2,1)S(1)}, u32[]{:S(2)}, u32[]{:S(2)}) collective-permute-start(bf16[1,64,192]{2,1,0:T(8,128)(2,1)S(1)} %get-tuple-element.70), channel_id=1, source_target_pairs={{0,16},{16,32},{32,48},{48,64},{64,80},{80,96},{96,112},{112,128},... | collective-permute-start | bytes 73736 | tf_op jit(solution)/shard_map/ppermute | solution.py:25
  8.9 0.9 fusion.3
  9.8 1.1 pad_maximum_fusion.stacked
  10.9 0.0 copy-start
  10.9 0.0 copy-start.1
  10.9 0.0 copy-start.2
  10.9 0.0 copy-start.3
  10.9 0.0 copy-start.4
  11.0 0.2 shard_map.126.own_taps
  11.1 0.0 collective-permute-done.1.high
  11.1 0.0 collective-permute-done.low
  11.2 4.6 %collective-permute-start.2 = (bf16[10,1,192]{2,1,0:T(2,128)(2,1)S(1)}, bf16[10,1,192]{2,1,0:T(2,128)(2,1)S(1)}, u32[]{:S(2)}, u32[]{:S(2)}) collective-permute-start(bf16[10,1,192]{2,1,0:T(2,128)(2,1)S(1)} %pad_maximum_fusion.3), channel_id=1, source_target_pairs={{0,1},{1,2},{2,3},{3,4},{4,5},{5,6},{6,7},{7,8},{8,9},{9,10},{10,1... | collective-permute-start | bytes 11528 | tf_op jit(solution)/shard_map/ppermute | solution.py:36
  15.8 5.6 %collective-permute-start.3 = (bf16[10,1,192]{2,1,0:T(2,128)(2,1)S(1)}, bf16[10,1,192]{2,1,0:T(2,128)(2,1)S(1)}, u32[]{:S(2)}, u32[]{:S(2)}) collective-permute-start(bf16[10,1,192]{2,1,0:T(2,128)(2,1)S(1)} %pad_maximum_fusion.4), channel_id=1, source_target_pairs={{1,0},{2,1},{3,2},{4,3},{5,4},{6,5},{7,6},{8,7},{9,8},{10,9},{11,1... | collective-permute-start | bytes 11528 | tf_op jit(solution)/shard_map/ppermute | solution.py:36
  21.4 0.0 collective-permute-done.2.left
  21.4 0.8 collective-permute-done.3.right
  22.2 0.0 copy-done
  22.2 0.0 copy-done.1
  22.2 0.0 copy-done.2
  22.2 0.0 copy-done.3
  22.2 0.0 copy-done.4
  22.2 2.6 %shard_map.127 = (bf16[8,64,128]{2,1,0:T(8,128)(2,1)}, f32[8,64,128]{2,1,0:T(8,128)}, f32[8,64,128]{2,1,0:T(8,128)}, bf16[512,512]{1,0:T(8,128)(2,1)S(1)}, bf16[...) custom-call(bf16[640,576]{1,0:T(8,128)(2,1)S(1)} %shard_map.126.own_taps, ...), custom_call_target="tpu_custom_call" | custom-call | flops 1358954496 | bytes 6071808 | tf_op jit(solution)/shard_map/pallas_call | solution.py:230
  24.8 2.3 %collective-permute-start.4 = (bf16[16,224,128]{2,1,0:T(8,128)(2,1)S(1)}, bf16[16,224,128]{2,1,0:T(8,128)(2,1)S(1)}, u32[]{:S(2)}, u32[]{:S(2)}) collective-permute-start(bf16[16,224,128]{2,1,0:T(8,128)(2,1)S(1)} %get-tuple-element.43), channel_id=1, source_target_pairs={{0,1},{1,0},{2,3},{3,2},{4,5},{5,4},{6,7},{7,6},{8,9},{9,8},{10,11... | collective-permute-start | bytes 2752520 | tf_op jit(solution)/shard_map/ppermute | solution.py:277
  27.1 2.1 %collective-permute-done.4.received = bf16[16,224,128]{2,1,0:T(8,128)(2,1)S(1)} collective-permute-done((bf16[16,224,128]{2,1,0:T(8,128)(2,1)S(1)}, bf16[16,224,128]{2,1,0:T(8,128)(2,1)S(1)}, u32[]{:S(2)}, u32[]{:S(2)}) %collective-permute-start.4) | collective-permute-done | bytes 917536 | tf_op jit(solution)/shard_map/ppermute | solution.py:277
  29.2 1.6 %shard_map.128 = bf16[16,224,128]{2,1,0:T(8,128)(2,1)} custom-call(bf16[640,576]{1,0:T(8,128)(2,1)S(1)} %get-tuple-element.40.taps, bf16[512,512]{1,0:T(8,128)(2,1)S(1)} %get-tuple-element.41.grad_gates, f32[8,512]{1,0:T(8,128)S(1)} %get-tuple-element.42.sums, bf16[16,224,128]{2,1,0:T(8,128)(2,1)S(1)} %collective-permute-done.4.received), custom_call_target="tpu_custom_call" | custom-call | flops 452984832 | bytes 3112960 | tf_op jit(solution)/shard_map/pallas_call | solution.py:230
  30.7 7.0 %all-to-all-start = ((bf16[16,224,128]{2,1,0:T(8,128)(2,1)}), bf16[16,224,128]{2,1,0:T(8,128)(2,1)S(1)}, u32[]{:S(2)}, u32[]{:S(2)}) async-start(bf16[16,224,128]{2,1,0:T(8,128)(2,1)} %shard_map.128), calls=%async_computation | async-start | bytes 1835008 | tf_op jit(solution)/shard_map/all_to_all | solution.py:285
  37.7 1.3 %collective-permute-start.6 = (bf16[1,64,512]{2,1,0:T(8,128)(2,1)S(1)}, bf16[1,64,512]{2,1,0:T(8,128)(2,1)S(1)}, u32[]{:S(2)}, u32[]{:S(2)}) collective-permute-start(bf16[1,64,512]{2,1,0:T(8,128)(2,1)S(1)} %get-tuple-element.65), channel_id=1, source_target_pairs={{16,0},{32,16},{48,32},{64,48},{80,64},{96,80},{112,96},{128,112},... | collective-permute-start | bytes 196616 | tf_op jit(solution)/shard_map/ppermute | solution.py:26
  39.0 5.5 %collective-permute-start.5 = (bf16[1,64,512]{2,1,0:T(8,128)(2,1)S(1)}, bf16[1,64,512]{2,1,0:T(8,128)(2,1)S(1)}, u32[]{:S(2)}, u32[]{:S(2)}) collective-permute-start(bf16[1,64,512]{2,1,0:T(8,128)(2,1)S(1)} %get-tuple-element.66), channel_id=1, source_target_pairs={{0,16},{16,32},{32,48},{48,64},{64,80},{80,96},{96,112},{112,128},... | collective-permute-start | bytes 196616 | tf_op jit(solution)/shard_map/ppermute | solution.py:25
  44.5 7.9 %collective-permute-done.6.high = bf16[1,64,512]{2,1,0:T(8,128)(2,1)S(1)} collective-permute-done((bf16[1,64,512]{2,1,0:T(8,128)(2,1)S(1)}, bf16[1,64,512]{2,1,0:T(8,128)(2,1)S(1)}, u32[]{:S(2)}, u32[]{:S(2)}) %collective-permute-start.6) | collective-permute-done | bytes 65568 | tf_op jit(solution)/shard_map/ppermute | solution.py:26
  52.5 0.0 collective-permute-done.5.low
  52.5 0.4 all-to-all-done
  52.9 0.1 reduce_sum.21
  53.0 29.4 %all_to_all.20 = bf16[16,14,128]{2,1,0:T(8,128)(2,1)S(1)} all-to-all(bf16[16,14,128]{2,1,0:T(8,128)(2,1)S(1)} %reshape.40), channel_id=1, replica_groups=mesh['z'=16,'xh'=2,'y'=4,'xl'=2,'core'=2] {'z'}, dimensions={0} | all-to-all | bytes 114688 | tf_op jit(solution)/shard_map/all_to_all | solution.py:289
  82.5 14.4 %all_to_all.21 = bf16[16,14,128]{2,1,0:T(8,128)(2,1)S(1)} all-to-all(bf16[16,14,128]{2,1,0:T(8,128)(2,1)S(1)} %broadcast_in_dim.6), channel_id=1, replica_groups=mesh['z'=16,'xh'=2,'y'=4,'xl'=2,'core'=2] {'z'}, dimensions={0} | all-to-all | bytes 114688 | tf_op jit(solution)/shard_map/all_to_all | solution.py:292
  96.9 1.0 broadcast_in_dim.15
  97.9 4.7 %all-to-all-start.3 = ((bf16[16,224,128]{2,1,0:T(8,128)(2,1)}), bf16[16,224,128]{2,1,0:T(8,128)(2,1)S(1)}, u32[]{:S(2)}, u32[]{:S(2)}) async-start(bf16[16,224,128]{2,1,0:T(8,128)(2,1)} %broadcast_in_dim.15), calls=%async_computation.3 | async-start | bytes 1835008 | tf_op jit(solution)/shard_map/all_to_all | solution.py:296
  102.8 7.2 %collective-permute-start.7 = (bf16[10,1,512]{2,1,0:T(2,128)(2,1)S(1)}, bf16[10,1,512]{2,1,0:T(2,128)(2,1)S(1)}, u32[]{:S(2)}, u32[]{:S(2)}) collective-permute-start(bf16[10,1,512]{2,1,0:T(2,128)(2,1)S(1)} %pad_maximum_fusion.1), channel_id=1, source_target_pairs={{0,1},{1,2},{2,3},{3,4},{4,5},{5,6},{6,7},{7,8},{8,9},{9,10},{10,1... | collective-permute-start | bytes 30728 | tf_op jit(solution)/shard_map/ppermute | solution.py:36
  110.0 1.9 %collective-permute-start.8 = (bf16[10,1,512]{2,1,0:T(2,128)(2,1)S(1)}, bf16[10,1,512]{2,1,0:T(2,128)(2,1)S(1)}, u32[]{:S(2)}, u32[]{:S(2)}) collective-permute-start(bf16[10,1,512]{2,1,0:T(2,128)(2,1)S(1)} %pad_maximum_fusion.2), channel_id=1, source_target_pairs={{1,0},{2,1},{3,2},{4,3},{5,4},{6,5},{7,6},{8,7},{9,8},{10,9},{11,1... | collective-permute-start | bytes 30728 | tf_op jit(solution)/shard_map/ppermute | solution.py:36
  111.9 0.0 collective-permute-done.7.left
  111.9 4.5 %collective-permute-done.8.right = bf16[10,1,512]{2,1,0:T(2,128)(2,1)S(1)} collective-permute-done((bf16[10,1,512]{2,1,0:T(2,128)(2,1)S(1)}, bf16[10,1,512]{2,1,0:T(2,128)(2,1)S(1)}, u32[]{:S(2)}, u32[]{:S(2)}) %collective-permute-start.8) | collective-permute-done | bytes 10272 | tf_op jit(solution)/shard_map/ppermute | solution.py:36
  116.4 2.4 %shard_map.129 = (bf16[8,64,64]{2,1,0:T(8,128)(2,1)}, bf16[8,64,128]{2,1,0:T(8,128)(2,1)}) custom-call(bf16[512,512]{1,0:T(8,128)(2,1)S(1)} %get-tuple-element.41.grad_gates, bf16[1,64,512]{2,1,0:T(8,128)(2,1)S(1)} %collective-permute-done.5.low, bf16[1,64,512]{2,1,0:T(8,128)(2,1)S(1)} %collective-permute-done.6.high, ...), custom_call_target="tpu_custom_call" | custom-call | flops 905969664 | bytes 2641920 | tf_op jit(solution)/shard_map/pallas_call | solution.py:230
  118.7 0.0 all-to-all-done.3.slots
  118.7 2.9 %collective-permute-start.9 = (bf16[16,224,128]{2,1,0:T(8,128)(2,1)S(1)}, bf16[16,224,128]{2,1,0:T(8,128)(2,1)S(1)}, u32[]{:S(2)}, u32[]{:S(2)}) collective-permute-start(bf16[16,224,128]{2,1,0:T(8,128)(2,1)S(1)} %all-to-all-done.3.slots), channel_id=1, source_target_pairs={{0,1},{1,0},{2,3},{3,2},{4,5},{5,4},{6,7},{7,6},{8,9},{9,8},{10,11... | collective-permute-start | bytes 2752520 | tf_op jit(solution)/shard_map/ppermute | solution.py:308
  121.6 1.1 shard_map.130
  122.7 1.0 collective-permute-done.9.slots
  123.7 1.6 %shard_map.131 = (bf16[1728,512]{1,0:T(8,128)(2,1)}, f32[1,512]{1,0:T(1,128)}) custom-call(f32[1,512]{1,0:T(1,128)S(1)} %get-tuple-element.59.own_bias, bf16[16,224,128]{2,1,0:T(8,128)(2,1)S(1)} %collective-permute-done.9.slots, bf16[1728,512]{1,0:T(8,128)(2,1)} %get-tuple-element.60.own_kernel_part), custom_call_target="tpu_custom_call", output_to_operand_aliasing={{0}: (2, {})} | custom-call | bytes 4460544 | tf_op jit(solution)/shard_map/pallas_call | solution.py:230
  (14 shorter events, 0.3 us)
Async XLA Ops:
  1.5 9.6 %collective-permute-start.1 = (bf16[1,64,192]{2,1,0:T(8,128)(2,1)S(1)}, bf16[1,64,192]{2,1,0:T(8,128)(2,1)S(1)}, u32[]{:S(2)}, u32[]{:S(2)}) collective-permute-start(bf16[1,64,192]{2,1,0:T(8,128)(2,1)S(1)} %get-tuple-element.69), channel_id=1, source_target_pairs={{16,0},{32,16},{48,32},{64,48},{80,64},{96,80},{112,96},{128,112},... | collective-permute-start | bytes 73736 | tf_op jit(solution)/shard_map/ppermute | solution.py:26
  2.8 8.4 %collective-permute-start = (bf16[1,64,192]{2,1,0:T(8,128)(2,1)S(1)}, bf16[1,64,192]{2,1,0:T(8,128)(2,1)S(1)}, u32[]{:S(2)}, u32[]{:S(2)}) collective-permute-start(bf16[1,64,192]{2,1,0:T(8,128)(2,1)S(1)} %get-tuple-element.70), channel_id=1, source_target_pairs={{0,16},{16,32},{32,48},{48,64},{64,80},{80,96},{96,112},{112,128},... | collective-permute-start | bytes 73736 | tf_op jit(solution)/shard_map/ppermute | solution.py:25
  10.9 11.3 %copy-start = (bf16[3,3,192,512]{3,2,1,0:T(8,128)(2,1)S(1)}, bf16[3,3,192,512]{3,2,1,0:T(8,128)(2,1)}, u32[]{:S(2)}) copy-start(bf16[3,3,192,512]{3,2,1,0:T(8,128)(2,1)} %param.10) | copy-start | bytes 5308420
  10.9 11.3 %copy-start.1 = (f32[8,64,128]{2,1,0:T(8,128)S(1)}, f32[8,64,128]{2,1,0:T(8,128)}, u32[]{:S(2)}) copy-start(f32[8,64,128]{2,1,0:T(8,128)} %cell_prev.1) | copy-start | bytes 786436
  10.9 11.3 %copy-start.2 = (f32[8,64,128]{2,1,0:T(8,128)S(1)}, f32[8,64,128]{2,1,0:T(8,128)}, u32[]{:S(2)}) copy-start(f32[8,64,128]{2,1,0:T(8,128)} %cell_cot.1) | copy-start | bytes 786436
  10.9 11.3 %copy-start.3 = (bf16[8,64,128]{2,1,0:T(8,128)(2,1)S(1)}, bf16[8,64,128]{2,1,0:T(8,128)(2,1)}, u32[]{:S(2)}) copy-start(bf16[8,64,128]{2,1,0:T(8,128)(2,1)} %hidden_cot.1) | copy-start | bytes 393220
  10.9 11.3 %copy-start.4 = (f32[512]{0:T(512)S(1)}, f32[512]{0:T(512)}, u32[]{:S(2)}) copy-start(f32[512]{0:T(512)} %param.11) | copy-start | bytes 6148
  11.2 10.2 %collective-permute-start.2 = (bf16[10,1,192]{2,1,0:T(2,128)(2,1)S(1)}, bf16[10,1,192]{2,1,0:T(2,128)(2,1)S(1)}, u32[]{:S(2)}, u32[]{:S(2)}) collective-permute-start(bf16[10,1,192]{2,1,0:T(2,128)(2,1)S(1)} %pad_maximum_fusion.3), channel_id=1, source_target_pairs={{0,1},{1,2},{2,3},{3,4},{4,5},{5,6},{6,7},{7,8},{8,9},{9,10},{10,1... | collective-permute-start | bytes 11528 | tf_op jit(solution)/shard_map/ppermute | solution.py:36
  15.8 6.4 %collective-permute-start.3 = (bf16[10,1,192]{2,1,0:T(2,128)(2,1)S(1)}, bf16[10,1,192]{2,1,0:T(2,128)(2,1)S(1)}, u32[]{:S(2)}, u32[]{:S(2)}) collective-permute-start(bf16[10,1,192]{2,1,0:T(2,128)(2,1)S(1)} %pad_maximum_fusion.4), channel_id=1, source_target_pairs={{1,0},{2,1},{3,2},{4,3},{5,4},{6,5},{7,6},{8,7},{9,8},{10,9},{11,1... | collective-permute-start | bytes 11528 | tf_op jit(solution)/shard_map/ppermute | solution.py:36
  24.8 4.4 %collective-permute-start.4 = (bf16[16,224,128]{2,1,0:T(8,128)(2,1)S(1)}, bf16[16,224,128]{2,1,0:T(8,128)(2,1)S(1)}, u32[]{:S(2)}, u32[]{:S(2)}) collective-permute-start(bf16[16,224,128]{2,1,0:T(8,128)(2,1)S(1)} %get-tuple-element.43), channel_id=1, source_target_pairs={{0,1},{1,0},{2,3},{3,2},{4,5},{5,4},{6,7},{7,6},{8,9},{9,8},{10,11... | collective-permute-start | bytes 2752520 | tf_op jit(solution)/shard_map/ppermute | solution.py:277
  30.7 22.1 %all-to-all-start = ((bf16[16,224,128]{2,1,0:T(8,128)(2,1)}), bf16[16,224,128]{2,1,0:T(8,128)(2,1)S(1)}, u32[]{:S(2)}, u32[]{:S(2)}) async-start(bf16[16,224,128]{2,1,0:T(8,128)(2,1)} %shard_map.128), calls=%async_computation | async-start | bytes 1835008 | tf_op jit(solution)/shard_map/all_to_all | solution.py:285
  37.7 14.7 %collective-permute-start.6 = (bf16[1,64,512]{2,1,0:T(8,128)(2,1)S(1)}, bf16[1,64,512]{2,1,0:T(8,128)(2,1)S(1)}, u32[]{:S(2)}, u32[]{:S(2)}) collective-permute-start(bf16[1,64,512]{2,1,0:T(8,128)(2,1)S(1)} %get-tuple-element.65), channel_id=1, source_target_pairs={{16,0},{32,16},{48,32},{64,48},{80,64},{96,80},{112,96},{128,112},... | collective-permute-start | bytes 196616 | tf_op jit(solution)/shard_map/ppermute | solution.py:26
  39.0 13.4 %collective-permute-start.5 = (bf16[1,64,512]{2,1,0:T(8,128)(2,1)S(1)}, bf16[1,64,512]{2,1,0:T(8,128)(2,1)S(1)}, u32[]{:S(2)}, u32[]{:S(2)}) collective-permute-start(bf16[1,64,512]{2,1,0:T(8,128)(2,1)S(1)} %get-tuple-element.66), channel_id=1, source_target_pairs={{0,16},{16,32},{32,48},{48,64},{64,80},{80,96},{96,112},{112,128},... | collective-permute-start | bytes 196616 | tf_op jit(solution)/shard_map/ppermute | solution.py:25
  97.9 20.8 %all-to-all-start.3 = ((bf16[16,224,128]{2,1,0:T(8,128)(2,1)}), bf16[16,224,128]{2,1,0:T(8,128)(2,1)S(1)}, u32[]{:S(2)}, u32[]{:S(2)}) async-start(bf16[16,224,128]{2,1,0:T(8,128)(2,1)} %broadcast_in_dim.15), calls=%async_computation.3 | async-start | bytes 1835008 | tf_op jit(solution)/shard_map/all_to_all | solution.py:296
  102.8 9.1 %collective-permute-start.7 = (bf16[10,1,512]{2,1,0:T(2,128)(2,1)S(1)}, bf16[10,1,512]{2,1,0:T(2,128)(2,1)S(1)}, u32[]{:S(2)}, u32[]{:S(2)}) collective-permute-start(bf16[10,1,512]{2,1,0:T(2,128)(2,1)S(1)} %pad_maximum_fusion.1), channel_id=1, source_target_pairs={{0,1},{1,2},{2,3},{3,4},{4,5},{5,6},{6,7},{7,8},{8,9},{9,10},{10,1... | collective-permute-start | bytes 30728 | tf_op jit(solution)/shard_map/ppermute | solution.py:36
  110.0 6.4 %collective-permute-start.8 = (bf16[10,1,512]{2,1,0:T(2,128)(2,1)S(1)}, bf16[10,1,512]{2,1,0:T(2,128)(2,1)S(1)}, u32[]{:S(2)}, u32[]{:S(2)}) collective-permute-start(bf16[10,1,512]{2,1,0:T(2,128)(2,1)S(1)} %pad_maximum_fusion.2), channel_id=1, source_target_pairs={{1,0},{2,1},{3,2},{4,3},{5,4},{6,5},{7,6},{8,7},{9,8},{10,9},{11,1... | collective-permute-start | bytes 30728 | tf_op jit(solution)/shard_map/ppermute | solution.py:36
  118.7 4.9 %collective-permute-start.9 = (bf16[16,224,128]{2,1,0:T(8,128)(2,1)S(1)}, bf16[16,224,128]{2,1,0:T(8,128)(2,1)S(1)}, u32[]{:S(2)}, u32[]{:S(2)}) collective-permute-start(bf16[16,224,128]{2,1,0:T(8,128)(2,1)S(1)} %all-to-all-done.3.slots), channel_id=1, source_target_pairs={{0,1},{1,0},{2,3},{3,2},{4,5},{5,4},{6,7},{7,6},{8,9},{9,8},{10,11... | collective-permute-start | bytes 2752520 | tf_op jit(solution)/shard_map/ppermute | solution.py:308

commit v5 on v4

--- a/solution.py
+++ b/solution.py
@@ -18,22 +18,24 @@
 VMEM = 40 * 1024 * 1024
 
 
+def to_neighbours(axes, last, first):
+    count = lax.axis_size(axes)
+    inner = [(i, i ^ 1) for i in range(count)]
+    outer = [(i, i + 1 if i % 2 else i - 1) for i in range(1, count - 1)]
+    even = lax.axis_index(axes[-1]) == 0
+    near = lax.ppermute(jnp.where(even, last, first), axes, inner)
+    far = lax.ppermute(jnp.where(even, first, last), axes, outer)
+    return jnp.where(even, far, near), jnp.where(even, near, far)
+
+
 def halo_rows(block):
-    count = lax.axis_size(ROWS)
-    forward = [(i, i + 1) for i in range(count - 1)]
-    backward = [(target, source) for source, target in forward]
-    low = lax.ppermute(block[TR - 1 :], ROWS, forward)
-    high = lax.ppermute(block[:1], ROWS, backward)
-    return low, high
+    return to_neighbours(ROWS, block[TR - 1 :], block[:1])
 
 
 def halo_cols(low, block, high):
-    count = lax.axis_size(COLS)
-    forward = [(i, i + 1) for i in range(count - 1)]
-    backward = [(target, source) for source, target in forward]
     last = jnp.concatenate([low[:, TC - 1 :], block[:, TC - 1 :], high[:, TC - 1 :]], axis=0)
     first = jnp.concatenate([low[:, :1], block[:, :1], high[:, :1]], axis=0)
-    return lax.ppermute(last, COLS, forward), lax.ppermute(first, COLS, backward)
+    return to_neighbours(COLS, last, first)
 
 
 def shifted(row, before, after):
@@ -149,37 +151,55 @@
         copy(slot).wait()
 
 
-def input_kernel(
-    grad_gates, low, high, left, right, kernel, grad_features, grad_hidden, moved, result
+def input_kernel(grad_gates, kernel, inner, edges, to_left, to_right, spread):
+    spread[...] = jnp.zeros_like(spread)
+    for a in range(3):
+        spread[a * TC : a * TC + CELLS, :] += lax.dot_general(
+            grad_gates[...], kernel[a], (((1,), (1,)), ((), ())), preferred_element_type=F32
+        )
+    lefts, rights = [], []
+    for r in range(TR + 2):
+        rows = spread[r * TC : (r + 1) * TC, :]
+        lower, middle, upper = rows[:, :ZCH], rows[:, ZCH : 2 * ZCH], rows[:, 2 * ZCH :]
+        _, from_lower = shifted(lower, 0.0, 0.0)
+        from_upper, _ = shifted(upper, 0.0, 0.0)
+        total = middle + from_lower + from_upper
+        lefts.append(lower[:1])
+        rights.append(upper[TC - 1 :])
+        if r == 0:
+            edges[0] = total
+        elif r == TR + 1:
+            edges[1] = total
+        else:
+            inner[(r - 1) * TC : r * TC, :] = total
+    to_left[...] = jnp.concatenate(lefts, axis=0).astype(BF16)
+    to_right[...] = jnp.concatenate(rights, axis=0).astype(BF16)
+
+
+def with_columns(row, before, after):
+    place = lax.broadcasted_iota(jnp.int32, row.shape, 0)
+    return row + jnp.where(place == 0, before, 0.0) + jnp.where(place == TC - 1, after, 0.0)
+
+
+def edge_kernel(edges, from_left, from_right, to_above, to_below):
+    before, after = from_left[...].astype(F32), from_right[...].astype(F32)
+    to_above[0] = with_columns(edges[0], before[:1], after[:1]).astype(BF16)
+    to_below[0] = with_columns(edges[1], before[TR + 1 :], after[TR + 1 :]).astype(BF16)
+
+
+def sum_kernel(
+    inner, from_left, from_right, from_above, from_below, grad_features, grad_hidden
 ):
-    for r in range(TR + 2):
+    before, after = from_left[...].astype(F32), from_right[...].astype(F32)
+    for r in range(TR):
+        row = inner[r * TC : (r + 1) * TC, :]
+        row = with_columns(row, before[r + 1 : r + 2], after[r + 1 : r + 2])
         if r == 0:
-            row = low[0]
-        elif r == TR + 1:
-            row = high[0]
-        else:
-            row = grad_gates[(r - 1) * TC : r * TC, :]
-        rows = slice(r * TC, (r + 1) * TC)
-        down, up = shifted(row.astype(F32), left[r].astype(F32), right[r].astype(F32))
-        moved[0, rows, :] = down.astype(BF16)
-        moved[1, rows, :] = row
-        moved[2, rows, :] = up.astype(BF16)
-    for tap in range(9):
-        a, b = tap // 3, tap % 3
-        term = lax.dot_general(
-            moved[2 - b, (2 - a) * TC : (2 - a) * TC + CELLS, :],
-            kernel[a, b * ZCH : (b + 1) * ZCH, :],
-            (((1,), (1,)), ((), ())),
-            preferred_element_type=F32,
-        )
-        if tap == 0:
-            result[...] = term
-        else:
-            result[...] += term
-    for r in range(TR):
-        block = result[r * TC : (r + 1) * TC, :]
-        grad_features[r] = block[:, :FEAT].astype(BF16)
-        grad_hidden[r] = block[:, FEAT:].astype(BF16)
+            row = row + from_above[0].astype(F32)
+        if r == TR - 1:
+            row = row + from_below[0].astype(F32)
+        grad_features[r] = row[:, :FEAT].astype(BF16)
+        grad_hidden[r] = row[:, FEAT:].astype(BF16)
 
 
 def place_half(slots, place, grad_kernel, grad_bias, last_slots, sems):
@@ -275,41 +295,53 @@
         flops=work + work // 2,
     )
     received = lax.ppermute(send, "core", swap)
+    inner, edges, to_left, to_right = call(
+        input_kernel,
+        (
+            shape((CELLS, ZCH), F32),
+            shape((2, TC, ZCH), F32),
+            shape((TR + 2, ZCH), BF16),
+            shape((TR + 2, ZCH), BF16),
+        ),
+        grad_gates, weights,
+        scratch=[pltpu.VMEM(((TR + 2) * TC, TAPS), F32)],
+        flops=work,
+    )
+    received, to_left, to_right = lax.optimization_barrier((received, to_left, to_right))
     (half,) = call(
         own_kernel, (shape((plane, SLOT, 128), BF16),), taps, grad_gates, sums, received,
         scratch=[pltpu.VMEM((plane, SLOT, 128), BF16), pltpu.SemaphoreType.DMA((plane,))],
         flops=work // 2,
         far_outs=1,
     )
-    half, gate_tile = lax.optimization_barrier((half, grad_gates.reshape(TR, TC, GATES)))
+    half, to_left, to_right = lax.optimization_barrier((half, to_left, to_right))
     part = lax.all_to_all(half, PLANE, 0, 0, tiled=True)
-    gate_low, gate_high = halo_rows(gate_tile)
-    part, gate_low, gate_high = lax.optimization_barrier((part, gate_low, gate_high))
+    from_left, from_right = to_neighbours(COLS, to_right, to_left)
+    part, from_left, from_right = lax.optimization_barrier((part, from_left, from_right))
     part = jnp.sum(part.astype(F32), axis=0).astype(BF16)
     part = lax.all_to_all(part.reshape(depth, SLOT // depth, 128), "z", 0, 0, tiled=True)
     scale = 1.0 / (TR * lax.axis_size(ROWS))
     part = (jnp.sum(part.astype(F32), axis=0) * scale).astype(BF16)
     part = lax.all_to_all(copies_of(part, depth), "z", 0, 0, tiled=True).reshape(SLOT, 128)
-    copies, gate_low, gate_tile, gate_high = lax.optimization_barrier(
-        (copies_of(part, plane), gate_low, gate_tile, gate_high)
-    )
+    copies, edges = lax.optimization_barrier((copies_of(part, plane), edges))
     half = lax.all_to_all(copies, PLANE, 0, 0, tiled=True)
-    gate_left, gate_right = halo_cols(gate_low, gate_tile, gate_high)
+    row = shape((1, TC, ZCH), BF16)
+    to_above, to_below = call(edge_kernel, (row, row), edges, from_left, from_right)
+    from_above, from_below = to_neighbours(ROWS, to_below, to_above)
+    half, from_above, from_below = lax.optimization_barrier((half, from_above, from_below))
     grad_features, grad_hidden = call(
-        input_kernel,
+        sum_kernel,
         (shape((TR, TC, FEAT), BF16), shape((TR, TC, CH), BF16)),
-        grad_gates, gate_low, gate_high, gate_left, gate_right, weights,
-        scratch=[pltpu.VMEM((3, (TR + 2) * TC, GATES), BF16), pltpu.VMEM((CELLS, ZCH), F32)],
-        flops=work,
-    )
-    half, grad_features, grad_hidden = lax.optimization_barrier(
-        (half, grad_features, grad_hidden)
+        inner, from_left, from_right, from_above, from_below,
     )
     other = lax.ppermute(half, "core", swap)
     outs = (shape((3 * TAPS, GATES), BF16), shape((1, GATES), F32))
     scratch = [pltpu.VMEM((2, 16, 128), BF16), pltpu.SemaphoreType.DMA((2 * GROUPS + 2,))]
     grad_kernel, own_bias = call(
         join_own_kernel, outs, half, scratch=scratch, far=1, far_outs=1
+    )
+    other, grad_features, grad_hidden = lax.optimization_barrier(
+        (other, grad_features, grad_hidden)
     )
     grad_kernel, grad_bias = call(
         join_other_kernel, outs, own_bias, other, grad_kernel,

time: 126 us -> 123 us (0.976)
  blocking collectives: 43.8 us -> 39.8 us
  waiting for transfers between devices: 16.7 us -> 20.3 us
  starting transfers between devices: 50.2 us -> 47.4 us
    ppermute x8, starting transfers between devices: 33.4 us -> 27.6 us  [the longest x4 21 us: to_neighbours(): near = lax.ppermute(jnp.where(even, last, first), axes, inner)]
    all_to_all x1, blocking collectives: 29.4 us -> 25.4 us  [local(): lax.all_to_all(part.reshape(depth, SLOT // depth, 128), 'z', 0, 0, tiled=...]
    ppermute x1, starting transfers between devices: 2.86 us -> 6.63 us  [local(): other = lax.ppermute(half, 'core', swap)]
    ppermute x8, waiting for transfers between devices: 13.2 us -> 15.6 us  [the longest x4 10.1 us: to_neighbours(): far = lax.ppermute(jnp.where(even, first, last), axes, outer)]
    all_to_all x1, waiting for transfers between devices: 0.41 us -> 2.32 us  [local(): part = lax.all_to_all(half, PLANE, 0, 0, tiled=True)]
    all_to_all x1, waiting for transfers between devices: 0.01 us -> 1.47 us  [local(): half = lax.all_to_all(copies, PLANE, 0, 0, tiled=True)]
    ppermute x1, waiting for transfers between devices: 2.09 us -> 0.75 us  [local(): received = lax.ppermute(send, 'core', swap)]
    concatenate x3 -> x2, other arithmetic: 2.84 us -> 1.97 us  [local(): stacked = jnp.concatenate([features, hidden_prev], axis=2)]
  transfers between devices with their start and end apart: 12 -> 12, of which waited for: 6 -> 7; matrix products, arithmetic and copies ran while one was open for 2% -> 2% of each run, Pallas kernels for 3% -> 3%
where the time goes in v5:
time: 123 us; the launch traced here: 122 us
  starting transfers between devices  47.4 us (39%)
  blocking collectives  39.8 us (32%)
  waiting for transfers between devices  20.3 us (17%)
  Pallas kernels  9.55 us (8%)
  other arithmetic  3.12 us (3%)
    all_to_all x1, blocking collectives, local(): lax.all_to_all(part.reshape(depth, SLOT // depth, 128), 'z', 0, 0, tiled=...  25.4 us
    ppermute x4, starting transfers between devices, to_neighbours(): near = lax.ppermute(jnp.where(even, last, first), axes, inner)  21 us
    all_to_all x1, blocking collectives, local(): lax.all_to_all(copies_of(part, depth), 'z', 0, 0, tiled=True)  14.4 us
    ppermute x4, waiting for transfers between devices, to_neighbours(): far = lax.ppermute(jnp.where(even, first, last), axes, outer)  10.1 us
    pallas_call x8, Pallas kernels, call(): pl.pallas_call(body, out_shape=outs, in_specs=[whole] * (len(args) - far)...  9.55 us
    ppermute x4, starting transfers between devices, to_neighbours(): far = lax.ppermute(jnp.where(even, first, last), axes, outer)  6.69 us
    ppermute x1, starting transfers between devices, local(): other = lax.ppermute(half, 'core', swap)  6.63 us
    all_to_all x1, starting transfers between devices, local(): part = lax.all_to_all(half, PLANE, 0, 0, tiled=True)  6.03 us
  transfers between devices with their start and end apart: 12, of which 7 were waited for; matrix products, arithmetic and copies ran while one was open for 2% of the time, Pallas kernels for 3%

profile of v5, /device:TPU:1, one launch (start us, length us, event | category | flops | bytes accessed | tf_op | source)
XLA Modules:
  0.0 122.3 jit_solution(4338512125319769031)
XLA Ops:
  0.6 0.9 broadcast_select_fusion.6
  1.5 0.7 collective-permute-start
  2.2 8.3 %collective-permute-start.1 = (bf16[1,64,192]{2,1,0:T(8,128)(2,1)S(1)}, bf16[1,64,192]{2,1,0:T(8,128)(2,1)S(1)}, u32[]{:S(2)}, u32[]{:S(2)}) collective-permute-start(bf16[1,64,192]{2,1,0:T(8,128)(2,1)S(1)} %get-tuple-element.85), channel_id=1, source_target_pairs={{0,16},{16,0},{32,48},{48,32},{64,80},{80,64},{96,112},{112,96},{1... | collective-permute-start | bytes 73736 | tf_op jit(solution)/shard_map/ppermute | solution.py:26
  10.5 0.9 fusion.2
  11.4 1.1 pad_maximum_fusion.stacked
  12.5 0.0 copy-start
  12.5 0.0 copy-start.1
  12.5 0.0 copy-start.2
  12.5 0.0 copy-start.3
  12.5 0.0 copy-start.4
  12.6 0.2 shard_map.126.own_taps
  12.7 0.0 collective-permute-done
  12.7 0.0 collective-permute-done.1
  12.8 5.5 %collective-permute-start.3 = (bf16[10,1,192]{2,1,0:T(2,128)(2,1)S(1)}, bf16[10,1,192]{2,1,0:T(2,128)(2,1)S(1)}, u32[]{:S(2)}, u32[]{:S(2)}) collective-permute-start(bf16[10,1,192]{2,1,0:T(2,128)(2,1)S(1)} %get-tuple-element.102), channel_id=1, source_target_pairs={{0,1},{1,0},{2,3},{3,2},{4,5},{5,4},{6,7},{7,6},{8,9},{9,8},{10,11... | collective-permute-start | bytes 11528 | tf_op jit(solution)/shard_map/ppermute | solution.py:26
  18.4 1.9 %collective-permute-start.2 = (bf16[10,1,192]{2,1,0:T(2,128)(2,1)S(1)}, bf16[10,1,192]{2,1,0:T(2,128)(2,1)S(1)}, u32[]{:S(2)}, u32[]{:S(2)}) collective-permute-start(bf16[10,1,192]{2,1,0:T(2,128)(2,1)S(1)} %get-tuple-element.103), channel_id=1, source_target_pairs={{1,2},{2,1},{3,4},{4,3},{5,6},{6,5},{7,8},{8,7},{9,10},{10,9},{11,... | collective-permute-start | bytes 11528 | tf_op jit(solution)/shard_map/ppermute | solution.py:27
  20.3 0.0 collective-permute-done.3
  20.3 3.1 %collective-permute-done.2 = bf16[10,1,192]{2,1,0:T(2,128)(2,1)S(1)} collective-permute-done((bf16[10,1,192]{2,1,0:T(2,128)(2,1)S(1)}, bf16[10,1,192]{2,1,0:T(2,128)(2,1)S(1)}, u32[]{:S(2)}, u32[]{:S(2)}) %collective-permute-start.2) | collective-permute-done | bytes 3872 | tf_op jit(solution)/shard_map/ppermute | solution.py:27
  23.4 0.0 copy-done
  23.4 0.0 copy-done.1
  23.4 0.0 copy-done.2
  23.4 0.0 copy-done.3
  23.4 0.0 copy-done.4
  23.5 2.6 %shard_map.127 = (bf16[8,64,128]{2,1,0:T(8,128)(2,1)}, f32[8,64,128]{2,1,0:T(8,128)}, f32[8,64,128]{2,1,0:T(8,128)}, bf16[512,512]{1,0:T(8,128)(2,1)S(1)}, bf16[...) custom-call(bf16[640,576]{1,0:T(8,128)(2,1)S(1)} %shard_map.126.own_taps, ...), custom_call_target="tpu_custom_call" | custom-call | flops 1358954496 | bytes 6071808 | tf_op jit(solution)/shard_map/pallas_call | solution.py:250
  26.1 1.9 %collective-permute-start.4 = (bf16[16,224,128]{2,1,0:T(8,128)(2,1)S(1)}, bf16[16,224,128]{2,1,0:T(8,128)(2,1)S(1)}, u32[]{:S(2)}, u32[]{:S(2)}) collective-permute-start(bf16[16,224,128]{2,1,0:T(8,128)(2,1)S(1)} %get-tuple-element.54), channel_id=1, source_target_pairs={{0,1},{1,0},{2,3},{3,2},{4,5},{5,4},{6,7},{7,6},{8,9},{9,8},{10,11... | collective-permute-start | bytes 2752520 | tf_op jit(solution)/shard_map/ppermute | solution.py:297
  28.0 1.7 %shard_map.128 = (f32[512,192]{1,0:T(8,128)S(1)}, f32[2,64,192]{2,1,0:T(8,128)S(1)}, bf16[10,192]{1,0:T(8,128)(2,1)S(1)}, bf16[10,192]{1,0:T(8,128)(2,1)S(1)}) custom-call(bf16[512,512]{1,0:T(8,128)(2,1)S(1)} %get-tuple-element.52.grad_gates, bf16[3,576,512]{2,1,0:T(8,128)(2,1)S(1)} %bitcast.5), custom_call_target="tpu_custom_call" | custom-call | flops 905969664 | bytes 2792960 | tf_op jit(solution)/shard_map/pallas_call | solution.py:250
  29.7 0.7 collective-permute-done.4.received
  30.4 1.6 %shard_map.129 = bf16[16,224,128]{2,1,0:T(8,128)(2,1)} custom-call(bf16[640,576]{1,0:T(8,128)(2,1)S(1)} %get-tuple-element.51.taps, bf16[512,512]{1,0:T(8,128)(2,1)S(1)} %get-tuple-element.52.grad_gates, f32[8,512]{1,0:T(8,128)S(1)} %get-tuple-element.53.sums, bf16[16,224,128]{2,1,0:T(8,128)(2,1)S(1)} %collective-permute-done.4.received), custom_call_target="tpu_custom_call" | custom-call | flops 452984832 | bytes 3112960 | tf_op jit(solution)/shard_map/pallas_call | solution.py:250
  32.0 6.0 %all-to-all-start = ((bf16[16,224,128]{2,1,0:T(8,128)(2,1)}), bf16[16,224,128]{2,1,0:T(8,128)(2,1)S(1)}, u32[]{:S(2)}, u32[]{:S(2)}) async-start(bf16[16,224,128]{2,1,0:T(8,128)(2,1)} %shard_map.129), calls=%async_computation | async-start | bytes 1835008 | tf_op jit(solution)/shard_map/all_to_all | solution.py:318
  38.1 2.3 %collective-permute-start.6 = (bf16[10,192]{1,0:T(8,128)(2,1)S(1)}, bf16[10,192]{1,0:T(8,128)(2,1)S(1)}, u32[]{:S(2)}, u32[]{:S(2)}) collective-permute-start(bf16[10,192]{1,0:T(8,128)(2,1)S(1)} %get-tuple-element.106), channel_id=1, source_target_pairs={{0,1},{1,0},{2,3},{3,2},{4,5},{5,4},{6,7},{7,6},{8,9},{9,8},{10,11... | collective-permute-start | bytes 11528 | tf_op jit(solution)/shard_map/ppermute | solution.py:26
  40.4 3.4 %collective-permute-start.5 = (bf16[10,192]{1,0:T(8,128)(2,1)S(1)}, bf16[10,192]{1,0:T(8,128)(2,1)S(1)}, u32[]{:S(2)}, u32[]{:S(2)}) collective-permute-start(bf16[10,192]{1,0:T(8,128)(2,1)S(1)} %get-tuple-element.107), channel_id=1, source_target_pairs={{1,2},{2,1},{3,4},{4,3},{5,6},{6,5},{7,8},{8,7},{9,10},{10,9},{11,... | collective-permute-start | bytes 11528 | tf_op jit(solution)/shard_map/ppermute | solution.py:27
  43.9 0.0 collective-permute-done.6
  43.9 7.0 %collective-permute-done.5 = bf16[10,192]{1,0:T(8,128)(2,1)S(1)} collective-permute-done((bf16[10,192]{1,0:T(8,128)(2,1)S(1)}, bf16[10,192]{1,0:T(8,128)(2,1)S(1)}, u32[]{:S(2)}, u32[]{:S(2)}) %collective-permute-start.5) | collective-permute-done | bytes 3872 | tf_op jit(solution)/shard_map/ppermute | solution.py:27
  50.9 2.3 %all-to-all-done = bf16[16,224,128]{2,1,0:T(8,128)(2,1)S(1)} async-done(((bf16[16,224,128]{2,1,0:T(8,128)(2,1)}), bf16[16,224,128]{2,1,0:T(8,128)(2,1)S(1)}, u32[]{:S(2)}, u32[]{:S(2)}) %all-to-all-start) | async-done | bytes 917536 | tf_op jit(solution)/shard_map/all_to_all | solution.py:318
  53.2 0.1 reduce_sum.21
  53.4 25.4 %all_to_all.20 = bf16[16,14,128]{2,1,0:T(8,128)(2,1)S(1)} all-to-all(bf16[16,14,128]{2,1,0:T(8,128)(2,1)S(1)} %reshape.188), channel_id=1, replica_groups=mesh['z'=16,'xh'=2,'y'=4,'xl'=2,'core'=2] {'z'}, dimensions={0} | all-to-all | bytes 114688 | tf_op jit(solution)/shard_map/all_to_all | solution.py:322
  78.8 14.4 %all_to_all.21 = bf16[16,14,128]{2,1,0:T(8,128)(2,1)S(1)} all-to-all(bf16[16,14,128]{2,1,0:T(8,128)(2,1)S(1)} %broadcast_in_dim.6), channel_id=1, replica_groups=mesh['z'=16,'xh'=2,'y'=4,'xl'=2,'core'=2] {'z'}, dimensions={0} | all-to-all | bytes 114688 | tf_op jit(solution)/shard_map/all_to_all | solution.py:325
  93.3 1.0 broadcast_in_dim.15
  94.3 5.2 %all-to-all-start.3 = ((bf16[16,224,128]{2,1,0:T(8,128)(2,1)}), bf16[16,224,128]{2,1,0:T(8,128)(2,1)S(1)}, u32[]{:S(2)}, u32[]{:S(2)}) async-start(bf16[16,224,128]{2,1,0:T(8,128)(2,1)} %broadcast_in_dim.15), calls=%async_computation.3 | async-start | bytes 1835008 | tf_op jit(solution)/shard_map/all_to_all | solution.py:327
  99.6 4.8 %collective-permute-start.8 = (bf16[1,64,192]{2,1,0:T(8,128)(2,1)S(1)}, bf16[1,64,192]{2,1,0:T(8,128)(2,1)S(1)}, u32[]{:S(2)}, u32[]{:S(2)}) collective-permute-start(bf16[1,64,192]{2,1,0:T(8,128)(2,1)S(1)} %get-tuple-element.92), channel_id=1, source_target_pairs={{0,16},{16,0},{32,48},{48,32},{64,80},{80,64},{96,112},{112,96},{1... | collective-permute-start | bytes 73736 | tf_op jit(solution)/shard_map/ppermute | solution.py:26
  104.4 0.7 collective-permute-start.7
  105.0 5.5 %collective-permute-done.8 = bf16[1,64,192]{2,1,0:T(8,128)(2,1)S(1)} collective-permute-done((bf16[1,64,192]{2,1,0:T(8,128)(2,1)S(1)}, bf16[1,64,192]{2,1,0:T(8,128)(2,1)S(1)}, u32[]{:S(2)}, u32[]{:S(2)}) %collective-permute-start.8) | collective-permute-done | bytes 24608 | tf_op jit(solution)/shard_map/ppermute | solution.py:26
  110.5 0.0 collective-permute-done.7
  110.5 1.5 %all-to-all-done.3.slots = bf16[16,224,128]{2,1,0:T(8,128)(2,1)S(1)} async-done(((bf16[16,224,128]{2,1,0:T(8,128)(2,1)}), bf16[16,224,128]{2,1,0:T(8,128)(2,1)S(1)}, u32[]{:S(2)}, u32[]{:S(2)}) %all-to-all-start.3) | async-done | bytes 917536 | tf_op jit(solution)/shard_map/all_to_all | solution.py:327
  112.0 6.6 %collective-permute-start.9 = (bf16[16,224,128]{2,1,0:T(8,128)(2,1)S(1)}, bf16[16,224,128]{2,1,0:T(8,128)(2,1)S(1)}, u32[]{:S(2)}, u32[]{:S(2)}) collective-permute-start(bf16[16,224,128]{2,1,0:T(8,128)(2,1)S(1)} %all-to-all-done.3.slots), channel_id=1, source_target_pairs={{0,1},{1,0},{2,3},{3,2},{4,5},{5,4},{6,7},{7,6},{8,9},{9,8},{10,11... | collective-permute-start | bytes 2752520 | tf_op jit(solution)/shard_map/ppermute | solution.py:337
  118.6 1.1 shard_map.132
  119.7 0.8 shard_map.131
  120.5 0.2 collective-permute-done.9.slots
  120.7 1.6 %shard_map.133 = (bf16[1728,512]{1,0:T(8,128)(2,1)}, f32[1,512]{1,0:T(1,128)}) custom-call(f32[1,512]{1,0:T(1,128)S(1)} %get-tuple-element.80.own_bias, bf16[16,224,128]{2,1,0:T(8,128)(2,1)S(1)} %collective-permute-done.9.slots, bf16[1728,512]{1,0:T(8,128)(2,1)} %get-tuple-element.82.own_kernel_part), custom_call_target="tpu_custom_call", output_to_operand_aliasing={{0}: (2, {})} | custom-call | bytes 4460544 | tf_op jit(solution)/shard_map/pallas_call | solution.py:250
  (15 shorter events, 0.2 us)
Async XLA Ops:
  1.5 11.2 %collective-permute-start = (bf16[1,64,192]{2,1,0:T(8,128)(2,1)S(1)}, bf16[1,64,192]{2,1,0:T(8,128)(2,1)S(1)}, u32[]{:S(2)}, u32[]{:S(2)}) collective-permute-start(bf16[1,64,192]{2,1,0:T(8,128)(2,1)S(1)} %broadcast_select_fusion.7), channel_id=1, source_target_pairs={{16,32},{32,16},{48,64},{64,48},{80,96},{96,80},{112,128},{128,112... | collective-permute-start | bytes 73736 | tf_op jit(solution)/shard_map/ppermute | solution.py:27
  2.2 10.6 %collective-permute-start.1 = (bf16[1,64,192]{2,1,0:T(8,128)(2,1)S(1)}, bf16[1,64,192]{2,1,0:T(8,128)(2,1)S(1)}, u32[]{:S(2)}, u32[]{:S(2)}) collective-permute-start(bf16[1,64,192]{2,1,0:T(8,128)(2,1)S(1)} %get-tuple-element.85), channel_id=1, source_target_pairs={{0,16},{16,0},{32,48},{48,32},{64,80},{80,64},{96,112},{112,96},{1... | collective-permute-start | bytes 73736 | tf_op jit(solution)/shard_map/ppermute | solution.py:26
  12.5 10.9 %copy-start = (bf16[3,3,192,512]{3,2,1,0:T(8,128)(2,1)S(1)}, bf16[3,3,192,512]{3,2,1,0:T(8,128)(2,1)}, u32[]{:S(2)}) copy-start(bf16[3,3,192,512]{3,2,1,0:T(8,128)(2,1)} %param.10) | copy-start | bytes 5308420
  12.5 10.9 %copy-start.1 = (f32[8,64,128]{2,1,0:T(8,128)S(1)}, f32[8,64,128]{2,1,0:T(8,128)}, u32[]{:S(2)}) copy-start(f32[8,64,128]{2,1,0:T(8,128)} %cell_prev.1) | copy-start | bytes 786436
  12.5 10.9 %copy-start.2 = (f32[8,64,128]{2,1,0:T(8,128)S(1)}, f32[8,64,128]{2,1,0:T(8,128)}, u32[]{:S(2)}) copy-start(f32[8,64,128]{2,1,0:T(8,128)} %cell_cot.1) | copy-start | bytes 786436
  12.5 10.9 %copy-start.3 = (bf16[8,64,128]{2,1,0:T(8,128)(2,1)S(1)}, bf16[8,64,128]{2,1,0:T(8,128)(2,1)}, u32[]{:S(2)}) copy-start(bf16[8,64,128]{2,1,0:T(8,128)(2,1)} %hidden_cot.1) | copy-start | bytes 393220
  12.5 10.9 %copy-start.4 = (f32[512]{0:T(512)S(1)}, f32[512]{0:T(512)}, u32[]{:S(2)}) copy-start(f32[512]{0:T(512)} %param.11) | copy-start | bytes 6148
  12.8 7.5 %collective-permute-start.3 = (bf16[10,1,192]{2,1,0:T(2,128)(2,1)S(1)}, bf16[10,1,192]{2,1,0:T(2,128)(2,1)S(1)}, u32[]{:S(2)}, u32[]{:S(2)}) collective-permute-start(bf16[10,1,192]{2,1,0:T(2,128)(2,1)S(1)} %get-tuple-element.102), channel_id=1, source_target_pairs={{0,1},{1,0},{2,3},{3,2},{4,5},{5,4},{6,7},{7,6},{8,9},{9,8},{10,11... | collective-permute-start | bytes 11528 | tf_op jit(solution)/shard_map/ppermute | solution.py:26
  18.4 5.0 %collective-permute-start.2 = (bf16[10,1,192]{2,1,0:T(2,128)(2,1)S(1)}, bf16[10,1,192]{2,1,0:T(2,128)(2,1)S(1)}, u32[]{:S(2)}, u32[]{:S(2)}) collective-permute-start(bf16[10,1,192]{2,1,0:T(2,128)(2,1)S(1)} %get-tuple-element.103), channel_id=1, source_target_pairs={{1,2},{2,1},{3,4},{4,3},{5,6},{6,5},{7,8},{8,7},{9,10},{10,9},{11,... | collective-permute-start | bytes 11528 | tf_op jit(solution)/shard_map/ppermute | solution.py:27
  26.1 4.4 %collective-permute-start.4 = (bf16[16,224,128]{2,1,0:T(8,128)(2,1)S(1)}, bf16[16,224,128]{2,1,0:T(8,128)(2,1)S(1)}, u32[]{:S(2)}, u32[]{:S(2)}) collective-permute-start(bf16[16,224,128]{2,1,0:T(8,128)(2,1)S(1)} %get-tuple-element.54), channel_id=1, source_target_pairs={{0,1},{1,0},{2,3},{3,2},{4,5},{5,4},{6,7},{7,6},{8,9},{9,8},{10,11... | collective-permute-start | bytes 2752520 | tf_op jit(solution)/shard_map/ppermute | solution.py:297
  32.0 21.2 %all-to-all-start = ((bf16[16,224,128]{2,1,0:T(8,128)(2,1)}), bf16[16,224,128]{2,1,0:T(8,128)(2,1)S(1)}, u32[]{:S(2)}, u32[]{:S(2)}) async-start(bf16[16,224,128]{2,1,0:T(8,128)(2,1)} %shard_map.129), calls=%async_computation | async-start | bytes 1835008 | tf_op jit(solution)/shard_map/all_to_all | solution.py:318
  38.1 5.8 %collective-permute-start.6 = (bf16[10,192]{1,0:T(8,128)(2,1)S(1)}, bf16[10,192]{1,0:T(8,128)(2,1)S(1)}, u32[]{:S(2)}, u32[]{:S(2)}) collective-permute-start(bf16[10,192]{1,0:T(8,128)(2,1)S(1)} %get-tuple-element.106), channel_id=1, source_target_pairs={{0,1},{1,0},{2,3},{3,2},{4,5},{5,4},{6,7},{7,6},{8,9},{9,8},{10,11... | collective-permute-start | bytes 11528 | tf_op jit(solution)/shard_map/ppermute | solution.py:26
  40.4 10.5 %collective-permute-start.5 = (bf16[10,192]{1,0:T(8,128)(2,1)S(1)}, bf16[10,192]{1,0:T(8,128)(2,1)S(1)}, u32[]{:S(2)}, u32[]{:S(2)}) collective-permute-start(bf16[10,192]{1,0:T(8,128)(2,1)S(1)} %get-tuple-element.107), channel_id=1, source_target_pairs={{1,2},{2,1},{3,4},{4,3},{5,6},{6,5},{7,8},{8,7},{9,10},{10,9},{11,... | collective-permute-start | bytes 11528 | tf_op jit(solution)/shard_map/ppermute | solution.py:27
  94.3 17.7 %all-to-all-start.3 = ((bf16[16,224,128]{2,1,0:T(8,128)(2,1)}), bf16[16,224,128]{2,1,0:T(8,128)(2,1)S(1)}, u32[]{:S(2)}, u32[]{:S(2)}) async-start(bf16[16,224,128]{2,1,0:T(8,128)(2,1)} %broadcast_in_dim.15), calls=%async_computation.3 | async-start | bytes 1835008 | tf_op jit(solution)/shard_map/all_to_all | solution.py:327
  99.6 10.9 %collective-permute-start.8 = (bf16[1,64,192]{2,1,0:T(8,128)(2,1)S(1)}, bf16[1,64,192]{2,1,0:T(8,128)(2,1)S(1)}, u32[]{:S(2)}, u32[]{:S(2)}) collective-permute-start(bf16[1,64,192]{2,1,0:T(8,128)(2,1)S(1)} %get-tuple-element.92), channel_id=1, source_target_pairs={{0,16},{16,0},{32,48},{48,32},{64,80},{80,64},{96,112},{112,96},{1... | collective-permute-start | bytes 73736 | tf_op jit(solution)/shard_map/ppermute | solution.py:26
  104.4 6.1 %collective-permute-start.7 = (bf16[1,64,192]{2,1,0:T(8,128)(2,1)S(1)}, bf16[1,64,192]{2,1,0:T(8,128)(2,1)S(1)}, u32[]{:S(2)}, u32[]{:S(2)}) collective-permute-start(bf16[1,64,192]{2,1,0:T(8,128)(2,1)S(1)} %get-tuple-element.93), channel_id=1, source_target_pairs={{16,32},{32,16},{48,64},{64,48},{80,96},{96,80},{112,128},{128,112... | collective-permute-start | bytes 73736 | tf_op jit(solution)/shard_map/ppermute | solution.py:27
  112.0 8.7 %collective-permute-start.9 = (bf16[16,224,128]{2,1,0:T(8,128)(2,1)S(1)}, bf16[16,224,128]{2,1,0:T(8,128)(2,1)S(1)}, u32[]{:S(2)}, u32[]{:S(2)}) collective-permute-start(bf16[16,224,128]{2,1,0:T(8,128)(2,1)S(1)} %all-to-all-done.3.slots), channel_id=1, source_target_pairs={{0,1},{1,0},{2,3},{3,2},{4,5},{5,4},{6,7},{7,6},{8,9},{9,8},{10,11... | collective-permute-start | bytes 2752520 | tf_op jit(solution)/shard_map/ppermute | solution.py:337

commit v6 on v5

--- a/solution.py
+++ b/solution.py
@@ -81,7 +81,8 @@
 
 def cell_kernel(
     own_taps, low, high, left, right, kernel, cell_prev, hidden_cot, cell_cot, bias,
-    hidden_new, cell_new, grad_cell, grad_gates, taps, sums, send, gates,
+    hidden_out, cell_out, grad_cell_out, grad_gates, taps, sums, send,
+    gates, hidden_new, cell_new, grad_cell, sent,
 ):
     for r, halo in ((0, low), (TR + 1, high)):
         row = halo[0].astype(F32)
@@ -126,6 +127,14 @@
         grad_gates[rows, :] = rounded
         wide = rounded.astype(F32).reshape(TC // 8, 8, GATES)
         bias_sum = bias_sum + jnp.sum(wide, axis=0)
+    copies = [
+        pltpu.make_async_copy(source, target, sent.at[i])
+        for i, (source, target) in enumerate(
+            ((hidden_new, hidden_out), (cell_new, cell_out), (grad_cell, grad_cell_out))
+        )
+    ]
+    for copy in copies:
+        copy.start()
     sums[...] = jnp.broadcast_to(jnp.sum(bias_sum, axis=0, keepdims=True), (8, GATES))
     columns = pl.ds(pl.multiple_of((1 - lax.axis_index("core")) * 256, 256), 256)
 
@@ -133,6 +142,8 @@
         send[slot, top:end, :] = block.astype(BF16)
 
     half_products(taps, grad_gates[:, columns], sums[:, columns], store)
+    for copy in copies:
+        copy.wait()
 
 
 def own_kernel(taps, grad_gates, sums, received, result, total, sent):
@@ -151,64 +162,82 @@
         copy(slot).wait()
 
 
-def input_kernel(grad_gates, kernel, inner, edges, to_left, to_right, spread):
+def input_kernel(grad_gates, kernel, inner, to_above, to_below, lefts, rights, spread):
     spread[...] = jnp.zeros_like(spread)
     for a in range(3):
         spread[a * TC : a * TC + CELLS, :] += lax.dot_general(
             grad_gates[...], kernel[a], (((1,), (1,)), ((), ())), preferred_element_type=F32
         )
-    lefts, rights = [], []
+    sides = []
     for r in range(TR + 2):
         rows = spread[r * TC : (r + 1) * TC, :]
         lower, middle, upper = rows[:, :ZCH], rows[:, ZCH : 2 * ZCH], rows[:, 2 * ZCH :]
         _, from_lower = shifted(lower, 0.0, 0.0)
         from_upper, _ = shifted(upper, 0.0, 0.0)
         total = middle + from_lower + from_upper
-        lefts.append(lower[:1])
-        rights.append(upper[TC - 1 :])
-        if r == 0:
-            edges[0] = total
-        elif r == TR + 1:
-            edges[1] = total
+        if 0 < r < TR + 1:
+            inner[(r - 1) * TC : r * TC, :] = total
+            sides.append((lower[:1], upper[TC - 1 :]))
         else:
-            inner[(r - 1) * TC : r * TC, :] = total
-    to_left[...] = jnp.concatenate(lefts, axis=0).astype(BF16)
-    to_right[...] = jnp.concatenate(rights, axis=0).astype(BF16)
-
-
-def with_columns(row, before, after):
-    place = lax.broadcasted_iota(jnp.int32, row.shape, 0)
-    return row + jnp.where(place == 0, before, 0.0) + jnp.where(place == TC - 1, after, 0.0)
-
-
-def edge_kernel(edges, from_left, from_right, to_above, to_below):
-    before, after = from_left[...].astype(F32), from_right[...].astype(F32)
-    to_above[0] = with_columns(edges[0], before[:1], after[:1]).astype(BF16)
-    to_below[0] = with_columns(edges[1], before[TR + 1 :], after[TR + 1 :]).astype(BF16)
+            target = to_above if r == 0 else to_below
+            corners = [lower[:1], upper[TC - 1 :], jnp.zeros((14, ZCH), F32)]
+            target[0:TC, :] = total.astype(BF16)
+            target[TC : TC + 16, :] = jnp.concatenate(corners, axis=0).astype(BF16)
+    lefts[...] = jnp.concatenate([left for left, _ in sides], axis=0)
+    rights[...] = jnp.concatenate([right for _, right in sides], axis=0)
+
+
+def side_kernel(lefts, rights, from_above, from_below, to_left, to_right):
+    place = lax.broadcasted_iota(jnp.int32, (TR, ZCH), 0)
+    above = from_above[TC : TC + 16, :].astype(F32)
+    below = from_below[TC : TC + 16, :].astype(F32)
+    for i, own, target in ((0, lefts, to_left), (1, rights, to_right)):
+        extra = jnp.where(place == 0, above[i : i + 1], 0.0)
+        extra += jnp.where(place == TR - 1, below[i : i + 1], 0.0)
+        target[...] = (own[...] + extra).astype(BF16)
 
 
 def sum_kernel(
-    inner, from_left, from_right, from_above, from_below, grad_features, grad_hidden
+    inner, from_above, from_below, from_left, from_right, grad_features, grad_hidden
 ):
     before, after = from_left[...].astype(F32), from_right[...].astype(F32)
+    place = lax.broadcasted_iota(jnp.int32, (TC, ZCH), 0)
     for r in range(TR):
         row = inner[r * TC : (r + 1) * TC, :]
-        row = with_columns(row, before[r + 1 : r + 2], after[r + 1 : r + 2])
+        row += jnp.where(place == 0, before[r : r + 1], 0.0)
+        row += jnp.where(place == TC - 1, after[r : r + 1], 0.0)
         if r == 0:
-            row = row + from_above[0].astype(F32)
+            row += from_above[0:TC, :].astype(F32)
         if r == TR - 1:
-            row = row + from_below[0].astype(F32)
+            row += from_below[0:TC, :].astype(F32)
         grad_features[r] = row[:, :FEAT].astype(BF16)
         grad_hidden[r] = row[:, FEAT:].astype(BF16)
 
 
-def place_half(slots, place, grad_kernel, grad_bias, last_slots, sems):
+def plane_sum_kernel(parts, total):
+    result = parts[0].astype(F32)
+    for i in range(1, parts.shape[0]):
+        result += parts[i].astype(F32)
+    total[...] = result.astype(BF16)
+
+
+def copies_kernel(part, copies, sems):
+    moves = [
+        pltpu.make_async_copy(part, copies.at[i], sems.at[i]) for i in range(copies.shape[0])
+    ]
+    for move in moves:
+        move.start()
+    for move in moves:
+        move.wait()
+
+
+def place_half(slots, place, grad_kernel, last_slots, sems):
     last = 3 * TAPS - (GROUPS - 1) * SLOT
-    copies = []
+    heads, copies = [], []
     for j in range(2):
         columns = pl.ds(pl.multiple_of(place * 256 + j * 128, 128), 128)
         slot = j * GROUPS + GROUPS - 1
-        copies.append(
+        heads.append(
             pltpu.make_async_copy(
                 slots.at[slot, last : last + 16, :], last_slots.at[j], sems.at[2 * GROUPS + j]
             )
@@ -222,25 +251,35 @@
                     sems.at[j * GROUPS + i],
                 )
             )
-    for copy in copies:
+    for copy in heads + copies:
         copy.start()
+    for copy in heads:
+        copy.wait()
+    return [last_slots[j].astype(F32)[0:1] for j in range(2)], copies
+
+
+def join_own_kernel(slots, grad_kernel, own_bias, last_slots, sems):
+    core = lax.axis_index("core")
+    rows, copies = place_half(slots, core, grad_kernel, last_slots, sems)
+    own_bias[...] = jnp.zeros_like(own_bias)
+    for j in range(2):
+        own_bias[:, pl.ds(pl.multiple_of(core * 256 + j * 128, 128), 128)] = rows[j]
     for copy in copies:
         copy.wait()
+
+
+def join_other_kernel(
+    own_bias, slots, own_kernel_part, grad_kernel, grad_bias, last_slots, bias, sems
+):
+    place = 1 - lax.axis_index("core")
+    rows, copies = place_half(slots, place, grad_kernel, last_slots, sems)
+    bias[...] = own_bias[...]
     for j in range(2):
-        columns = pl.ds(pl.multiple_of(place * 256 + j * 128, 128), 128)
-        grad_bias[:, columns] = last_slots[j].astype(F32)[0:1]
-
-
-def join_own_kernel(slots, grad_kernel, grad_bias, last_slots, sems):
-    grad_bias[...] = jnp.zeros_like(grad_bias)
-    place_half(slots, lax.axis_index("core"), grad_kernel, grad_bias, last_slots, sems)
-
-
-def join_other_kernel(
-    own_bias, slots, own_kernel_part, grad_kernel, grad_bias, last_slots, sems
-):
-    grad_bias[...] = own_bias[...]
-    place_half(slots, 1 - lax.axis_index("core"), grad_kernel, grad_bias, last_slots, sems)
+        bias[:, pl.ds(pl.multiple_of(place * 256 + j * 128, 128), 128)] = rows[j]
+    copies.append(pltpu.make_async_copy(bias, grad_bias, sems.at[2 * GROUPS + 2]))
+    copies[-1].start()
+    for copy in copies:
+        copy.wait()
 
 
 def call(body, outs, *args, scratch=(), flops=0, far=0, far_outs=0, aliases=()):
@@ -291,61 +330,76 @@
         ),
         own_taps, low, high, left, right, weights, cell_prev, hidden_cot, cell_cot,
         bias.reshape(1, GATES),
-        scratch=[pltpu.VMEM((CELLS, GATES), F32)],
+        scratch=[
+            pltpu.VMEM((CELLS, GATES), F32),
+            pltpu.VMEM((TR, TC, CH), BF16),
+            pltpu.VMEM((TR, TC, CH), F32),
+            pltpu.VMEM((TR, TC, CH), F32),
+            pltpu.SemaphoreType.DMA((3,)),
+        ],
         flops=work + work // 2,
+        far_outs=3,
     )
     received = lax.ppermute(send, "core", swap)
-    inner, edges, to_left, to_right = call(
+    inner, to_above, to_below, lefts, rights = call(
         input_kernel,
         (
             shape((CELLS, ZCH), F32),
-            shape((2, TC, ZCH), F32),
-            shape((TR + 2, ZCH), BF16),
-            shape((TR + 2, ZCH), BF16),
+            shape((TC + 16, ZCH), BF16),
+            shape((TC + 16, ZCH), BF16),
+            shape((TR, ZCH), F32),
+            shape((TR, ZCH), F32),
         ),
         grad_gates, weights,
         scratch=[pltpu.VMEM(((TR + 2) * TC, TAPS), F32)],
         flops=work,
     )
-    received, to_left, to_right = lax.optimization_barrier((received, to_left, to_right))
+    received, to_above, to_below = lax.optimization_barrier((received, to_above, to_below))
     (half,) = call(
         own_kernel, (shape((plane, SLOT, 128), BF16),), taps, grad_gates, sums, received,
         scratch=[pltpu.VMEM((plane, SLOT, 128), BF16), pltpu.SemaphoreType.DMA((plane,))],
         flops=work // 2,
         far_outs=1,
     )
-    half, to_left, to_right = lax.optimization_barrier((half, to_left, to_right))
+    half, to_above, to_below = lax.optimization_barrier((half, to_above, to_below))
     part = lax.all_to_all(half, PLANE, 0, 0, tiled=True)
-    from_left, from_right = to_neighbours(COLS, to_right, to_left)
-    part, from_left, from_right = lax.optimization_barrier((part, from_left, from_right))
-    part = jnp.sum(part.astype(F32), axis=0).astype(BF16)
+    from_above, from_below = to_neighbours(ROWS, to_below, to_above)
+    part, from_above, from_below = lax.optimization_barrier((part, from_above, from_below))
+    (part,) = call(plane_sum_kernel, (shape((SLOT, 128), BF16),), part)
     part = lax.all_to_all(part.reshape(depth, SLOT // depth, 128), "z", 0, 0, tiled=True)
     scale = 1.0 / (TR * lax.axis_size(ROWS))
     part = (jnp.sum(part.astype(F32), axis=0) * scale).astype(BF16)
     part = lax.all_to_all(copies_of(part, depth), "z", 0, 0, tiled=True).reshape(SLOT, 128)
-    copies, edges = lax.optimization_barrier((copies_of(part, plane), edges))
+    (copies,) = call(
+        copies_kernel, (shape((plane, SLOT, 128), BF16),), part,
+        scratch=[pltpu.SemaphoreType.DMA((plane,))],
+        far_outs=1,
+    )
+    copies, lefts = lax.optimization_barrier((copies, lefts))
     half = lax.all_to_all(copies, PLANE, 0, 0, tiled=True)
-    row = shape((1, TC, ZCH), BF16)
-    to_above, to_below = call(edge_kernel, (row, row), edges, from_left, from_right)
-    from_above, from_below = to_neighbours(ROWS, to_below, to_above)
-    half, from_above, from_below = lax.optimization_barrier((half, from_above, from_below))
+    side = shape((TR, ZCH), BF16)
+    to_left, to_right = call(side_kernel, (side, side), lefts, rights, from_above, from_below)
+    from_left, from_right = to_neighbours(COLS, to_right, to_left)
+    half, from_left, from_right = lax.optimization_barrier((half, from_left, from_right))
     grad_features, grad_hidden = call(
         sum_kernel,
         (shape((TR, TC, FEAT), BF16), shape((TR, TC, CH), BF16)),
-        inner, from_left, from_right, from_above, from_below,
+        inner, from_above, from_below, from_left, from_right,
     )
     other = lax.ppermute(half, "core", swap)
     outs = (shape((3 * TAPS, GATES), BF16), shape((1, GATES), F32))
-    scratch = [pltpu.VMEM((2, 16, 128), BF16), pltpu.SemaphoreType.DMA((2 * GROUPS + 2,))]
+    tails = pltpu.VMEM((2, 16, 128), BF16)
+    sems = pltpu.SemaphoreType.DMA((2 * GROUPS + 3,))
     grad_kernel, own_bias = call(
-        join_own_kernel, outs, half, scratch=scratch, far=1, far_outs=1
+        join_own_kernel, outs, half, scratch=[tails, sems], far=1, far_outs=1
     )
     other, grad_features, grad_hidden = lax.optimization_barrier(
         (other, grad_features, grad_hidden)
     )
     grad_kernel, grad_bias = call(
         join_other_kernel, outs, own_bias, other, grad_kernel,
-        scratch=scratch, far=2, far_outs=1, aliases={2: 0},
+        scratch=[tails, pltpu.VMEM((1, GATES), F32), sems],
+        far=2, far_outs=2, aliases={2: 0},
     )
     return (
         hidden_new,

time: 123 us -> 122 us (level)
  waiting for transfers between devices: 20.3 us -> 17.6 us
  starting transfers between devices: 47.4 us -> 49.6 us
    ppermute x4, starting transfers between devices: 21 us -> 24.7 us  [to_neighbours(): near = lax.ppermute(jnp.where(even, last, first), axes, inner)]
    ppermute x4, waiting for transfers between devices: 10.1 us -> 6.96 us  [to_neighbours(): far = lax.ppermute(jnp.where(even, first, last), axes, outer)]
    ppermute x4, waiting for transfers between devices: 5.46 us -> 8.49 us  [to_neighbours(): near = lax.ppermute(jnp.where(even, last, first), axes, inner)]
    all_to_all x1, waiting for transfers between devices: 1.47 us -> 0.01 us  [local(): half = lax.all_to_all(copies, PLANE, 0, 0, tiled=True)]
    pallas_call x8 -> x10, Pallas kernels: 9.55 us -> 10.2 us  [call(): pl.pallas_call(body, out_shape=outs, in_specs=[whole] * (len(args) - far)...]
  transfers between devices with their start and end apart: 12 -> 12, of which waited for: 7 -> 6; matrix products, arithmetic and copies ran while one was open for 2% -> 2% of each run, Pallas kernels for 3% -> 3%
where the time goes in v6:
time: 122 us
  starting transfers between devices  49.6 us (41%)
  blocking collectives  40.2 us (33%)
  waiting for transfers between devices  17.6 us (14%)
  Pallas kernels  10.2 us (8%)
  other arithmetic  2.99 us (2%)
    all_to_all x1, blocking collectives, local(): lax.all_to_all(part.reshape(depth, SLOT // depth, 128), 'z', 0, 0, tiled=...  25.8 us
    ppermute x4, starting transfers between devices, to_neighbours(): near = lax.ppermute(jnp.where(even, last, first), axes, inner)  24.7 us
    all_to_all x1, blocking collectives, local(): lax.all_to_all(copies_of(part, depth), 'z', 0, 0, tiled=True)  14.4 us
    pallas_call x10, Pallas kernels, call(): pl.pallas_call(body, out_shape=outs, in_specs=[whole] * (len(args) - far)...  10.2 us
    ppermute x4, waiting for transfers between devices, to_neighbours(): near = lax.ppermute(jnp.where(even, last, first), axes, inner)  8.49 us
    ppermute x4, waiting for transfers between devices, to_neighbours(): far = lax.ppermute(jnp.where(even, first, last), axes, outer)  6.96 us
    ppermute x4, starting transfers between devices, to_neighbours(): far = lax.ppermute(jnp.where(even, first, last), axes, outer)  6.57 us
    all_to_all x1, starting transfers between devices, local(): part = lax.all_to_all(half, PLANE, 0, 0, tiled=True)  6.03 us
  transfers between devices with their start and end apart: 12, of which 6 were waited for; matrix products, arithmetic and copies ran while one was open for 2% of the time, Pallas kernels for 3%

profile of v6, /device:TPU:1, one launch (start us, length us, event | category | flops | bytes accessed | tf_op | source)
XLA Modules:
  0.0 121.7 jit_solution(3314204222949072191)
XLA Ops:
  0.6 0.9 broadcast_select_fusion.6
  1.5 0.7 collective-permute-start
  2.2 8.3 %collective-permute-start.1 = (bf16[1,64,192]{2,1,0:T(8,128)(2,1)S(1)}, bf16[1,64,192]{2,1,0:T(8,128)(2,1)S(1)}, u32[]{:S(2)}, u32[]{:S(2)}) collective-permute-start(bf16[1,64,192]{2,1,0:T(8,128)(2,1)S(1)} %get-tuple-element.87), channel_id=1, source_target_pairs={{0,16},{16,0},{32,48},{48,32},{64,80},{80,64},{96,112},{112,96},{1... | collective-permute-start | bytes 73736 | tf_op jit(solution)/shard_map/ppermute | solution.py:26
  10.5 0.9 fusion.2
  11.4 1.1 pad_maximum_fusion.stacked
  12.5 0.0 copy-start
  12.5 0.0 copy-start.1
  12.5 0.0 copy-start.2
  12.5 0.0 copy-start.3
  12.5 0.0 copy-start.4
  12.6 0.2 shard_map.126.own_taps
  12.7 0.0 collective-permute-done
  12.7 0.0 collective-permute-done.1
  12.8 5.5 %collective-permute-start.3 = (bf16[10,1,192]{2,1,0:T(2,128)(2,1)S(1)}, bf16[10,1,192]{2,1,0:T(2,128)(2,1)S(1)}, u32[]{:S(2)}, u32[]{:S(2)}) collective-permute-start(bf16[10,1,192]{2,1,0:T(2,128)(2,1)S(1)} %get-tuple-element.104), channel_id=1, source_target_pairs={{0,1},{1,0},{2,3},{3,2},{4,5},{5,4},{6,7},{7,6},{8,9},{9,8},{10,11... | collective-permute-start | bytes 11528 | tf_op jit(solution)/shard_map/ppermute | solution.py:26
  18.4 1.9 %collective-permute-start.2 = (bf16[10,1,192]{2,1,0:T(2,128)(2,1)S(1)}, bf16[10,1,192]{2,1,0:T(2,128)(2,1)S(1)}, u32[]{:S(2)}, u32[]{:S(2)}) collective-permute-start(bf16[10,1,192]{2,1,0:T(2,128)(2,1)S(1)} %get-tuple-element.105), channel_id=1, source_target_pairs={{1,2},{2,1},{3,4},{4,3},{5,6},{6,5},{7,8},{8,7},{9,10},{10,9},{11,... | collective-permute-start | bytes 11528 | tf_op jit(solution)/shard_map/ppermute | solution.py:27
  20.3 0.0 collective-permute-done.3
  20.3 3.1 %collective-permute-done.2 = bf16[10,1,192]{2,1,0:T(2,128)(2,1)S(1)} collective-permute-done((bf16[10,1,192]{2,1,0:T(2,128)(2,1)S(1)}, bf16[10,1,192]{2,1,0:T(2,128)(2,1)S(1)}, u32[]{:S(2)}, u32[]{:S(2)}) %collective-permute-start.2) | collective-permute-done | bytes 3872 | tf_op jit(solution)/shard_map/ppermute | solution.py:27
  23.4 0.0 copy-done
  23.4 0.0 copy-done.1
  23.4 0.0 copy-done.2
  23.4 0.0 copy-done.3
  23.4 0.0 copy-done.4
  23.5 2.6 %shard_map.127 = (bf16[8,64,128]{2,1,0:T(8,128)(2,1)}, f32[8,64,128]{2,1,0:T(8,128)}, f32[8,64,128]{2,1,0:T(8,128)}, bf16[512,512]{1,0:T(8,128)(2,1)S(1)}, bf16[...) custom-call(bf16[640,576]{1,0:T(8,128)(2,1)S(1)} %shard_map.126.own_taps, ...), custom_call_target="tpu_custom_call" | custom-call | flops 1358954496 | bytes 6071808 | tf_op jit(solution)/shard_map/pallas_call | solution.py:289
  26.1 1.9 %collective-permute-start.4 = (bf16[16,224,128]{2,1,0:T(8,128)(2,1)S(1)}, bf16[16,224,128]{2,1,0:T(8,128)(2,1)S(1)}, u32[]{:S(2)}, u32[]{:S(2)}) collective-permute-start(bf16[16,224,128]{2,1,0:T(8,128)(2,1)S(1)} %get-tuple-element.55), channel_id=1, source_target_pairs={{0,1},{1,0},{2,3},{3,2},{4,5},{5,4},{6,7},{7,6},{8,9},{9,8},{10,11... | collective-permute-start | bytes 2752520 | tf_op jit(solution)/shard_map/ppermute | solution.py:343
  28.0 1.7 %shard_map.128 = (f32[512,192]{1,0:T(8,128)S(1)}, bf16[80,192]{1,0:T(8,128)(2,1)S(1)}, bf16[80,192]{1,0:T(8,128)(2,1)S(1)}, f32[8,192]{1,0:T(8,128)S(1)}, f32[8,192]{1,0:T(8,128)S(1)}) custom-call(bf16[512,512]{1,0:T(8,128)(2,1)S(1)} %get-tuple-element.53.grad_gates, bf16[3,576,512]{2,1,0:T(8,128)(2,1)S(1)} %bitcast.5), custom_call_target="tpu_custom_call" | custom-call | flops 905969664 | bytes 2760704 | tf_op jit(solution)/shard_map/pallas_call | solution.py:289
  29.7 0.8 collective-permute-done.4.received
  30.5 1.6 %shard_map.129 = bf16[16,224,128]{2,1,0:T(8,128)(2,1)} custom-call(bf16[640,576]{1,0:T(8,128)(2,1)S(1)} %get-tuple-element.52.taps, bf16[512,512]{1,0:T(8,128)(2,1)S(1)} %get-tuple-element.53.grad_gates, f32[8,512]{1,0:T(8,128)S(1)} %get-tuple-element.54.sums, bf16[16,224,128]{2,1,0:T(8,128)(2,1)S(1)} %collective-permute-done.4.received), custom_call_target="tpu_custom_call" | custom-call | flops 452984832 | bytes 3112960 | tf_op jit(solution)/shard_map/pallas_call | solution.py:289
  32.1 6.0 %all-to-all-start = ((bf16[16,224,128]{2,1,0:T(8,128)(2,1)}), bf16[16,224,128]{2,1,0:T(8,128)(2,1)S(1)}, u32[]{:S(2)}, u32[]{:S(2)}) async-start(bf16[16,224,128]{2,1,0:T(8,128)(2,1)} %shard_map.129), calls=%async_computation | async-start | bytes 1835008 | tf_op jit(solution)/shard_map/all_to_all | solution.py:365
  38.1 4.8 %collective-permute-start.6 = (bf16[80,192]{1,0:T(8,128)(2,1)S(1)}, bf16[80,192]{1,0:T(8,128)(2,1)S(1)}, u32[]{:S(2)}, u32[]{:S(2)}) collective-permute-start(bf16[80,192]{1,0:T(8,128)(2,1)S(1)} %get-tuple-element.94), channel_id=1, source_target_pairs={{0,16},{16,0},{32,48},{48,32},{64,80},{80,64},{96,112},{112,96},{1... | collective-permute-start | bytes 92168 | tf_op jit(solution)/shard_map/ppermute | solution.py:26
  42.9 0.7 collective-permute-start.5
  43.6 8.5 %collective-permute-done.6 = bf16[80,192]{1,0:T(8,128)(2,1)S(1)} collective-permute-done((bf16[80,192]{1,0:T(8,128)(2,1)S(1)}, bf16[80,192]{1,0:T(8,128)(2,1)S(1)}, u32[]{:S(2)}, u32[]{:S(2)}) %collective-permute-start.6) | collective-permute-done | bytes 30752 | tf_op jit(solution)/shard_map/ppermute | solution.py:26
  52.1 0.0 collective-permute-done.5
  52.1 1.2 %all-to-all-done.parts = bf16[16,224,128]{2,1,0:T(8,128)(2,1)S(1)} async-done(((bf16[16,224,128]{2,1,0:T(8,128)(2,1)}), bf16[16,224,128]{2,1,0:T(8,128)(2,1)S(1)}, u32[]{:S(2)}, u32[]{:S(2)}) %all-to-all-start) | async-done | bytes 917536 | tf_op jit(solution)/shard_map/all_to_all | solution.py:365
  53.3 0.1 shard_map.130
  53.4 25.8 %all_to_all.20 = bf16[16,14,128]{2,1,0:T(8,128)(2,1)S(1)} all-to-all(bf16[16,14,128]{2,1,0:T(8,128)(2,1)S(1)} %reshape.190), channel_id=1, replica_groups=mesh['z'=16,'xh'=2,'y'=4,'xl'=2,'core'=2] {'z'}, dimensions={0} | all-to-all | bytes 114688 | tf_op jit(solution)/shard_map/all_to_all | solution.py:369
  79.3 14.4 %all_to_all.21 = bf16[16,14,128]{2,1,0:T(8,128)(2,1)S(1)} all-to-all(bf16[16,14,128]{2,1,0:T(8,128)(2,1)S(1)} %broadcast_in_dim.2), channel_id=1, replica_groups=mesh['z'=16,'xh'=2,'y'=4,'xl'=2,'core'=2] {'z'}, dimensions={0} | all-to-all | bytes 114688 | tf_op jit(solution)/shard_map/all_to_all | solution.py:372
  93.8 1.0 shard_map.131
  94.8 4.6 %all-to-all-start.3 = ((bf16[16,224,128]{2,1,0:T(8,128)(2,1)}), bf16[16,224,128]{2,1,0:T(8,128)(2,1)S(1)}, u32[]{:S(2)}, u32[]{:S(2)}) async-start(bf16[16,224,128]{2,1,0:T(8,128)(2,1)} %shard_map.131), calls=%async_computation.3 | async-start | bytes 1835008 | tf_op jit(solution)/shard_map/all_to_all | solution.py:379
  99.5 6.1 %collective-permute-start.8 = (bf16[8,192]{1,0:T(8,128)(2,1)S(1)}, bf16[8,192]{1,0:T(8,128)(2,1)S(1)}, u32[]{:S(2)}, u32[]{:S(2)}) collective-permute-start(bf16[8,192]{1,0:T(8,128)(2,1)S(1)} %get-tuple-element.108), channel_id=1, source_target_pairs={{0,1},{1,0},{2,3},{3,2},{4,5},{5,4},{6,7},{7,6},{8,9},{9,8},{10,11... | collective-permute-start | bytes 9224 | tf_op jit(solution)/shard_map/ppermute | solution.py:26
  105.5 3.3 %collective-permute-start.7 = (bf16[8,192]{1,0:T(8,128)(2,1)S(1)}, bf16[8,192]{1,0:T(8,128)(2,1)S(1)}, u32[]{:S(2)}, u32[]{:S(2)}) collective-permute-start(bf16[8,192]{1,0:T(8,128)(2,1)S(1)} %get-tuple-element.109), channel_id=1, source_target_pairs={{1,2},{2,1},{3,4},{4,3},{5,6},{6,5},{7,8},{8,7},{9,10},{10,9},{11,... | collective-permute-start | bytes 9224 | tf_op jit(solution)/shard_map/ppermute | solution.py:27
  108.9 0.0 collective-permute-done.8
  108.9 3.9 %collective-permute-done.7 = bf16[8,192]{1,0:T(8,128)(2,1)S(1)} collective-permute-done((bf16[8,192]{1,0:T(8,128)(2,1)S(1)}, bf16[8,192]{1,0:T(8,128)(2,1)S(1)}, u32[]{:S(2)}, u32[]{:S(2)}) %collective-permute-start.7) | collective-permute-done | bytes 3104 | tf_op jit(solution)/shard_map/ppermute | solution.py:27
  112.8 0.0 all-to-all-done.3.slots
  112.8 5.8 %collective-permute-start.9 = (bf16[16,224,128]{2,1,0:T(8,128)(2,1)S(1)}, bf16[16,224,128]{2,1,0:T(8,128)(2,1)S(1)}, u32[]{:S(2)}, u32[]{:S(2)}) collective-permute-start(bf16[16,224,128]{2,1,0:T(8,128)(2,1)S(1)} %all-to-all-done.3.slots), channel_id=1, source_target_pairs={{0,1},{1,0},{2,3},{3,2},{4,5},{5,4},{6,7},{7,6},{8,9},{9,8},{10,11... | collective-permute-start | bytes 2752520 | tf_op jit(solution)/shard_map/ppermute | solution.py:389
  118.6 1.1 shard_map.134
  119.7 0.8 shard_map.133
  120.5 0.2 collective-permute-done.9.slots
  120.7 1.1 shard_map.135
  (15 shorter events, 0.2 us)
Async XLA Ops:
  1.5 11.2 %collective-permute-start = (bf16[1,64,192]{2,1,0:T(8,128)(2,1)S(1)}, bf16[1,64,192]{2,1,0:T(8,128)(2,1)S(1)}, u32[]{:S(2)}, u32[]{:S(2)}) collective-permute-start(bf16[1,64,192]{2,1,0:T(8,128)(2,1)S(1)} %broadcast_select_fusion.7), channel_id=1, source_target_pairs={{16,32},{32,16},{48,64},{64,48},{80,96},{96,80},{112,128},{128,112... | collective-permute-start | bytes 73736 | tf_op jit(solution)/shard_map/ppermute | solution.py:27
  2.2 10.6 %collective-permute-start.1 = (bf16[1,64,192]{2,1,0:T(8,128)(2,1)S(1)}, bf16[1,64,192]{2,1,0:T(8,128)(2,1)S(1)}, u32[]{:S(2)}, u32[]{:S(2)}) collective-permute-start(bf16[1,64,192]{2,1,0:T(8,128)(2,1)S(1)} %get-tuple-element.87), channel_id=1, source_target_pairs={{0,16},{16,0},{32,48},{48,32},{64,80},{80,64},{96,112},{112,96},{1... | collective-permute-start | bytes 73736 | tf_op jit(solution)/shard_map/ppermute | solution.py:26
  12.5 10.9 %copy-start = (bf16[3,3,192,512]{3,2,1,0:T(8,128)(2,1)S(1)}, bf16[3,3,192,512]{3,2,1,0:T(8,128)(2,1)}, u32[]{:S(2)}) copy-start(bf16[3,3,192,512]{3,2,1,0:T(8,128)(2,1)} %param.10) | copy-start | bytes 5308420
  12.5 10.9 %copy-start.1 = (f32[8,64,128]{2,1,0:T(8,128)S(1)}, f32[8,64,128]{2,1,0:T(8,128)}, u32[]{:S(2)}) copy-start(f32[8,64,128]{2,1,0:T(8,128)} %cell_prev.1) | copy-start | bytes 786436
  12.5 10.9 %copy-start.2 = (f32[8,64,128]{2,1,0:T(8,128)S(1)}, f32[8,64,128]{2,1,0:T(8,128)}, u32[]{:S(2)}) copy-start(f32[8,64,128]{2,1,0:T(8,128)} %cell_cot.1) | copy-start | bytes 786436
  12.5 10.9 %copy-start.3 = (bf16[8,64,128]{2,1,0:T(8,128)(2,1)S(1)}, bf16[8,64,128]{2,1,0:T(8,128)(2,1)}, u32[]{:S(2)}) copy-start(bf16[8,64,128]{2,1,0:T(8,128)(2,1)} %hidden_cot.1) | copy-start | bytes 393220
  12.5 10.9 %copy-start.4 = (f32[512]{0:T(512)S(1)}, f32[512]{0:T(512)}, u32[]{:S(2)}) copy-start(f32[512]{0:T(512)} %param.11) | copy-start | bytes 6148
  12.8 7.5 %collective-permute-start.3 = (bf16[10,1,192]{2,1,0:T(2,128)(2,1)S(1)}, bf16[10,1,192]{2,1,0:T(2,128)(2,1)S(1)}, u32[]{:S(2)}, u32[]{:S(2)}) collective-permute-start(bf16[10,1,192]{2,1,0:T(2,128)(2,1)S(1)} %get-tuple-element.104), channel_id=1, source_target_pairs={{0,1},{1,0},{2,3},{3,2},{4,5},{5,4},{6,7},{7,6},{8,9},{9,8},{10,11... | collective-permute-start | bytes 11528 | tf_op jit(solution)/shard_map/ppermute | solution.py:26
  18.4 5.0 %collective-permute-start.2 = (bf16[10,1,192]{2,1,0:T(2,128)(2,1)S(1)}, bf16[10,1,192]{2,1,0:T(2,128)(2,1)S(1)}, u32[]{:S(2)}, u32[]{:S(2)}) collective-permute-start(bf16[10,1,192]{2,1,0:T(2,128)(2,1)S(1)} %get-tuple-element.105), channel_id=1, source_target_pairs={{1,2},{2,1},{3,4},{4,3},{5,6},{6,5},{7,8},{8,7},{9,10},{10,9},{11,... | collective-permute-start | bytes 11528 | tf_op jit(solution)/shard_map/ppermute | solution.py:27
  26.1 4.4 %collective-permute-start.4 = (bf16[16,224,128]{2,1,0:T(8,128)(2,1)S(1)}, bf16[16,224,128]{2,1,0:T(8,128)(2,1)S(1)}, u32[]{:S(2)}, u32[]{:S(2)}) collective-permute-start(bf16[16,224,128]{2,1,0:T(8,128)(2,1)S(1)} %get-tuple-element.55), channel_id=1, source_target_pairs={{0,1},{1,0},{2,3},{3,2},{4,5},{5,4},{6,7},{7,6},{8,9},{9,8},{10,11... | collective-permute-start | bytes 2752520 | tf_op jit(solution)/shard_map/ppermute | solution.py:343
  32.1 21.2 %all-to-all-start = ((bf16[16,224,128]{2,1,0:T(8,128)(2,1)}), bf16[16,224,128]{2,1,0:T(8,128)(2,1)S(1)}, u32[]{:S(2)}, u32[]{:S(2)}) async-start(bf16[16,224,128]{2,1,0:T(8,128)(2,1)} %shard_map.129), calls=%async_computation | async-start | bytes 1835008 | tf_op jit(solution)/shard_map/all_to_all | solution.py:365
  38.1 13.9 %collective-permute-start.6 = (bf16[80,192]{1,0:T(8,128)(2,1)S(1)}, bf16[80,192]{1,0:T(8,128)(2,1)S(1)}, u32[]{:S(2)}, u32[]{:S(2)}) collective-permute-start(bf16[80,192]{1,0:T(8,128)(2,1)S(1)} %get-tuple-element.94), channel_id=1, source_target_pairs={{0,16},{16,0},{32,48},{48,32},{64,80},{80,64},{96,112},{112,96},{1... | collective-permute-start | bytes 92168 | tf_op jit(solution)/shard_map/ppermute | solution.py:26
  42.9 9.2 %collective-permute-start.5 = (bf16[80,192]{1,0:T(8,128)(2,1)S(1)}, bf16[80,192]{1,0:T(8,128)(2,1)S(1)}, u32[]{:S(2)}, u32[]{:S(2)}) collective-permute-start(bf16[80,192]{1,0:T(8,128)(2,1)S(1)} %get-tuple-element.95), channel_id=1, source_target_pairs={{16,32},{32,16},{48,64},{64,48},{80,96},{96,80},{112,128},{128,112... | collective-permute-start | bytes 92168 | tf_op jit(solution)/shard_map/ppermute | solution.py:27
  94.8 18.0 %all-to-all-start.3 = ((bf16[16,224,128]{2,1,0:T(8,128)(2,1)}), bf16[16,224,128]{2,1,0:T(8,128)(2,1)S(1)}, u32[]{:S(2)}, u32[]{:S(2)}) async-start(bf16[16,224,128]{2,1,0:T(8,128)(2,1)} %shard_map.131), calls=%async_computation.3 | async-start | bytes 1835008 | tf_op jit(solution)/shard_map/all_to_all | solution.py:379
  99.5 9.4 %collective-permute-start.8 = (bf16[8,192]{1,0:T(8,128)(2,1)S(1)}, bf16[8,192]{1,0:T(8,128)(2,1)S(1)}, u32[]{:S(2)}, u32[]{:S(2)}) collective-permute-start(bf16[8,192]{1,0:T(8,128)(2,1)S(1)} %get-tuple-element.108), channel_id=1, source_target_pairs={{0,1},{1,0},{2,3},{3,2},{4,5},{5,4},{6,7},{7,6},{8,9},{9,8},{10,11... | collective-permute-start | bytes 9224 | tf_op jit(solution)/shard_map/ppermute | solution.py:26
  105.5 7.2 %collective-permute-start.7 = (bf16[8,192]{1,0:T(8,128)(2,1)S(1)}, bf16[8,192]{1,0:T(8,128)(2,1)S(1)}, u32[]{:S(2)}, u32[]{:S(2)}) collective-permute-start(bf16[8,192]{1,0:T(8,128)(2,1)S(1)} %get-tuple-element.109), channel_id=1, source_target_pairs={{1,2},{2,1},{3,4},{4,3},{5,6},{6,5},{7,8},{8,7},{9,10},{10,9},{11,... | collective-permute-start | bytes 9224 | tf_op jit(solution)/shard_map/ppermute | solution.py:27
  112.8 7.9 %collective-permute-start.9 = (bf16[16,224,128]{2,1,0:T(8,128)(2,1)S(1)}, bf16[16,224,128]{2,1,0:T(8,128)(2,1)S(1)}, u32[]{:S(2)}, u32[]{:S(2)}) collective-permute-start(bf16[16,224,128]{2,1,0:T(8,128)(2,1)S(1)} %all-to-all-done.3.slots), channel_id=1, source_target_pairs={{0,1},{1,0},{2,3},{3,2},{4,5},{5,4},{6,7},{7,6},{8,9},{9,8},{10,11... | collective-permute-start | bytes 2752520 | tf_op jit(solution)/shard_map/ppermute | solution.py:389

commit v7 on v6

--- a/solution.py
+++ b/solution.py
@@ -98,9 +98,9 @@
         block = own_taps[end - 16 : end, :].astype(F32)
         side = jnp.where(place == 15, right[r].astype(F32), block[:, 2 * ZCH :])
         taps[end - 16 : end, :] = jnp.concatenate([block[:, : 2 * ZCH], side], axis=1).astype(BF16)
-    total = jnp.dot(taps[0:CELLS, :], kernel[0], preferred_element_type=F32)
-    total += jnp.dot(taps[TC : TC + CELLS, :], kernel[1], preferred_element_type=F32)
-    total += jnp.dot(taps[2 * TC : 2 * TC + CELLS, :], kernel[2], preferred_element_type=F32)
+    wide = jnp.concatenate([taps[a * TC : a * TC + CELLS, :] for a in range(3)], axis=1)
+    weights = kernel[...].reshape(3 * TAPS, GATES)
+    total = jnp.dot(wide, weights, preferred_element_type=F32)
     gates[...] = total + bias[...]
     bias_sum = jnp.zeros((8, GATES), F32)
     for r in range(TR):

time: 122 us -> 122 us (level)
  no operation moved by 1% of the time
where the time goes in v7:
time: 122 us
  starting transfers between devices  49.6 us (41%)
  blocking collectives  40.2 us (33%)
  waiting for transfers between devices  17.6 us (14%)
  Pallas kernels  10 us (8%)
  other arithmetic  2.99 us (2%)
    all_to_all x1, blocking collectives, local(): lax.all_to_all(part.reshape(depth, SLOT // depth, 128), 'z', 0, 0, tiled=...  25.8 us
    ppermute x4, starting transfers between devices, to_neighbours(): near = lax.ppermute(jnp.where(even, last, first), axes, inner)  24.7 us
    all_to_all x1, blocking collectives, local(): lax.all_to_all(copies_of(part, depth), 'z', 0, 0, tiled=True)  14.4 us
    pallas_call x10, Pallas kernels, call(): pl.pallas_call(body, out_shape=outs, in_specs=[whole] * (len(args) - far)...  10 us
    ppermute x4, waiting for transfers between devices, to_neighbours(): near = lax.ppermute(jnp.where(even, last, first), axes, inner)  8.49 us
    ppermute x4, waiting for transfers between devices, to_neighbours(): far = lax.ppermute(jnp.where(even, first, last), axes, outer)  6.96 us
    ppermute x4, starting transfers between devices, to_neighbours(): far = lax.ppermute(jnp.where(even, first, last), axes, outer)  6.57 us
    all_to_all x1, starting transfers between devices, local(): part = lax.all_to_all(half, PLANE, 0, 0, tiled=True)  6.03 us
  transfers between devices with their start and end apart: 12, of which 6 were waited for; matrix products, arithmetic and copies ran while one was open for 2% of the time, Pallas kernels for 3%

profile of v7, /device:TPU:1, one launch (start us, length us, event | category | flops | bytes accessed | tf_op | source)
XLA Modules:
  0.0 121.5 jit_solution(11932745916142506745)
XLA Ops:
  0.6 0.9 broadcast_select_fusion.6
  1.5 0.7 collective-permute-start
  2.2 8.3 %collective-permute-start.1 = (bf16[1,64,192]{2,1,0:T(8,128)(2,1)S(1)}, bf16[1,64,192]{2,1,0:T(8,128)(2,1)S(1)}, u32[]{:S(2)}, u32[]{:S(2)}) collective-permute-start(bf16[1,64,192]{2,1,0:T(8,128)(2,1)S(1)} %get-tuple-element.87), channel_id=1, source_target_pairs={{0,16},{16,0},{32,48},{48,32},{64,80},{80,64},{96,112},{112,96},{1... | collective-permute-start | bytes 73736 | tf_op jit(solution)/shard_map/ppermute | solution.py:26
  10.5 0.9 fusion.2
  11.4 1.1 pad_maximum_fusion.stacked
  12.5 0.0 copy-start
  12.5 0.0 copy-start.1
  12.5 0.0 copy-start.2
  12.5 0.0 copy-start.3
  12.5 0.0 copy-start.4
  12.6 0.2 shard_map.126.own_taps
  12.7 0.0 collective-permute-done
  12.7 0.0 collective-permute-done.1
  12.8 5.5 %collective-permute-start.3 = (bf16[10,1,192]{2,1,0:T(2,128)(2,1)S(1)}, bf16[10,1,192]{2,1,0:T(2,128)(2,1)S(1)}, u32[]{:S(2)}, u32[]{:S(2)}) collective-permute-start(bf16[10,1,192]{2,1,0:T(2,128)(2,1)S(1)} %get-tuple-element.104), channel_id=1, source_target_pairs={{0,1},{1,0},{2,3},{3,2},{4,5},{5,4},{6,7},{7,6},{8,9},{9,8},{10,11... | collective-permute-start | bytes 11528 | tf_op jit(solution)/shard_map/ppermute | solution.py:26
  18.4 1.9 %collective-permute-start.2 = (bf16[10,1,192]{2,1,0:T(2,128)(2,1)S(1)}, bf16[10,1,192]{2,1,0:T(2,128)(2,1)S(1)}, u32[]{:S(2)}, u32[]{:S(2)}) collective-permute-start(bf16[10,1,192]{2,1,0:T(2,128)(2,1)S(1)} %get-tuple-element.105), channel_id=1, source_target_pairs={{1,2},{2,1},{3,4},{4,3},{5,6},{6,5},{7,8},{8,7},{9,10},{10,9},{11,... | collective-permute-start | bytes 11528 | tf_op jit(solution)/shard_map/ppermute | solution.py:27
  20.3 0.0 collective-permute-done.3
  20.3 3.1 %collective-permute-done.2 = bf16[10,1,192]{2,1,0:T(2,128)(2,1)S(1)} collective-permute-done((bf16[10,1,192]{2,1,0:T(2,128)(2,1)S(1)}, bf16[10,1,192]{2,1,0:T(2,128)(2,1)S(1)}, u32[]{:S(2)}, u32[]{:S(2)}) %collective-permute-start.2) | collective-permute-done | bytes 3872 | tf_op jit(solution)/shard_map/ppermute | solution.py:27
  23.4 0.0 copy-done
  23.4 0.0 copy-done.1
  23.4 0.0 copy-done.2
  23.4 0.0 copy-done.3
  23.4 0.0 copy-done.4
  23.5 2.4 %shard_map.127 = (bf16[8,64,128]{2,1,0:T(8,128)(2,1)}, f32[8,64,128]{2,1,0:T(8,128)}, f32[8,64,128]{2,1,0:T(8,128)}, bf16[512,512]{1,0:T(8,128)(2,1)S(1)}, bf16[...) custom-call(bf16[640,576]{1,0:T(8,128)(2,1)S(1)} %shard_map.126.own_taps, ...), custom_call_target="tpu_custom_call" | custom-call | flops 1358954496 | bytes 6071808 | tf_op jit(solution)/shard_map/pallas_call | solution.py:289
  25.9 1.9 %collective-permute-start.4 = (bf16[16,224,128]{2,1,0:T(8,128)(2,1)S(1)}, bf16[16,224,128]{2,1,0:T(8,128)(2,1)S(1)}, u32[]{:S(2)}, u32[]{:S(2)}) collective-permute-start(bf16[16,224,128]{2,1,0:T(8,128)(2,1)S(1)} %get-tuple-element.55), channel_id=1, source_target_pairs={{0,1},{1,0},{2,3},{3,2},{4,5},{5,4},{6,7},{7,6},{8,9},{9,8},{10,11... | collective-permute-start | bytes 2752520 | tf_op jit(solution)/shard_map/ppermute | solution.py:343
  27.8 1.7 %shard_map.128 = (f32[512,192]{1,0:T(8,128)S(1)}, bf16[80,192]{1,0:T(8,128)(2,1)S(1)}, bf16[80,192]{1,0:T(8,128)(2,1)S(1)}, f32[8,192]{1,0:T(8,128)S(1)}, f32[8,192]{1,0:T(8,128)S(1)}) custom-call(bf16[512,512]{1,0:T(8,128)(2,1)S(1)} %get-tuple-element.53.grad_gates, bf16[3,576,512]{2,1,0:T(8,128)(2,1)S(1)} %bitcast.5), custom_call_target="tpu_custom_call" | custom-call | flops 905969664 | bytes 2760704 | tf_op jit(solution)/shard_map/pallas_call | solution.py:289
  29.5 0.8 collective-permute-done.4.received
  30.3 1.6 %shard_map.129 = bf16[16,224,128]{2,1,0:T(8,128)(2,1)} custom-call(bf16[640,576]{1,0:T(8,128)(2,1)S(1)} %get-tuple-element.52.taps, bf16[512,512]{1,0:T(8,128)(2,1)S(1)} %get-tuple-element.53.grad_gates, f32[8,512]{1,0:T(8,128)S(1)} %get-tuple-element.54.sums, bf16[16,224,128]{2,1,0:T(8,128)(2,1)S(1)} %collective-permute-done.4.received), custom_call_target="tpu_custom_call" | custom-call | flops 452984832 | bytes 3112960 | tf_op jit(solution)/shard_map/pallas_call | solution.py:289
  31.9 6.0 %all-to-all-start = ((bf16[16,224,128]{2,1,0:T(8,128)(2,1)}), bf16[16,224,128]{2,1,0:T(8,128)(2,1)S(1)}, u32[]{:S(2)}, u32[]{:S(2)}) async-start(bf16[16,224,128]{2,1,0:T(8,128)(2,1)} %shard_map.129), calls=%async_computation | async-start | bytes 1835008 | tf_op jit(solution)/shard_map/all_to_all | solution.py:365
  37.9 4.8 %collective-permute-start.6 = (bf16[80,192]{1,0:T(8,128)(2,1)S(1)}, bf16[80,192]{1,0:T(8,128)(2,1)S(1)}, u32[]{:S(2)}, u32[]{:S(2)}) collective-permute-start(bf16[80,192]{1,0:T(8,128)(2,1)S(1)} %get-tuple-element.94), channel_id=1, source_target_pairs={{0,16},{16,0},{32,48},{48,32},{64,80},{80,64},{96,112},{112,96},{1... | collective-permute-start | bytes 92168 | tf_op jit(solution)/shard_map/ppermute | solution.py:26
  42.7 0.7 collective-permute-start.5
  43.4 8.5 %collective-permute-done.6 = bf16[80,192]{1,0:T(8,128)(2,1)S(1)} collective-permute-done((bf16[80,192]{1,0:T(8,128)(2,1)S(1)}, bf16[80,192]{1,0:T(8,128)(2,1)S(1)}, u32[]{:S(2)}, u32[]{:S(2)}) %collective-permute-start.6) | collective-permute-done | bytes 30752 | tf_op jit(solution)/shard_map/ppermute | solution.py:26
  51.9 0.0 collective-permute-done.5
  51.9 1.2 %all-to-all-done.parts = bf16[16,224,128]{2,1,0:T(8,128)(2,1)S(1)} async-done(((bf16[16,224,128]{2,1,0:T(8,128)(2,1)}), bf16[16,224,128]{2,1,0:T(8,128)(2,1)S(1)}, u32[]{:S(2)}, u32[]{:S(2)}) %all-to-all-start) | async-done | bytes 917536 | tf_op jit(solution)/shard_map/all_to_all | solution.py:365
  53.1 0.1 shard_map.130
  53.3 25.8 %all_to_all.20 = bf16[16,14,128]{2,1,0:T(8,128)(2,1)S(1)} all-to-all(bf16[16,14,128]{2,1,0:T(8,128)(2,1)S(1)} %reshape.190), channel_id=1, replica_groups=mesh['z'=16,'xh'=2,'y'=4,'xl'=2,'core'=2] {'z'}, dimensions={0} | all-to-all | bytes 114688 | tf_op jit(solution)/shard_map/all_to_all | solution.py:369
  79.1 14.4 %all_to_all.21 = bf16[16,14,128]{2,1,0:T(8,128)(2,1)S(1)} all-to-all(bf16[16,14,128]{2,1,0:T(8,128)(2,1)S(1)} %broadcast_in_dim.2), channel_id=1, replica_groups=mesh['z'=16,'xh'=2,'y'=4,'xl'=2,'core'=2] {'z'}, dimensions={0} | all-to-all | bytes 114688 | tf_op jit(solution)/shard_map/all_to_all | solution.py:372
  93.6 1.0 shard_map.131
  94.6 4.6 %all-to-all-start.3 = ((bf16[16,224,128]{2,1,0:T(8,128)(2,1)}), bf16[16,224,128]{2,1,0:T(8,128)(2,1)S(1)}, u32[]{:S(2)}, u32[]{:S(2)}) async-start(bf16[16,224,128]{2,1,0:T(8,128)(2,1)} %shard_map.131), calls=%async_computation.3 | async-start | bytes 1835008 | tf_op jit(solution)/shard_map/all_to_all | solution.py:379
  99.3 6.1 %collective-permute-start.8 = (bf16[8,192]{1,0:T(8,128)(2,1)S(1)}, bf16[8,192]{1,0:T(8,128)(2,1)S(1)}, u32[]{:S(2)}, u32[]{:S(2)}) collective-permute-start(bf16[8,192]{1,0:T(8,128)(2,1)S(1)} %get-tuple-element.108), channel_id=1, source_target_pairs={{0,1},{1,0},{2,3},{3,2},{4,5},{5,4},{6,7},{7,6},{8,9},{9,8},{10,11... | collective-permute-start | bytes 9224 | tf_op jit(solution)/shard_map/ppermute | solution.py:26
  105.3 3.3 %collective-permute-start.7 = (bf16[8,192]{1,0:T(8,128)(2,1)S(1)}, bf16[8,192]{1,0:T(8,128)(2,1)S(1)}, u32[]{:S(2)}, u32[]{:S(2)}) collective-permute-start(bf16[8,192]{1,0:T(8,128)(2,1)S(1)} %get-tuple-element.109), channel_id=1, source_target_pairs={{1,2},{2,1},{3,4},{4,3},{5,6},{6,5},{7,8},{8,7},{9,10},{10,9},{11,... | collective-permute-start | bytes 9224 | tf_op jit(solution)/shard_map/ppermute | solution.py:27
  108.7 0.0 collective-permute-done.8
  108.7 3.9 %collective-permute-done.7 = bf16[8,192]{1,0:T(8,128)(2,1)S(1)} collective-permute-done((bf16[8,192]{1,0:T(8,128)(2,1)S(1)}, bf16[8,192]{1,0:T(8,128)(2,1)S(1)}, u32[]{:S(2)}, u32[]{:S(2)}) %collective-permute-start.7) | collective-permute-done | bytes 3104 | tf_op jit(solution)/shard_map/ppermute | solution.py:27
  112.6 0.0 all-to-all-done.3.slots
  112.6 5.8 %collective-permute-start.9 = (bf16[16,224,128]{2,1,0:T(8,128)(2,1)S(1)}, bf16[16,224,128]{2,1,0:T(8,128)(2,1)S(1)}, u32[]{:S(2)}, u32[]{:S(2)}) collective-permute-start(bf16[16,224,128]{2,1,0:T(8,128)(2,1)S(1)} %all-to-all-done.3.slots), channel_id=1, source_target_pairs={{0,1},{1,0},{2,3},{3,2},{4,5},{5,4},{6,7},{7,6},{8,9},{9,8},{10,11... | collective-permute-start | bytes 2752520 | tf_op jit(solution)/shard_map/ppermute | solution.py:389
  118.4 1.1 shard_map.134
  119.5 0.8 shard_map.133
  120.3 0.2 collective-permute-done.9.slots
  120.5 1.1 shard_map.135
  (15 shorter events, 0.2 us)
Async XLA Ops:
  1.5 11.2 %collective-permute-start = (bf16[1,64,192]{2,1,0:T(8,128)(2,1)S(1)}, bf16[1,64,192]{2,1,0:T(8,128)(2,1)S(1)}, u32[]{:S(2)}, u32[]{:S(2)}) collective-permute-start(bf16[1,64,192]{2,1,0:T(8,128)(2,1)S(1)} %broadcast_select_fusion.7), channel_id=1, source_target_pairs={{16,32},{32,16},{48,64},{64,48},{80,96},{96,80},{112,128},{128,112... | collective-permute-start | bytes 73736 | tf_op jit(solution)/shard_map/ppermute | solution.py:27
  2.2 10.6 %collective-permute-start.1 = (bf16[1,64,192]{2,1,0:T(8,128)(2,1)S(1)}, bf16[1,64,192]{2,1,0:T(8,128)(2,1)S(1)}, u32[]{:S(2)}, u32[]{:S(2)}) collective-permute-start(bf16[1,64,192]{2,1,0:T(8,128)(2,1)S(1)} %get-tuple-element.87), channel_id=1, source_target_pairs={{0,16},{16,0},{32,48},{48,32},{64,80},{80,64},{96,112},{112,96},{1... | collective-permute-start | bytes 73736 | tf_op jit(solution)/shard_map/ppermute | solution.py:26
  12.5 10.9 %copy-start = (bf16[3,3,192,512]{3,2,1,0:T(8,128)(2,1)S(1)}, bf16[3,3,192,512]{3,2,1,0:T(8,128)(2,1)}, u32[]{:S(2)}) copy-start(bf16[3,3,192,512]{3,2,1,0:T(8,128)(2,1)} %param.10) | copy-start | bytes 5308420
  12.5 10.9 %copy-start.1 = (f32[8,64,128]{2,1,0:T(8,128)S(1)}, f32[8,64,128]{2,1,0:T(8,128)}, u32[]{:S(2)}) copy-start(f32[8,64,128]{2,1,0:T(8,128)} %cell_prev.1) | copy-start | bytes 786436
  12.5 10.9 %copy-start.2 = (f32[8,64,128]{2,1,0:T(8,128)S(1)}, f32[8,64,128]{2,1,0:T(8,128)}, u32[]{:S(2)}) copy-start(f32[8,64,128]{2,1,0:T(8,128)} %cell_cot.1) | copy-start | bytes 786436
  12.5 10.9 %copy-start.3 = (bf16[8,64,128]{2,1,0:T(8,128)(2,1)S(1)}, bf16[8,64,128]{2,1,0:T(8,128)(2,1)}, u32[]{:S(2)}) copy-start(bf16[8,64,128]{2,1,0:T(8,128)(2,1)} %hidden_cot.1) | copy-start | bytes 393220
  12.5 10.9 %copy-start.4 = (f32[512]{0:T(512)S(1)}, f32[512]{0:T(512)}, u32[]{:S(2)}) copy-start(f32[512]{0:T(512)} %param.11) | copy-start | bytes 6148
  12.8 7.5 %collective-permute-start.3 = (bf16[10,1,192]{2,1,0:T(2,128)(2,1)S(1)}, bf16[10,1,192]{2,1,0:T(2,128)(2,1)S(1)}, u32[]{:S(2)}, u32[]{:S(2)}) collective-permute-start(bf16[10,1,192]{2,1,0:T(2,128)(2,1)S(1)} %get-tuple-element.104), channel_id=1, source_target_pairs={{0,1},{1,0},{2,3},{3,2},{4,5},{5,4},{6,7},{7,6},{8,9},{9,8},{10,11... | collective-permute-start | bytes 11528 | tf_op jit(solution)/shard_map/ppermute | solution.py:26
  18.4 5.0 %collective-permute-start.2 = (bf16[10,1,192]{2,1,0:T(2,128)(2,1)S(1)}, bf16[10,1,192]{2,1,0:T(2,128)(2,1)S(1)}, u32[]{:S(2)}, u32[]{:S(2)}) collective-permute-start(bf16[10,1,192]{2,1,0:T(2,128)(2,1)S(1)} %get-tuple-element.105), channel_id=1, source_target_pairs={{1,2},{2,1},{3,4},{4,3},{5,6},{6,5},{7,8},{8,7},{9,10},{10,9},{11,... | collective-permute-start | bytes 11528 | tf_op jit(solution)/shard_map/ppermute | solution.py:27
  25.9 4.4 %collective-permute-start.4 = (bf16[16,224,128]{2,1,0:T(8,128)(2,1)S(1)}, bf16[16,224,128]{2,1,0:T(8,128)(2,1)S(1)}, u32[]{:S(2)}, u32[]{:S(2)}) collective-permute-start(bf16[16,224,128]{2,1,0:T(8,128)(2,1)S(1)} %get-tuple-element.55), channel_id=1, source_target_pairs={{0,1},{1,0},{2,3},{3,2},{4,5},{5,4},{6,7},{7,6},{8,9},{9,8},{10,11... | collective-permute-start | bytes 2752520 | tf_op jit(solution)/shard_map/ppermute | solution.py:343
  31.9 21.2 %all-to-all-start = ((bf16[16,224,128]{2,1,0:T(8,128)(2,1)}), bf16[16,224,128]{2,1,0:T(8,128)(2,1)S(1)}, u32[]{:S(2)}, u32[]{:S(2)}) async-start(bf16[16,224,128]{2,1,0:T(8,128)(2,1)} %shard_map.129), calls=%async_computation | async-start | bytes 1835008 | tf_op jit(solution)/shard_map/all_to_all | solution.py:365
  37.9 13.9 %collective-permute-start.6 = (bf16[80,192]{1,0:T(8,128)(2,1)S(1)}, bf16[80,192]{1,0:T(8,128)(2,1)S(1)}, u32[]{:S(2)}, u32[]{:S(2)}) collective-permute-start(bf16[80,192]{1,0:T(8,128)(2,1)S(1)} %get-tuple-element.94), channel_id=1, source_target_pairs={{0,16},{16,0},{32,48},{48,32},{64,80},{80,64},{96,112},{112,96},{1... | collective-permute-start | bytes 92168 | tf_op jit(solution)/shard_map/ppermute | solution.py:26
  42.7 9.2 %collective-permute-start.5 = (bf16[80,192]{1,0:T(8,128)(2,1)S(1)}, bf16[80,192]{1,0:T(8,128)(2,1)S(1)}, u32[]{:S(2)}, u32[]{:S(2)}) collective-permute-start(bf16[80,192]{1,0:T(8,128)(2,1)S(1)} %get-tuple-element.95), channel_id=1, source_target_pairs={{16,32},{32,16},{48,64},{64,48},{80,96},{96,80},{112,128},{128,112... | collective-permute-start | bytes 92168 | tf_op jit(solution)/shard_map/ppermute | solution.py:27
  94.6 18.0 %all-to-all-start.3 = ((bf16[16,224,128]{2,1,0:T(8,128)(2,1)}), bf16[16,224,128]{2,1,0:T(8,128)(2,1)S(1)}, u32[]{:S(2)}, u32[]{:S(2)}) async-start(bf16[16,224,128]{2,1,0:T(8,128)(2,1)} %shard_map.131), calls=%async_computation.3 | async-start | bytes 1835008 | tf_op jit(solution)/shard_map/all_to_all | solution.py:379
  99.3 9.4 %collective-permute-start.8 = (bf16[8,192]{1,0:T(8,128)(2,1)S(1)}, bf16[8,192]{1,0:T(8,128)(2,1)S(1)}, u32[]{:S(2)}, u32[]{:S(2)}) collective-permute-start(bf16[8,192]{1,0:T(8,128)(2,1)S(1)} %get-tuple-element.108), channel_id=1, source_target_pairs={{0,1},{1,0},{2,3},{3,2},{4,5},{5,4},{6,7},{7,6},{8,9},{9,8},{10,11... | collective-permute-start | bytes 9224 | tf_op jit(solution)/shard_map/ppermute | solution.py:26
  105.3 7.2 %collective-permute-start.7 = (bf16[8,192]{1,0:T(8,128)(2,1)S(1)}, bf16[8,192]{1,0:T(8,128)(2,1)S(1)}, u32[]{:S(2)}, u32[]{:S(2)}) collective-permute-start(bf16[8,192]{1,0:T(8,128)(2,1)S(1)} %get-tuple-element.109), channel_id=1, source_target_pairs={{1,2},{2,1},{3,4},{4,3},{5,6},{6,5},{7,8},{8,7},{9,10},{10,9},{11,... | collective-permute-start | bytes 9224 | tf_op jit(solution)/shard_map/ppermute | solution.py:27
  112.6 7.9 %collective-permute-start.9 = (bf16[16,224,128]{2,1,0:T(8,128)(2,1)S(1)}, bf16[16,224,128]{2,1,0:T(8,128)(2,1)S(1)}, u32[]{:S(2)}, u32[]{:S(2)}) collective-permute-start(bf16[16,224,128]{2,1,0:T(8,128)(2,1)S(1)} %all-to-all-done.3.slots), channel_id=1, source_target_pairs={{0,1},{1,0},{2,3},{3,2},{4,5},{5,4},{6,7},{7,6},{8,9},{9,8},{10,11... | collective-permute-start | bytes 2752520 | tf_op jit(solution)/shard_map/ppermute | solution.py:389

commit v8 on v7

--- a/solution.py
+++ b/solution.py
@@ -7,7 +7,7 @@
 
 ROWS = ("z", "xh")
 COLS = ("y", "xl", "core")
-PLANE = ("xh", "y", "xl")
+PLANE = ("y", "xl", "xh")
 BF16 = jnp.bfloat16
 F32 = jnp.float32
 TR, TC = 8, 64

time: 122 us -> 121 us (level)
  waiting for transfers between devices: 17.6 us -> 16.1 us
where the time goes in v8:
time: 121 us; the launch traced here: 120 us
  starting transfers between devices  49.3 us (41%)
  blocking collectives  40.3 us (33%)
  waiting for transfers between devices  16.1 us (13%)
  Pallas kernels  10 us (8%)
  other arithmetic  2.99 us (2%)
    all_to_all x1, blocking collectives, local(): lax.all_to_all(part.reshape(depth, SLOT // depth, 128), 'z', 0, 0, tiled=...  25.9 us
    ppermute x4, starting transfers between devices, to_neighbours(): near = lax.ppermute(jnp.where(even, last, first), axes, inner)  25.1 us
    all_to_all x1, blocking collectives, local(): lax.all_to_all(copies_of(part, depth), 'z', 0, 0, tiled=True)  14.4 us
    pallas_call x10, Pallas kernels, call(): pl.pallas_call(body, out_shape=outs, in_specs=[whole] * (len(args) - far)...  10 us
    ppermute x4, waiting for transfers between devices, to_neighbours(): near = lax.ppermute(jnp.where(even, last, first), axes, inner)  8.72 us
    ppermute x4, starting transfers between devices, to_neighbours(): far = lax.ppermute(jnp.where(even, first, last), axes, outer)  6.69 us
    ppermute x4, waiting for transfers between devices, to_neighbours(): far = lax.ppermute(jnp.where(even, first, last), axes, outer)  6.13 us
    all_to_all x1, starting transfers between devices, local(): part = lax.all_to_all(half, PLANE, 0, 0, tiled=True)  6.03 us
  transfers between devices with their start and end apart: 12, of which 6 were waited for; matrix products, arithmetic and copies ran while one was open for 2% of the time, Pallas kernels for 3%

profile of v8, /device:TPU:1, one launch (start us, length us, event | category | flops | bytes accessed | tf_op | source)
XLA Modules:
  0.0 119.8 jit_solution(15671763001919493101)
XLA Ops:
  0.6 0.9 broadcast_select_fusion.6
  1.5 0.7 collective-permute-start
  2.2 8.3 %collective-permute-start.1 = (bf16[1,64,192]{2,1,0:T(8,128)(2,1)S(1)}, bf16[1,64,192]{2,1,0:T(8,128)(2,1)S(1)}, u32[]{:S(2)}, u32[]{:S(2)}) collective-permute-start(bf16[1,64,192]{2,1,0:T(8,128)(2,1)S(1)} %get-tuple-element.87), channel_id=1, source_target_pairs={{0,16},{16,0},{32,48},{48,32},{64,80},{80,64},{96,112},{112,96},{1... | collective-permute-start | bytes 73736 | tf_op jit(solution)/shard_map/ppermute | solution.py:26
  10.5 0.9 fusion.2
  11.4 1.1 pad_maximum_fusion.stacked
  12.5 0.0 copy-start
  12.5 0.0 copy-start.1
  12.5 0.0 copy-start.2
  12.5 0.0 copy-start.3
  12.5 0.0 copy-start.4
  12.6 0.2 shard_map.126.own_taps
  12.7 0.0 collective-permute-done
  12.7 0.0 collective-permute-done.1
  12.8 5.5 %collective-permute-start.3 = (bf16[10,1,192]{2,1,0:T(2,128)(2,1)S(1)}, bf16[10,1,192]{2,1,0:T(2,128)(2,1)S(1)}, u32[]{:S(2)}, u32[]{:S(2)}) collective-permute-start(bf16[10,1,192]{2,1,0:T(2,128)(2,1)S(1)} %get-tuple-element.104), channel_id=1, source_target_pairs={{0,1},{1,0},{2,3},{3,2},{4,5},{5,4},{6,7},{7,6},{8,9},{9,8},{10,11... | collective-permute-start | bytes 11528 | tf_op jit(solution)/shard_map/ppermute | solution.py:26
  18.4 1.9 %collective-permute-start.2 = (bf16[10,1,192]{2,1,0:T(2,128)(2,1)S(1)}, bf16[10,1,192]{2,1,0:T(2,128)(2,1)S(1)}, u32[]{:S(2)}, u32[]{:S(2)}) collective-permute-start(bf16[10,1,192]{2,1,0:T(2,128)(2,1)S(1)} %get-tuple-element.105), channel_id=1, source_target_pairs={{1,2},{2,1},{3,4},{4,3},{5,6},{6,5},{7,8},{8,7},{9,10},{10,9},{11,... | collective-permute-start | bytes 11528 | tf_op jit(solution)/shard_map/ppermute | solution.py:27
  20.3 0.0 collective-permute-done.3
  20.3 3.1 %collective-permute-done.2 = bf16[10,1,192]{2,1,0:T(2,128)(2,1)S(1)} collective-permute-done((bf16[10,1,192]{2,1,0:T(2,128)(2,1)S(1)}, bf16[10,1,192]{2,1,0:T(2,128)(2,1)S(1)}, u32[]{:S(2)}, u32[]{:S(2)}) %collective-permute-start.2) | collective-permute-done | bytes 3872 | tf_op jit(solution)/shard_map/ppermute | solution.py:27
  23.4 0.0 copy-done
  23.4 0.0 copy-done.1
  23.4 0.0 copy-done.2
  23.4 0.0 copy-done.3
  23.4 0.0 copy-done.4
  23.5 2.4 %shard_map.127 = (bf16[8,64,128]{2,1,0:T(8,128)(2,1)}, f32[8,64,128]{2,1,0:T(8,128)}, f32[8,64,128]{2,1,0:T(8,128)}, bf16[512,512]{1,0:T(8,128)(2,1)S(1)}, bf16[...) custom-call(bf16[640,576]{1,0:T(8,128)(2,1)S(1)} %shard_map.126.own_taps, ...), custom_call_target="tpu_custom_call" | custom-call | flops 1358954496 | bytes 6071808 | tf_op jit(solution)/shard_map/pallas_call | solution.py:289
  25.9 1.9 %collective-permute-start.4 = (bf16[16,224,128]{2,1,0:T(8,128)(2,1)S(1)}, bf16[16,224,128]{2,1,0:T(8,128)(2,1)S(1)}, u32[]{:S(2)}, u32[]{:S(2)}) collective-permute-start(bf16[16,224,128]{2,1,0:T(8,128)(2,1)S(1)} %get-tuple-element.55), channel_id=1, source_target_pairs={{0,1},{1,0},{2,3},{3,2},{4,5},{5,4},{6,7},{7,6},{8,9},{9,8},{10,11... | collective-permute-start | bytes 2752520 | tf_op jit(solution)/shard_map/ppermute | solution.py:343
  27.8 1.7 %shard_map.128 = (f32[512,192]{1,0:T(8,128)S(1)}, bf16[80,192]{1,0:T(8,128)(2,1)S(1)}, bf16[80,192]{1,0:T(8,128)(2,1)S(1)}, f32[8,192]{1,0:T(8,128)S(1)}, f32[8,192]{1,0:T(8,128)S(1)}) custom-call(bf16[512,512]{1,0:T(8,128)(2,1)S(1)} %get-tuple-element.53.grad_gates, bf16[3,576,512]{2,1,0:T(8,128)(2,1)S(1)} %bitcast.5), custom_call_target="tpu_custom_call" | custom-call | flops 905969664 | bytes 2760704 | tf_op jit(solution)/shard_map/pallas_call | solution.py:289
  29.5 0.8 collective-permute-done.4.received
  30.3 1.6 %shard_map.129 = bf16[16,224,128]{2,1,0:T(8,128)(2,1)} custom-call(bf16[640,576]{1,0:T(8,128)(2,1)S(1)} %get-tuple-element.52.taps, bf16[512,512]{1,0:T(8,128)(2,1)S(1)} %get-tuple-element.53.grad_gates, f32[8,512]{1,0:T(8,128)S(1)} %get-tuple-element.54.sums, bf16[16,224,128]{2,1,0:T(8,128)(2,1)S(1)} %collective-permute-done.4.received), custom_call_target="tpu_custom_call" | custom-call | flops 452984832 | bytes 3112960 | tf_op jit(solution)/shard_map/pallas_call | solution.py:289
  31.9 6.0 %all-to-all-start = ((bf16[16,224,128]{2,1,0:T(8,128)(2,1)}), bf16[16,224,128]{2,1,0:T(8,128)(2,1)S(1)}, u32[]{:S(2)}, u32[]{:S(2)}) async-start(bf16[16,224,128]{2,1,0:T(8,128)(2,1)} %shard_map.129), calls=%async_computation | async-start | bytes 1835008 | tf_op jit(solution)/shard_map/all_to_all | solution.py:365
  37.9 4.8 %collective-permute-start.6 = (bf16[80,192]{1,0:T(8,128)(2,1)S(1)}, bf16[80,192]{1,0:T(8,128)(2,1)S(1)}, u32[]{:S(2)}, u32[]{:S(2)}) collective-permute-start(bf16[80,192]{1,0:T(8,128)(2,1)S(1)} %get-tuple-element.94), channel_id=1, source_target_pairs={{0,16},{16,0},{32,48},{48,32},{64,80},{80,64},{96,112},{112,96},{1... | collective-permute-start | bytes 92168 | tf_op jit(solution)/shard_map/ppermute | solution.py:26
  42.7 0.7 collective-permute-start.5
  43.4 8.7 %collective-permute-done.6 = bf16[80,192]{1,0:T(8,128)(2,1)S(1)} collective-permute-done((bf16[80,192]{1,0:T(8,128)(2,1)S(1)}, bf16[80,192]{1,0:T(8,128)(2,1)S(1)}, u32[]{:S(2)}, u32[]{:S(2)}) %collective-permute-start.6) | collective-permute-done | bytes 30752 | tf_op jit(solution)/shard_map/ppermute | solution.py:26
  52.1 0.0 collective-permute-done.5
  52.1 0.3 all-to-all-done.parts
  52.5 0.1 shard_map.130
  52.6 25.9 %all_to_all.20 = bf16[16,14,128]{2,1,0:T(8,128)(2,1)S(1)} all-to-all(bf16[16,14,128]{2,1,0:T(8,128)(2,1)S(1)} %reshape.190), channel_id=1, replica_groups=mesh['z'=16,'xh'=2,'y'=4,'xl'=2,'core'=2] {'z'}, dimensions={0} | all-to-all | bytes 114688 | tf_op jit(solution)/shard_map/all_to_all | solution.py:369
  78.6 14.4 %all_to_all.21 = bf16[16,14,128]{2,1,0:T(8,128)(2,1)S(1)} all-to-all(bf16[16,14,128]{2,1,0:T(8,128)(2,1)S(1)} %broadcast_in_dim.2), channel_id=1, replica_groups=mesh['z'=16,'xh'=2,'y'=4,'xl'=2,'core'=2] {'z'}, dimensions={0} | all-to-all | bytes 114688 | tf_op jit(solution)/shard_map/all_to_all | solution.py:372
  93.0 1.0 shard_map.131
  94.1 4.7 %all-to-all-start.3 = ((bf16[16,224,128]{2,1,0:T(8,128)(2,1)}), bf16[16,224,128]{2,1,0:T(8,128)(2,1)S(1)}, u32[]{:S(2)}, u32[]{:S(2)}) async-start(bf16[16,224,128]{2,1,0:T(8,128)(2,1)} %shard_map.131), calls=%async_computation.3 | async-start | bytes 1835008 | tf_op jit(solution)/shard_map/all_to_all | solution.py:379
  98.8 6.5 %collective-permute-start.8 = (bf16[8,192]{1,0:T(8,128)(2,1)S(1)}, bf16[8,192]{1,0:T(8,128)(2,1)S(1)}, u32[]{:S(2)}, u32[]{:S(2)}) collective-permute-start(bf16[8,192]{1,0:T(8,128)(2,1)S(1)} %get-tuple-element.108), channel_id=1, source_target_pairs={{0,1},{1,0},{2,3},{3,2},{4,5},{5,4},{6,7},{7,6},{8,9},{9,8},{10,11... | collective-permute-start | bytes 9224 | tf_op jit(solution)/shard_map/ppermute | solution.py:26
  105.3 3.4 %collective-permute-start.7 = (bf16[8,192]{1,0:T(8,128)(2,1)S(1)}, bf16[8,192]{1,0:T(8,128)(2,1)S(1)}, u32[]{:S(2)}, u32[]{:S(2)}) collective-permute-start(bf16[8,192]{1,0:T(8,128)(2,1)S(1)} %get-tuple-element.109), channel_id=1, source_target_pairs={{1,2},{2,1},{3,4},{4,3},{5,6},{6,5},{7,8},{8,7},{9,10},{10,9},{11,... | collective-permute-start | bytes 9224 | tf_op jit(solution)/shard_map/ppermute | solution.py:27
  108.8 0.0 collective-permute-done.8
  108.8 3.1 %collective-permute-done.7 = bf16[8,192]{1,0:T(8,128)(2,1)S(1)} collective-permute-done((bf16[8,192]{1,0:T(8,128)(2,1)S(1)}, bf16[8,192]{1,0:T(8,128)(2,1)S(1)}, u32[]{:S(2)}, u32[]{:S(2)}) %collective-permute-start.7) | collective-permute-done | bytes 3104 | tf_op jit(solution)/shard_map/ppermute | solution.py:27
  111.9 0.0 all-to-all-done.3.slots
  111.9 4.8 %collective-permute-start.9 = (bf16[16,224,128]{2,1,0:T(8,128)(2,1)S(1)}, bf16[16,224,128]{2,1,0:T(8,128)(2,1)S(1)}, u32[]{:S(2)}, u32[]{:S(2)}) collective-permute-start(bf16[16,224,128]{2,1,0:T(8,128)(2,1)S(1)} %all-to-all-done.3.slots), channel_id=1, source_target_pairs={{0,1},{1,0},{2,3},{3,2},{4,5},{5,4},{6,7},{7,6},{8,9},{9,8},{10,11... | collective-permute-start | bytes 2752520 | tf_op jit(solution)/shard_map/ppermute | solution.py:389
  116.7 1.1 shard_map.134
  117.8 0.8 shard_map.133
  118.6 0.2 collective-permute-done.9.slots
  118.8 1.1 shard_map.135
  (15 shorter events, 0.2 us)
Async XLA Ops:
  1.5 11.2 %collective-permute-start = (bf16[1,64,192]{2,1,0:T(8,128)(2,1)S(1)}, bf16[1,64,192]{2,1,0:T(8,128)(2,1)S(1)}, u32[]{:S(2)}, u32[]{:S(2)}) collective-permute-start(bf16[1,64,192]{2,1,0:T(8,128)(2,1)S(1)} %broadcast_select_fusion.7), channel_id=1, source_target_pairs={{16,32},{32,16},{48,64},{64,48},{80,96},{96,80},{112,128},{128,112... | collective-permute-start | bytes 73736 | tf_op jit(solution)/shard_map/ppermute | solution.py:27
  2.2 10.6 %collective-permute-start.1 = (bf16[1,64,192]{2,1,0:T(8,128)(2,1)S(1)}, bf16[1,64,192]{2,1,0:T(8,128)(2,1)S(1)}, u32[]{:S(2)}, u32[]{:S(2)}) collective-permute-start(bf16[1,64,192]{2,1,0:T(8,128)(2,1)S(1)} %get-tuple-element.87), channel_id=1, source_target_pairs={{0,16},{16,0},{32,48},{48,32},{64,80},{80,64},{96,112},{112,96},{1... | collective-permute-start | bytes 73736 | tf_op jit(solution)/shard_map/ppermute | solution.py:26
  12.5 10.9 %copy-start = (bf16[3,3,192,512]{3,2,1,0:T(8,128)(2,1)S(1)}, bf16[3,3,192,512]{3,2,1,0:T(8,128)(2,1)}, u32[]{:S(2)}) copy-start(bf16[3,3,192,512]{3,2,1,0:T(8,128)(2,1)} %param.10) | copy-start | bytes 5308420
  12.5 10.9 %copy-start.1 = (f32[8,64,128]{2,1,0:T(8,128)S(1)}, f32[8,64,128]{2,1,0:T(8,128)}, u32[]{:S(2)}) copy-start(f32[8,64,128]{2,1,0:T(8,128)} %cell_prev.1) | copy-start | bytes 786436
  12.5 10.9 %copy-start.2 = (f32[8,64,128]{2,1,0:T(8,128)S(1)}, f32[8,64,128]{2,1,0:T(8,128)}, u32[]{:S(2)}) copy-start(f32[8,64,128]{2,1,0:T(8,128)} %cell_cot.1) | copy-start | bytes 786436
  12.5 10.9 %copy-start.3 = (bf16[8,64,128]{2,1,0:T(8,128)(2,1)S(1)}, bf16[8,64,128]{2,1,0:T(8,128)(2,1)}, u32[]{:S(2)}) copy-start(bf16[8,64,128]{2,1,0:T(8,128)(2,1)} %hidden_cot.1) | copy-start | bytes 393220
  12.5 10.9 %copy-start.4 = (f32[512]{0:T(512)S(1)}, f32[512]{0:T(512)}, u32[]{:S(2)}) copy-start(f32[512]{0:T(512)} %param.11) | copy-start | bytes 6148
  12.8 7.5 %collective-permute-start.3 = (bf16[10,1,192]{2,1,0:T(2,128)(2,1)S(1)}, bf16[10,1,192]{2,1,0:T(2,128)(2,1)S(1)}, u32[]{:S(2)}, u32[]{:S(2)}) collective-permute-start(bf16[10,1,192]{2,1,0:T(2,128)(2,1)S(1)} %get-tuple-element.104), channel_id=1, source_target_pairs={{0,1},{1,0},{2,3},{3,2},{4,5},{5,4},{6,7},{7,6},{8,9},{9,8},{10,11... | collective-permute-start | bytes 11528 | tf_op jit(solution)/shard_map/ppermute | solution.py:26
  18.4 5.0 %collective-permute-start.2 = (bf16[10,1,192]{2,1,0:T(2,128)(2,1)S(1)}, bf16[10,1,192]{2,1,0:T(2,128)(2,1)S(1)}, u32[]{:S(2)}, u32[]{:S(2)}) collective-permute-start(bf16[10,1,192]{2,1,0:T(2,128)(2,1)S(1)} %get-tuple-element.105), channel_id=1, source_target_pairs={{1,2},{2,1},{3,4},{4,3},{5,6},{6,5},{7,8},{8,7},{9,10},{10,9},{11,... | collective-permute-start | bytes 11528 | tf_op jit(solution)/shard_map/ppermute | solution.py:27
  25.9 4.4 %collective-permute-start.4 = (bf16[16,224,128]{2,1,0:T(8,128)(2,1)S(1)}, bf16[16,224,128]{2,1,0:T(8,128)(2,1)S(1)}, u32[]{:S(2)}, u32[]{:S(2)}) collective-permute-start(bf16[16,224,128]{2,1,0:T(8,128)(2,1)S(1)} %get-tuple-element.55), channel_id=1, source_target_pairs={{0,1},{1,0},{2,3},{3,2},{4,5},{5,4},{6,7},{7,6},{8,9},{9,8},{10,11... | collective-permute-start | bytes 2752520 | tf_op jit(solution)/shard_map/ppermute | solution.py:343
  31.9 20.6 %all-to-all-start = ((bf16[16,224,128]{2,1,0:T(8,128)(2,1)}), bf16[16,224,128]{2,1,0:T(8,128)(2,1)S(1)}, u32[]{:S(2)}, u32[]{:S(2)}) async-start(bf16[16,224,128]{2,1,0:T(8,128)(2,1)} %shard_map.129), calls=%async_computation | async-start | bytes 1835008 | tf_op jit(solution)/shard_map/all_to_all | solution.py:365
  37.9 14.2 %collective-permute-start.6 = (bf16[80,192]{1,0:T(8,128)(2,1)S(1)}, bf16[80,192]{1,0:T(8,128)(2,1)S(1)}, u32[]{:S(2)}, u32[]{:S(2)}) collective-permute-start(bf16[80,192]{1,0:T(8,128)(2,1)S(1)} %get-tuple-element.94), channel_id=1, source_target_pairs={{0,16},{16,0},{32,48},{48,32},{64,80},{80,64},{96,112},{112,96},{1... | collective-permute-start | bytes 92168 | tf_op jit(solution)/shard_map/ppermute | solution.py:26
  42.7 9.4 %collective-permute-start.5 = (bf16[80,192]{1,0:T(8,128)(2,1)S(1)}, bf16[80,192]{1,0:T(8,128)(2,1)S(1)}, u32[]{:S(2)}, u32[]{:S(2)}) collective-permute-start(bf16[80,192]{1,0:T(8,128)(2,1)S(1)} %get-tuple-element.95), channel_id=1, source_target_pairs={{16,32},{32,16},{48,64},{64,48},{80,96},{96,80},{112,128},{128,112... | collective-permute-start | bytes 92168 | tf_op jit(solution)/shard_map/ppermute | solution.py:27
  94.1 17.8 %all-to-all-start.3 = ((bf16[16,224,128]{2,1,0:T(8,128)(2,1)}), bf16[16,224,128]{2,1,0:T(8,128)(2,1)S(1)}, u32[]{:S(2)}, u32[]{:S(2)}) async-start(bf16[16,224,128]{2,1,0:T(8,128)(2,1)} %shard_map.131), calls=%async_computation.3 | async-start | bytes 1835008 | tf_op jit(solution)/shard_map/all_to_all | solution.py:379
  98.8 10.0 %collective-permute-start.8 = (bf16[8,192]{1,0:T(8,128)(2,1)S(1)}, bf16[8,192]{1,0:T(8,128)(2,1)S(1)}, u32[]{:S(2)}, u32[]{:S(2)}) collective-permute-start(bf16[8,192]{1,0:T(8,128)(2,1)S(1)} %get-tuple-element.108), channel_id=1, source_target_pairs={{0,1},{1,0},{2,3},{3,2},{4,5},{5,4},{6,7},{7,6},{8,9},{9,8},{10,11... | collective-permute-start | bytes 9224 | tf_op jit(solution)/shard_map/ppermute | solution.py:26
  105.3 6.5 %collective-permute-start.7 = (bf16[8,192]{1,0:T(8,128)(2,1)S(1)}, bf16[8,192]{1,0:T(8,128)(2,1)S(1)}, u32[]{:S(2)}, u32[]{:S(2)}) collective-permute-start(bf16[8,192]{1,0:T(8,128)(2,1)S(1)} %get-tuple-element.109), channel_id=1, source_target_pairs={{1,2},{2,1},{3,4},{4,3},{5,6},{6,5},{7,8},{8,7},{9,10},{10,9},{11,... | collective-permute-start | bytes 9224 | tf_op jit(solution)/shard_map/ppermute | solution.py:27
  111.9 6.9 %collective-permute-start.9 = (bf16[16,224,128]{2,1,0:T(8,128)(2,1)S(1)}, bf16[16,224,128]{2,1,0:T(8,128)(2,1)S(1)}, u32[]{:S(2)}, u32[]{:S(2)}) collective-permute-start(bf16[16,224,128]{2,1,0:T(8,128)(2,1)S(1)} %all-to-all-done.3.slots), channel_id=1, source_target_pairs={{0,1},{1,0},{2,3},{3,2},{4,5},{5,4},{6,7},{7,6},{8,9},{9,8},{10,11... | collective-permute-start | bytes 2752520 | tf_op jit(solution)/shard_map/ppermute | solution.py:389
